TPU v7x, 128 devices: a whole 4x4x4 slice. The times are simulated.
128 devices in a mesh: gx: 8 (over y, core), gy: 16 (over z, x).
Axes of the slice: x: 4, y: 4, z: 4, core: 2. Of those that a mesh axis runs over, the one named last changes fastest.
Arguments:
- adjoint_state: float32 [9, 8, 512, 1024], P(None, None, 'gy', 'gx'), may hold values from -6 to 6
- lame_lambda: float32 [8, 512, 1024], P(None, 'gy', 'gx'), may hold values from 0.5 to 1.5
- shear_modulus: float32 [8, 512, 1024], P(None, 'gy', 'gx'), may hold values from 0.3 to 0.9
- buoyancy: float32 [8, 512, 1024], P(None, 'gy', 'gx'), may hold values from 0.6 to 1.2
- forward_dilation: bfloat16 [8, 8, 512, 1024], P(None, None, 'gy', 'gx'), may hold values from -6 to 6
- forward_shear: bfloat16 [8, 8, 512, 1024], P(None, None, 'gy', 'gx'), may hold values from -6 to 6
- residual: bfloat16 [12288, 3, 4096], P(('gx', 'gy')), may hold values from -6 to 6
- sample_counts: int32 [12288], P(('gx', 'gy')), may hold values from 2048 to 4096
- station_list: int32 [12288], P(('gx', 'gy')), may hold values from 0 to 511, as said below
- receiver_cells: int32 [512], P(('gx', 'gy')), may hold values from 0 to 524287, as said below
- tile_map: int32 [32768], P(('gx', 'gy')), may hold values from 0 to 32767, as said below
Outputs:
- model_kernels: float32 [2, 8, 32768], P(None, None, ('gx', 'gy'))
- adjoint_out: float32 [9, 8, 512, 1024], P(None, None, 'gy', 'gx')
Inputs may be any that keep to these rules, and one draw needn't show every extreme that they name: `station_list`: station s belongs to the device of index s // 4 (the order of the joined axes gx, gy). The rows of one device name stations of any one owner at most 2 times; in every draw some owner is named exactly 2 times by the rows of every device. `receiver_cells`: station s's cell lies in the tile of the device of index s // 4, on the surface; the first station sits at the grid's first corner and the last station at its last corner. `tile_map`: A permutation. The 256 columns of device p go 2 to each device q, into the slots q * 256 + p * 2 to q * 256 + (p + 1) * 2 - 1.
All inputs are finite; a program needn't handle non-finite values.
Results may differ from a plain program's by a relative error of at most 0.0003.
Values may be sent and summed in bfloat16 or wider, within the bound.
No kernel may reach another device: no remote copies, remote signals or barrier semaphores. Data moves between devices by JAX's collectives and lax.ppermute only.
A program may use at most 128 MiB of HBM per device.

v0:
```python
import math

import jax
import jax.numpy as jnp
from jax import lax
from jax.sharding import PartitionSpec as P

STEPS = 8


time_step = 0.25


def extended(cells, sides, width):
    for axis, dim in sides:
        count = lax.axis_size(axis)
        ends = count - 1
        head = lax.slice_in_dim(cells, 0, width, axis=dim)
        tail = lax.slice_in_dim(cells, cells.shape[dim] - width, cells.shape[dim], axis=dim)
        cells = jnp.concatenate(
            [
                lax.ppermute(tail, axis, [(i, (i + 1) % count) for i in range(ends)]),
                cells,
                lax.ppermute(head, axis, [((i + 1) % count, i) for i in range(ends)]),
            ],
            axis=dim,
        )
    return cells


def ahead_x(padded):
    return padded[1:-1, 1:-1, 2:] - padded[1:-1, 1:-1, 1:-1]


def behind_x(padded):
    return padded[1:-1, 1:-1, 1:-1] - padded[1:-1, 1:-1, :-2]


def ahead_y(padded):
    return padded[1:-1, 2:, 1:-1] - padded[1:-1, 1:-1, 1:-1]


def behind_y(padded):
    return padded[1:-1, 1:-1, 1:-1] - padded[1:-1, :-2, 1:-1]


def ahead_z(padded):
    return padded[2:, 1:-1, 1:-1] - padded[1:-1, 1:-1, 1:-1]


def behind_z(padded):
    return padded[1:-1, 1:-1, 1:-1] - padded[:-2, 1:-1, 1:-1]


def velocity_update(velocity, stress_pad, buoyancy, source_now):
    accel_x = ahead_x(stress_pad[0]) + behind_y(stress_pad[3]) + behind_z(stress_pad[4])
    accel_y = behind_x(stress_pad[3]) + ahead_y(stress_pad[1]) + behind_z(stress_pad[5])
    accel_z = behind_x(stress_pad[4]) + behind_y(stress_pad[5]) + ahead_z(stress_pad[2])
    velocity = velocity + time_step * buoyancy * jnp.stack([accel_x, accel_y, accel_z])
    return velocity.at[:, 0].add(time_step * buoyancy[0] * source_now)


def stress_update(stress, vel_pad, lame_lambda, shear_modulus):
    strain_xx = behind_x(vel_pad[0])
    strain_yy = behind_y(vel_pad[1])
    strain_zz = behind_z(vel_pad[2])
    dilation = strain_xx + strain_yy + strain_zz
    strain_xy = ahead_y(vel_pad[0]) + ahead_x(vel_pad[1])
    strain_xz = ahead_z(vel_pad[0]) + ahead_x(vel_pad[2])
    strain_yz = ahead_z(vel_pad[1]) + ahead_y(vel_pad[2])
    pressure = lame_lambda * dilation
    updated = jnp.stack(
        [
            stress[0] + time_step * (pressure + 2.0 * shear_modulus * strain_xx),
            stress[1] + time_step * (pressure + 2.0 * shear_modulus * strain_yy),
            stress[2] + time_step * (pressure + 2.0 * shear_modulus * strain_zz),
            stress[3] + time_step * shear_modulus * strain_xy,
            stress[4] + time_step * shear_modulus * strain_xz,
            stress[5] + time_step * shear_modulus * strain_yz,
        ]
    )
    return (updated, dilation, strain_xy)


def resample_rows(rows):
    samples = rows.shape[2]
    per_step = samples // STEPS
    position = jnp.arange(samples, dtype=jnp.float32) + 0.5
    centers = (jnp.arange(STEPS, dtype=jnp.float32) + 0.5) * per_step
    weight = jnp.maximum(0.0, 1.0 - jnp.abs(position[:, None] - centers[None, :]) / per_step)
    table = (weight / math.sqrt(per_step)).astype(jnp.bfloat16)
    result = jnp.dot(
        rows.reshape(rows.shape[0] * 3, samples), table, preferred_element_type=jnp.float32
    )
    return result.reshape(rows.shape[0], 3 * STEPS)


def pad_depth(field):
    return jnp.pad(field, ((0, 0), (1, 1), (0, 0), (0, 0)))


def local(
    adjoint_state,
    lame_lambda,
    shear_modulus,
    buoyancy,
    forward_dilation,
    forward_shear,
    residual,
    sample_counts,
    station_list,
    receiver_cells,
    tile_map,
):
    owners = lax.axis_size(("gx", "gy"))
    my_index = lax.axis_index(("gx", "gy"))
    tile_x = lax.axis_index("gx")
    tile_y = lax.axis_index("gy")
    depth, rows_y, cols_x = lame_lambda.shape
    width_x = cols_x * lax.axis_size("gx")
    rows_dev, samples = (residual.shape[0], residual.shape[2])
    capacity = max(2, 2 * rows_dev // owners)
    sta_dev = receiver_cells.shape[0]
    live_mask = jnp.arange(samples)[None, :] < sample_counts[:, None]
    masked = residual * live_mask[:, None, :].astype(jnp.bfloat16)
    owner_dev = station_list // sta_dev
    onehot = (owner_dev[:, None] == jnp.arange(owners)[None, :]).astype(jnp.int32)
    earlier = jnp.cumsum(onehot, 0) - onehot
    slot_rank = jnp.sum(earlier * onehot, 1)
    slot_index = owner_dev * capacity + slot_rank
    station_slots = jnp.full((owners * capacity,), -1, jnp.int32).at[slot_index].set(station_list)
    send_rows = jnp.zeros((owners * capacity, 3, samples), jnp.bfloat16).at[slot_index].set(masked)
    got_rows, station_ids = (
        lax.all_to_all(send_rows, ("gx", "gy"), split_axis=0, concat_axis=0, tiled=True),
        lax.all_to_all(station_slots, ("gx", "gy"), split_axis=0, concat_axis=0, tiled=True),
    )
    sources = resample_rows(got_rows)
    valid = station_ids >= 0
    local_station = jnp.where(valid, station_ids - my_index * sta_dev, 0)
    cell_index = receiver_cells[local_station]
    row_local = cell_index // width_x - tile_y * rows_y
    col_local = cell_index % width_x - tile_x * cols_x
    flat_index = jnp.where(valid, row_local * cols_x + col_local, 0)
    weights = sources * valid[:, None].astype(jnp.float32)
    source_flat = (
        jnp.zeros((3 * STEPS, rows_y * cols_x), jnp.float32).at[:, flat_index].add(weights.T)
    )
    kern_lambda = jnp.zeros((depth, rows_y, cols_x), jnp.float32)
    kern_shear = jnp.zeros((depth, rows_y, cols_x), jnp.float32)
    source_plane = source_flat.reshape(3, STEPS, rows_y, cols_x)
    velocity = adjoint_state[0:3]
    stress = adjoint_state[3:9]
    for instant in range(STEPS):
        stress_pad = pad_depth(extended(stress, (("gx", 3), ("gy", 2)), 1))
        velocity = velocity_update(velocity, stress_pad, buoyancy, source_plane[:, instant])
        vel_pad = pad_depth(extended(velocity, (("gx", 3), ("gy", 2)), 1))
        stress, dilation, strain_xy = stress_update(stress, vel_pad, lame_lambda, shear_modulus)
        kern_lambda = (
            kern_lambda + time_step * forward_dilation[instant].astype(jnp.float32) * dilation
        )
        kern_shear = kern_shear + time_step * forward_shear[instant].astype(jnp.float32) * strain_xy
    kernels = jnp.stack([kern_lambda, kern_shear])
    coarse = kernels.reshape(2, depth, rows_y // 4, 4, cols_x // 4, 4).sum(axis=(3, 5)) / 16.0
    cols_dev = rows_y // 4 * (cols_x // 4)
    coarse = coarse.reshape(2, depth, cols_dev)
    per_owner = cols_dev // owners
    target = tile_map // cols_dev
    within = tile_map % cols_dev - my_index * per_owner
    send_index = target * per_owner + within
    send_cols = jnp.zeros((2, depth, cols_dev), jnp.float32).at[:, :, send_index].set(coarse)
    model_kernels = lax.all_to_all(send_cols, ("gx", "gy"), split_axis=2, concat_axis=2, tiled=True)
    adjoint_out = jnp.concatenate([velocity, stress], 0)
    return (model_kernels, adjoint_out)


def solution(mesh):
    in_specs = (
        P(None, None, "gy", "gx"),
        P(None, "gy", "gx"),
        P(None, "gy", "gx"),
        P(None, "gy", "gx"),
        P(None, None, "gy", "gx"),
        P(None, None, "gy", "gx"),
        P(("gx", "gy"), None, None),
        P(("gx", "gy")),
        P(("gx", "gy")),
        P(("gx", "gy")),
        P(("gx", "gy")),
    )
    out_specs = (P(None, None, ("gx", "gy")), P(None, None, "gy", "gx"))
    return jax.shard_map(local, mesh=mesh, in_specs=in_specs, out_specs=out_specs, check_vma=False)
```

profile of v0, /device:TPU:1, one launch (start us, length us, event | category | flops | bytes accessed | tf_op | source)
XLA Modules:
  0.0 629.7 jit_solution(14185917768094463034)
XLA Ops:
  4.2 11.5 %all-to-all-start = ((s32[128,2,1]{1,2,0:T(1,128)}), s32[128,2,1]{1,2,0:T(1,128)S(1)}, u32[]{:S(2)}, u32[]{:S(2)}) async-start(s32[128,2,1]{1,2,0:T(1,128)} %bitcast.11), calls=%async_computation | async-start | bytes 131072 | tf_op jit(solution)/shard_map/all_to_all | solution.py:135
  18.4 2.0 copy.76
  20.5 7.5 %broadcast_in_dim.17 = bf16[256,3,4096]{2,1,0:T(4,128)(2,1)} broadcast(bf16[]{:T(256)} %constant.281.clone.1), dimensions={} | broadcast | bytes 6291458 | tf_op jit(solution)/shard_map/broadcast_in_dim | solution.py:132
  28.0 13.0 %scatter_fusion = bf16[256,3,4096]{2,1,0:T(4,128)(2,1)} fusion(bf16[256,3,4096]{2,1,0:T(4,128)(2,1)} %broadcast_in_dim.17, s32[96]{0:T(128)S(1)} %compare_select_fusion.6, bf16[96,3,4096]{2,1,0:T(4,128)(2,1)S(1)} %copy.76), kind=kCustom, calls=%fused_computation.1 | custom fusion | bytes 7078272 | tf_op jit(solution)/shard_map/scatter | solution.py:132
  40.9 10.2 %all-to-all-start.1 = ((bf16[256,3,4096]{2,1,0:T(4,128)(2,1)}), bf16[256,3,4096]{2,1,0:T(4,128)(2,1)}, u32[]{:S(2)}, u32[]{:S(2)}) async-start(bf16[256,3,4096]{2,1,0:T(4,128)(2,1)} %scatter_fusion), calls=%async_computation.1 | async-start | bytes 16777216 | tf_op jit(solution)/shard_map/all_to_all | solution.py:134
  51.8 3.0 collective-permute-start.1
  55.2 2.5 collective-permute-start
  59.2 2.5 compare_select_fusion
  61.7 85.2 %collective-permute-done.1 = f32[6,8,32,1]{2,1,3,0:T(8,128)S(1)} collective-permute-done((f32[6,8,32,1]{2,1,3,0:T(8,128)S(1)}, f32[6,8,32,1]{2,1,3,0:T(8,128)S(1)}, u32[]{:S(2)}, u32[]{:S(2)}) %collective-permute-start.1) | collective-permute-done | bytes 6176 | tf_op jit(solution)/shard_map/ppermute | solution.py:24
  151.2 4.9 collective-permute-start.2
  157.1 2.0 select_maximum_fusion.28
  159.8 13.7 %reshape.502 = bf16[768,4096]{1,0:T(8,128)(2,1)} reshape(bf16[256,3,4096]{2,1,0:T(4,128)(2,1)} %all-to-all-done.1) | data formatting | bytes 12582912 | tf_op jit(solution)/shard_map/reshape | solution.py:93
  173.5 4.6 fusion.160
  178.3 3.3 scatter_custom_fusion.2
  181.6 2.2 copy.78
  186.1 3.6 collective-permute-start.4
  189.7 3.5 collective-permute-done.5
  195.9 4.5 collective-permute-start.6
  209.5 1.9 collective-permute-start.9
  213.0 5.2 collective-permute-start.8
  223.7 4.9 collective-permute-start.10
  234.4 4.7 collective-permute-start.12
  239.2 3.5 collective-permute-done.13
  245.4 6.3 collective-permute-start.14
  259.0 2.1 copy.84
  264.0 5.2 collective-permute-start.16
  270.4 2.0 copy.85
  275.1 6.6 %collective-permute-start.18 = (f32[6,8,1,130]{3,2,1,0:T(1,128)S(1)}, f32[6,8,1,130]{3,2,1,0:T(1,128)S(1)}, u32[]{:S(2)}, u32[]{:S(2)}) collective-permute-start(f32[6,8,1,130]{3,2,1,0:T(1,128)S(1)} %get-tuple-element.261), channel_id=1, source_target_pairs={{0,1},{1,2},{2,3},{3,4},{4,5},{5,6},{6,7},{7,8},{8,9},{9,10},{10,1... | collective-permute-start | bytes 74888 | tf_op jit(solution)/shard_map/ppermute | solution.py:22
  287.6 5.2 collective-permute-start.20
  292.7 3.5 collective-permute-done.21
  299.0 6.7 %collective-permute-start.22 = (f32[3,8,1,130]{3,2,1,0:T(1,128)S(1)}, f32[3,8,1,130]{3,2,1,0:T(1,128)S(1)}, u32[]{:S(2)}, u32[]{:S(2)}) collective-permute-start(f32[3,8,1,130]{3,2,1,0:T(1,128)S(1)} %get-tuple-element.301), channel_id=1, source_target_pairs={{0,1},{1,2},{2,3},{3,4},{4,5},{5,6},{6,7},{7,8},{8,9},{9,10},{10,1... | collective-permute-start | bytes 37448 | tf_op jit(solution)/shard_map/ppermute | solution.py:22
  315.4 5.2 collective-permute-start.24
  323.6 6.7 %collective-permute-start.26 = (f32[6,8,1,130]{3,2,1,0:T(1,128)S(1)}, f32[6,8,1,130]{3,2,1,0:T(1,128)S(1)}, u32[]{:S(2)}, u32[]{:S(2)}) collective-permute-start(f32[6,8,1,130]{3,2,1,0:T(1,128)S(1)} %get-tuple-element.259), channel_id=1, source_target_pairs={{0,1},{1,2},{2,3},{3,4},{4,5},{5,6},{6,7},{7,8},{8,9},{9,10},{10,1... | collective-permute-start | bytes 74888 | tf_op jit(solution)/shard_map/ppermute | solution.py:22
  336.1 5.1 collective-permute-start.28
  341.2 3.5 collective-permute-done.29
  347.4 6.8 %collective-permute-start.30 = (f32[3,8,1,130]{3,2,1,0:T(1,128)S(1)}, f32[3,8,1,130]{3,2,1,0:T(1,128)S(1)}, u32[]{:S(2)}, u32[]{:S(2)}) collective-permute-start(f32[3,8,1,130]{3,2,1,0:T(1,128)S(1)} %get-tuple-element.299), channel_id=1, source_target_pairs={{0,1},{1,2},{2,3},{3,4},{4,5},{5,6},{6,7},{7,8},{8,9},{9,10},{10,1... | collective-permute-start | bytes 37448 | tf_op jit(solution)/shard_map/ppermute | solution.py:22
  360.8 1.9 collective-permute-start.33
  363.0 5.2 collective-permute-start.32
  371.2 6.7 %collective-permute-start.34 = (f32[6,8,1,130]{3,2,1,0:T(1,128)S(1)}, f32[6,8,1,130]{3,2,1,0:T(1,128)S(1)}, u32[]{:S(2)}, u32[]{:S(2)}) collective-permute-start(f32[6,8,1,130]{3,2,1,0:T(1,128)S(1)} %get-tuple-element.257), channel_id=1, source_target_pairs={{0,1},{1,2},{2,3},{3,4},{4,5},{5,6},{6,7},{7,8},{8,9},{9,10},{10,1... | collective-permute-start | bytes 74888 | tf_op jit(solution)/shard_map/ppermute | solution.py:22
  383.8 5.1 collective-permute-start.36
  388.8 3.5 collective-permute-done.37
  395.1 6.7 %collective-permute-start.38 = (f32[3,8,1,130]{3,2,1,0:T(1,128)S(1)}, f32[3,8,1,130]{3,2,1,0:T(1,128)S(1)}, u32[]{:S(2)}, u32[]{:S(2)}) collective-permute-start(f32[3,8,1,130]{3,2,1,0:T(1,128)S(1)} %get-tuple-element.297), channel_id=1, source_target_pairs={{0,1},{1,2},{2,3},{3,4},{4,5},{5,6},{6,7},{7,8},{8,9},{9,10},{10,1... | collective-permute-start | bytes 37448 | tf_op jit(solution)/shard_map/ppermute | solution.py:22
  409.8 1.9 collective-permute-start.41
  412.1 5.2 collective-permute-start.40
  420.3 6.7 %collective-permute-start.42 = (f32[6,8,1,130]{3,2,1,0:T(1,128)S(1)}, f32[6,8,1,130]{3,2,1,0:T(1,128)S(1)}, u32[]{:S(2)}, u32[]{:S(2)}) collective-permute-start(f32[6,8,1,130]{3,2,1,0:T(1,128)S(1)} %get-tuple-element.255), channel_id=1, source_target_pairs={{0,1},{1,2},{2,3},{3,4},{4,5},{5,6},{6,7},{7,8},{8,9},{9,10},{10,1... | collective-permute-start | bytes 74888 | tf_op jit(solution)/shard_map/ppermute | solution.py:22
  432.9 5.1 collective-permute-start.44
  437.9 3.5 collective-permute-done.45
  444.2 6.9 %collective-permute-start.46 = (f32[3,8,1,130]{3,2,1,0:T(1,128)S(1)}, f32[3,8,1,130]{3,2,1,0:T(1,128)S(1)}, u32[]{:S(2)}, u32[]{:S(2)}) collective-permute-start(f32[3,8,1,130]{3,2,1,0:T(1,128)S(1)} %get-tuple-element.295), channel_id=1, source_target_pairs={{0,1},{1,2},{2,3},{3,4},{4,5},{5,6},{6,7},{7,8},{8,9},{9,10},{10,1... | collective-permute-start | bytes 37448 | tf_op jit(solution)/shard_map/ppermute | solution.py:22
  460.5 5.2 collective-permute-start.48
  468.7 6.7 %collective-permute-start.50 = (f32[6,8,1,130]{3,2,1,0:T(1,128)S(1)}, f32[6,8,1,130]{3,2,1,0:T(1,128)S(1)}, u32[]{:S(2)}, u32[]{:S(2)}) collective-permute-start(f32[6,8,1,130]{3,2,1,0:T(1,128)S(1)} %get-tuple-element.253), channel_id=1, source_target_pairs={{0,1},{1,2},{2,3},{3,4},{4,5},{5,6},{6,7},{7,8},{8,9},{9,10},{10,1... | collective-permute-start | bytes 74888 | tf_op jit(solution)/shard_map/ppermute | solution.py:22
  481.2 5.1 collective-permute-start.52
  486.3 3.5 collective-permute-done.53
  492.5 6.7 %collective-permute-start.54 = (f32[3,8,1,130]{3,2,1,0:T(1,128)S(1)}, f32[3,8,1,130]{3,2,1,0:T(1,128)S(1)}, u32[]{:S(2)}, u32[]{:S(2)}) collective-permute-start(f32[3,8,1,130]{3,2,1,0:T(1,128)S(1)} %get-tuple-element.293), channel_id=1, source_target_pairs={{0,1},{1,2},{2,3},{3,4},{4,5},{5,6},{6,7},{7,8},{8,9},{9,10},{10,1... | collective-permute-start | bytes 37448 | tf_op jit(solution)/shard_map/ppermute | solution.py:22
  509.5 5.2 collective-permute-start.56
  517.7 6.7 %collective-permute-start.58 = (f32[6,8,1,130]{3,2,1,0:T(1,128)S(1)}, f32[6,8,1,130]{3,2,1,0:T(1,128)S(1)}, u32[]{:S(2)}, u32[]{:S(2)}) collective-permute-start(f32[6,8,1,130]{3,2,1,0:T(1,128)S(1)} %get-tuple-element.251), channel_id=1, source_target_pairs={{0,1},{1,2},{2,3},{3,4},{4,5},{5,6},{6,7},{7,8},{8,9},{9,10},{10,1... | collective-permute-start | bytes 74888 | tf_op jit(solution)/shard_map/ppermute | solution.py:22
  530.3 5.1 collective-permute-start.60
  535.4 3.5 collective-permute-done.61
  541.6 6.9 %collective-permute-start.62 = (f32[3,8,1,130]{3,2,1,0:T(1,128)S(1)}, f32[3,8,1,130]{3,2,1,0:T(1,128)S(1)}, u32[]{:S(2)}, u32[]{:S(2)}) collective-permute-start(f32[3,8,1,130]{3,2,1,0:T(1,128)S(1)} %get-tuple-element.291), channel_id=1, source_target_pairs={{0,1},{1,2},{2,3},{3,4},{4,5},{5,6},{6,7},{7,8},{8,9},{9,10},{10,1... | collective-permute-start | bytes 37448 | tf_op jit(solution)/shard_map/ppermute | solution.py:22
  555.2 2.1 fusion.152
  557.3 2.9 copy.107
  560.2 3.4 maximum_reduce_fusion
  564.7 24.3 %scatter_fusion.1 = f32[2,8,256]{1,0,2:T(2,128)} fusion(f32[2,8,256]{1,0,2:T(2,128)} %broadcast_in_dim.12, s32[256]{0:T(256)S(1)} %compare_select_fusion.5, f32[256,2,8]{2,1,0:T(2,128)S(1)} %bitcast.427), kind=kCustom, calls=%fused_computation.3 | custom fusion | bytes 50176 | tf_op jit(solution)/shard_map/scatter | solution.py:170
  589.0 28.2 %all-to-all-start.2 = ((f32[2,8,256]{1,0,2:T(2,128)}), f32[2,8,256]{1,0,2:T(2,128)S(1)}, u32[]{:S(2)}, u32[]{:S(2)}) async-start(f32[2,8,256]{1,0,2:T(2,128)} %scatter_fusion.1), calls=%async_computation.2 | async-start | bytes 524288 | tf_op jit(solution)/shard_map/all_to_all | solution.py:171
  618.9 9.7 %all-to-all-done.2 = f32[2,8,256]{1,0,2:T(2,128)S(1)} async-done(((f32[2,8,256]{1,0,2:T(2,128)}), f32[2,8,256]{1,0,2:T(2,128)S(1)}, u32[]{:S(2)}, u32[]{:S(2)}) %all-to-all-start.2) | async-done | bytes 16416 | tf_op jit(solution)/shard_map/all_to_all | solution.py:171
  (422 shorter events, 178.0 us)
Async XLA Ops:
  4.2 36.8 %all-to-all-start = ((s32[128,2,1]{1,2,0:T(1,128)}), s32[128,2,1]{1,2,0:T(1,128)S(1)}, u32[]{:S(2)}, u32[]{:S(2)}) async-start(s32[128,2,1]{1,2,0:T(1,128)} %bitcast.11), calls=%async_computation | async-start | bytes 131072 | tf_op jit(solution)/shard_map/all_to_all | solution.py:135
  40.9 118.9 %all-to-all-start.1 = ((bf16[256,3,4096]{2,1,0:T(4,128)(2,1)}), bf16[256,3,4096]{2,1,0:T(4,128)(2,1)}, u32[]{:S(2)}, u32[]{:S(2)}) async-start(bf16[256,3,4096]{2,1,0:T(4,128)(2,1)} %scatter_fusion), calls=%async_computation.1 | async-start | bytes 16777216 | tf_op jit(solution)/shard_map/all_to_all | solution.py:134
  51.8 95.1 %collective-permute-start.1 = (f32[6,8,32,1]{2,1,3,0:T(8,128)S(1)}, f32[6,8,32,1]{2,1,3,0:T(8,128)S(1)}, u32[]{:S(2)}, u32[]{:S(2)}) collective-permute-start(f32[6,8,32,1]{2,1,3,0:T(8,128)S(1)} %copy.113), channel_id=1, source_target_pairs={{16,0},{32,16},{48,32},{64,48},{80,64},{96,80},{112,96},{17,1},{33... | collective-permute-start | bytes 18440 | tf_op jit(solution)/shard_map/ppermute | solution.py:24
  55.2 92.0 %collective-permute-start = (f32[6,8,32,1]{2,1,3,0:T(8,128)S(1)}, f32[6,8,32,1]{2,1,3,0:T(8,128)S(1)}, u32[]{:S(2)}, u32[]{:S(2)}) collective-permute-start(f32[6,8,32,1]{2,1,3,0:T(8,128)S(1)} %copy.112), channel_id=1, source_target_pairs={{0,16},{16,32},{32,48},{48,64},{64,80},{80,96},{96,112},{1,17},{17... | collective-permute-start | bytes 18440 | tf_op jit(solution)/shard_map/ppermute | solution.py:22
  149.9 6.6 %collective-permute-start.3 = (f32[6,8,1,130]{3,2,1,0:T(1,128)S(1)}, f32[6,8,1,130]{3,2,1,0:T(1,128)S(1)}, u32[]{:S(2)}, u32[]{:S(2)}) collective-permute-start(f32[6,8,1,130]{3,2,1,0:T(1,128)S(1)} %get-tuple-element.266), channel_id=1, source_target_pairs={{1,0},{2,1},{3,2},{4,3},{5,4},{6,5},{7,6},{8,7},{9,8},{10,9},{11,1... | collective-permute-start | bytes 74888 | tf_op jit(solution)/shard_map/ppermute | solution.py:24
  184.1 9.1 %collective-permute-start.5 = (f32[3,8,32,1]{3,2,1,0:T(8,128)S(1)}, f32[3,8,32,1]{3,2,1,0:T(8,128)S(1)}, u32[]{:S(2)}, u32[]{:S(2)}) collective-permute-start(f32[3,8,32,1]{3,2,1,0:T(8,128)S(1)} %get-tuple-element.362), channel_id=1, source_target_pairs={{16,0},{32,16},{48,32},{64,48},{80,64},{96,80},{112,96},{17,1},{33... | collective-permute-start | bytes 9224 | tf_op jit(solution)/shard_map/ppermute | solution.py:24
  186.1 8.3 %collective-permute-start.4 = (f32[3,8,32,1]{3,2,1,0:T(8,128)S(1)}, f32[3,8,32,1]{3,2,1,0:T(8,128)S(1)}, u32[]{:S(2)}, u32[]{:S(2)}) collective-permute-start(f32[3,8,32,1]{3,2,1,0:T(8,128)S(1)} %get-tuple-element.361), channel_id=1, source_target_pairs={{0,16},{16,32},{32,48},{48,64},{64,80},{80,96},{96,112},{1,17},{17... | collective-permute-start | bytes 9224 | tf_op jit(solution)/shard_map/ppermute | solution.py:22
  209.5 8.7 %collective-permute-start.9 = (f32[6,8,32,1]{2,1,3,0:T(8,128)S(1)}, f32[6,8,32,1]{2,1,3,0:T(8,128)S(1)}, u32[]{:S(2)}, u32[]{:S(2)}) collective-permute-start(f32[6,8,32,1]{2,1,3,0:T(8,128)S(1)} %copy.80), channel_id=1, source_target_pairs={{16,0},{32,16},{48,32},{64,48},{80,64},{96,80},{112,96},{17,1},{33... | collective-permute-start | bytes 18440 | tf_op jit(solution)/shard_map/ppermute | solution.py:24
  213.0 6.5 %collective-permute-start.8 = (f32[6,8,32,1]{2,1,3,0:T(8,128)S(1)}, f32[6,8,32,1]{2,1,3,0:T(8,128)S(1)}, u32[]{:S(2)}, u32[]{:S(2)}) collective-permute-start(f32[6,8,32,1]{2,1,3,0:T(8,128)S(1)} %copy.79), channel_id=1, source_target_pairs={{0,16},{16,32},{32,48},{48,64},{64,80},{80,96},{96,112},{1,17},{17... | collective-permute-start | bytes 18440 | tf_op jit(solution)/shard_map/ppermute | solution.py:22
  222.4 6.2 collective-permute-start.11
  223.7 6.1 collective-permute-start.10
  232.5 10.2 %collective-permute-start.13 = (f32[3,8,32,1]{3,2,1,0:T(8,128)S(1)}, f32[3,8,32,1]{3,2,1,0:T(8,128)S(1)}, u32[]{:S(2)}, u32[]{:S(2)}) collective-permute-start(f32[3,8,32,1]{3,2,1,0:T(8,128)S(1)} %get-tuple-element.360), channel_id=1, source_target_pairs={{16,0},{32,16},{48,32},{64,48},{80,64},{96,80},{112,96},{17,1},{33... | collective-permute-start | bytes 9224 | tf_op jit(solution)/shard_map/ppermute | solution.py:24
  234.4 9.4 %collective-permute-start.12 = (f32[3,8,32,1]{3,2,1,0:T(8,128)S(1)}, f32[3,8,32,1]{3,2,1,0:T(8,128)S(1)}, u32[]{:S(2)}, u32[]{:S(2)}) collective-permute-start(f32[3,8,32,1]{3,2,1,0:T(8,128)S(1)} %get-tuple-element.359), channel_id=1, source_target_pairs={{0,16},{16,32},{32,48},{48,64},{64,80},{80,96},{96,112},{1,17},{17... | collective-permute-start | bytes 9224 | tf_op jit(solution)/shard_map/ppermute | solution.py:22
  244.1 7.6 %collective-permute-start.15 = (f32[3,8,1,130]{3,2,1,0:T(1,128)S(1)}, f32[3,8,1,130]{3,2,1,0:T(1,128)S(1)}, u32[]{:S(2)}, u32[]{:S(2)}) collective-permute-start(f32[3,8,1,130]{3,2,1,0:T(1,128)S(1)} %get-tuple-element.304), channel_id=1, source_target_pairs={{1,0},{2,1},{3,2},{4,3},{5,4},{6,5},{7,6},{8,7},{9,8},{10,9},{11,1... | collective-permute-start | bytes 37448 | tf_op jit(solution)/shard_map/ppermute | solution.py:24
  245.4 6.8 %collective-permute-start.14 = (f32[3,8,1,130]{3,2,1,0:T(1,128)S(1)}, f32[3,8,1,130]{3,2,1,0:T(1,128)S(1)}, u32[]{:S(2)}, u32[]{:S(2)}) collective-permute-start(f32[3,8,1,130]{3,2,1,0:T(1,128)S(1)} %get-tuple-element.303), channel_id=1, source_target_pairs={{0,1},{1,2},{2,3},{3,4},{4,5},{5,6},{6,7},{7,8},{8,9},{9,10},{10,1... | collective-permute-start | bytes 37448 | tf_op jit(solution)/shard_map/ppermute | solution.py:22
  261.1 8.1 %collective-permute-start.17 = (f32[6,8,32,1]{2,1,3,0:T(8,128)}, f32[6,8,32,1]{2,1,3,0:T(8,128)}, u32[]{:S(2)}, u32[]{:S(2)}) collective-permute-start(f32[6,8,32,1]{2,1,3,0:T(8,128)} %copy.84), channel_id=1, source_target_pairs={{16,0},{32,16},{48,32},{64,48},{80,64},{96,80},{112,96},{17,1},{33... | collective-permute-start | bytes 18440 | tf_op jit(solution)/shard_map/ppermute | solution.py:24
  264.0 6.4 %collective-permute-start.16 = (f32[6,8,32,1]{2,1,3,0:T(8,128)}, f32[6,8,32,1]{2,1,3,0:T(8,128)}, u32[]{:S(2)}, u32[]{:S(2)}) collective-permute-start(f32[6,8,32,1]{2,1,3,0:T(8,128)} %copy.83), channel_id=1, source_target_pairs={{0,16},{16,32},{32,48},{48,64},{64,80},{80,96},{96,112},{1,17},{17... | collective-permute-start | bytes 18440 | tf_op jit(solution)/shard_map/ppermute | solution.py:22
  273.8 7.9 %collective-permute-start.19 = (f32[6,8,1,130]{3,2,1,0:T(1,128)S(1)}, f32[6,8,1,130]{3,2,1,0:T(1,128)S(1)}, u32[]{:S(2)}, u32[]{:S(2)}) collective-permute-start(f32[6,8,1,130]{3,2,1,0:T(1,128)S(1)} %get-tuple-element.262), channel_id=1, source_target_pairs={{1,0},{2,1},{3,2},{4,3},{5,4},{6,5},{7,6},{8,7},{9,8},{10,9},{11,1... | collective-permute-start | bytes 74888 | tf_op jit(solution)/shard_map/ppermute | solution.py:24
  275.1 7.8 %collective-permute-start.18 = (f32[6,8,1,130]{3,2,1,0:T(1,128)S(1)}, f32[6,8,1,130]{3,2,1,0:T(1,128)S(1)}, u32[]{:S(2)}, u32[]{:S(2)}) collective-permute-start(f32[6,8,1,130]{3,2,1,0:T(1,128)S(1)} %get-tuple-element.261), channel_id=1, source_target_pairs={{0,1},{1,2},{2,3},{3,4},{4,5},{5,6},{6,7},{7,8},{8,9},{9,10},{10,1... | collective-permute-start | bytes 74888 | tf_op jit(solution)/shard_map/ppermute | solution.py:22
  285.6 10.6 %collective-permute-start.21 = (f32[3,8,32,1]{3,2,1,0:T(8,128)S(1)}, f32[3,8,32,1]{3,2,1,0:T(8,128)S(1)}, u32[]{:S(2)}, u32[]{:S(2)}) collective-permute-start(f32[3,8,32,1]{3,2,1,0:T(8,128)S(1)} %get-tuple-element.358), channel_id=1, source_target_pairs={{16,0},{32,16},{48,32},{64,48},{80,64},{96,80},{112,96},{17,1},{33... | collective-permute-start | bytes 9224 | tf_op jit(solution)/shard_map/ppermute | solution.py:24
  287.6 9.9 %collective-permute-start.20 = (f32[3,8,32,1]{3,2,1,0:T(8,128)S(1)}, f32[3,8,32,1]{3,2,1,0:T(8,128)S(1)}, u32[]{:S(2)}, u32[]{:S(2)}) collective-permute-start(f32[3,8,32,1]{3,2,1,0:T(8,128)S(1)} %get-tuple-element.357), channel_id=1, source_target_pairs={{0,16},{16,32},{32,48},{48,64},{64,80},{80,96},{96,112},{1,17},{17... | collective-permute-start | bytes 9224 | tf_op jit(solution)/shard_map/ppermute | solution.py:22
  297.7 8.0 %collective-permute-start.23 = (f32[3,8,1,130]{3,2,1,0:T(1,128)S(1)}, f32[3,8,1,130]{3,2,1,0:T(1,128)S(1)}, u32[]{:S(2)}, u32[]{:S(2)}) collective-permute-start(f32[3,8,1,130]{3,2,1,0:T(1,128)S(1)} %get-tuple-element.302), channel_id=1, source_target_pairs={{1,0},{2,1},{3,2},{4,3},{5,4},{6,5},{7,6},{8,7},{9,8},{10,9},{11,1... | collective-permute-start | bytes 37448 | tf_op jit(solution)/shard_map/ppermute | solution.py:24
  299.0 7.6 %collective-permute-start.22 = (f32[3,8,1,130]{3,2,1,0:T(1,128)S(1)}, f32[3,8,1,130]{3,2,1,0:T(1,128)S(1)}, u32[]{:S(2)}, u32[]{:S(2)}) collective-permute-start(f32[3,8,1,130]{3,2,1,0:T(1,128)S(1)} %get-tuple-element.301), channel_id=1, source_target_pairs={{0,1},{1,2},{2,3},{3,4},{4,5},{5,6},{6,7},{7,8},{8,9},{9,10},{10,1... | collective-permute-start | bytes 37448 | tf_op jit(solution)/shard_map/ppermute | solution.py:22
  313.1 7.5 %collective-permute-start.25 = (f32[6,8,32,1]{2,1,3,0:T(8,128)S(1)}, f32[6,8,32,1]{2,1,3,0:T(8,128)S(1)}, u32[]{:S(2)}, u32[]{:S(2)}) collective-permute-start(f32[6,8,32,1]{2,1,3,0:T(8,128)S(1)} %copy.88), channel_id=1, source_target_pairs={{16,0},{32,16},{48,32},{64,48},{80,64},{96,80},{112,96},{17,1},{33... | collective-permute-start | bytes 18440 | tf_op jit(solution)/shard_map/ppermute | solution.py:24
  315.4 6.2 collective-permute-start.24
  322.3 8.0 %collective-permute-start.27 = (f32[6,8,1,130]{3,2,1,0:T(1,128)S(1)}, f32[6,8,1,130]{3,2,1,0:T(1,128)S(1)}, u32[]{:S(2)}, u32[]{:S(2)}) collective-permute-start(f32[6,8,1,130]{3,2,1,0:T(1,128)S(1)} %get-tuple-element.260), channel_id=1, source_target_pairs={{1,0},{2,1},{3,2},{4,3},{5,4},{6,5},{7,6},{8,7},{9,8},{10,9},{11,1... | collective-permute-start | bytes 74888 | tf_op jit(solution)/shard_map/ppermute | solution.py:24
  323.6 7.9 %collective-permute-start.26 = (f32[6,8,1,130]{3,2,1,0:T(1,128)S(1)}, f32[6,8,1,130]{3,2,1,0:T(1,128)S(1)}, u32[]{:S(2)}, u32[]{:S(2)}) collective-permute-start(f32[6,8,1,130]{3,2,1,0:T(1,128)S(1)} %get-tuple-element.259), channel_id=1, source_target_pairs={{0,1},{1,2},{2,3},{3,4},{4,5},{5,6},{6,7},{7,8},{8,9},{9,10},{10,1... | collective-permute-start | bytes 74888 | tf_op jit(solution)/shard_map/ppermute | solution.py:22
  334.2 10.5 %collective-permute-start.29 = (f32[3,8,32,1]{3,2,1,0:T(8,128)S(1)}, f32[3,8,32,1]{3,2,1,0:T(8,128)S(1)}, u32[]{:S(2)}, u32[]{:S(2)}) collective-permute-start(f32[3,8,32,1]{3,2,1,0:T(8,128)S(1)} %get-tuple-element.356), channel_id=1, source_target_pairs={{16,0},{32,16},{48,32},{64,48},{80,64},{96,80},{112,96},{17,1},{33... | collective-permute-start | bytes 9224 | tf_op jit(solution)/shard_map/ppermute | solution.py:24
  336.1 9.8 %collective-permute-start.28 = (f32[3,8,32,1]{3,2,1,0:T(8,128)S(1)}, f32[3,8,32,1]{3,2,1,0:T(8,128)S(1)}, u32[]{:S(2)}, u32[]{:S(2)}) collective-permute-start(f32[3,8,32,1]{3,2,1,0:T(8,128)S(1)} %get-tuple-element.355), channel_id=1, source_target_pairs={{0,16},{16,32},{32,48},{48,64},{64,80},{80,96},{96,112},{1,17},{17... | collective-permute-start | bytes 9224 | tf_op jit(solution)/shard_map/ppermute | solution.py:22
  346.1 8.2 %collective-permute-start.31 = (f32[3,8,1,130]{3,2,1,0:T(1,128)S(1)}, f32[3,8,1,130]{3,2,1,0:T(1,128)S(1)}, u32[]{:S(2)}, u32[]{:S(2)}) collective-permute-start(f32[3,8,1,130]{3,2,1,0:T(1,128)S(1)} %get-tuple-element.300), channel_id=1, source_target_pairs={{1,0},{2,1},{3,2},{4,3},{5,4},{6,5},{7,6},{8,7},{9,8},{10,9},{11,1... | collective-permute-start | bytes 37448 | tf_op jit(solution)/shard_map/ppermute | solution.py:24
  347.4 7.6 %collective-permute-start.30 = (f32[3,8,1,130]{3,2,1,0:T(1,128)S(1)}, f32[3,8,1,130]{3,2,1,0:T(1,128)S(1)}, u32[]{:S(2)}, u32[]{:S(2)}) collective-permute-start(f32[3,8,1,130]{3,2,1,0:T(1,128)S(1)} %get-tuple-element.299), channel_id=1, source_target_pairs={{0,1},{1,2},{2,3},{3,4},{4,5},{5,6},{6,7},{7,8},{8,9},{9,10},{10,1... | collective-permute-start | bytes 37448 | tf_op jit(solution)/shard_map/ppermute | solution.py:22
  360.8 7.5 %collective-permute-start.33 = (f32[6,8,32,1]{2,1,3,0:T(8,128)S(1)}, f32[6,8,32,1]{2,1,3,0:T(8,128)S(1)}, u32[]{:S(2)}, u32[]{:S(2)}) collective-permute-start(f32[6,8,32,1]{2,1,3,0:T(8,128)S(1)} %copy.92), channel_id=1, source_target_pairs={{16,0},{32,16},{48,32},{64,48},{80,64},{96,80},{112,96},{17,1},{33... | collective-permute-start | bytes 18440 | tf_op jit(solution)/shard_map/ppermute | solution.py:24
  363.0 6.2 collective-permute-start.32
  369.9 8.0 %collective-permute-start.35 = (f32[6,8,1,130]{3,2,1,0:T(1,128)S(1)}, f32[6,8,1,130]{3,2,1,0:T(1,128)S(1)}, u32[]{:S(2)}, u32[]{:S(2)}) collective-permute-start(f32[6,8,1,130]{3,2,1,0:T(1,128)S(1)} %get-tuple-element.258), channel_id=1, source_target_pairs={{1,0},{2,1},{3,2},{4,3},{5,4},{6,5},{7,6},{8,7},{9,8},{10,9},{11,1... | collective-permute-start | bytes 74888 | tf_op jit(solution)/shard_map/ppermute | solution.py:24
  371.2 7.9 %collective-permute-start.34 = (f32[6,8,1,130]{3,2,1,0:T(1,128)S(1)}, f32[6,8,1,130]{3,2,1,0:T(1,128)S(1)}, u32[]{:S(2)}, u32[]{:S(2)}) collective-permute-start(f32[6,8,1,130]{3,2,1,0:T(1,128)S(1)} %get-tuple-element.257), channel_id=1, source_target_pairs={{0,1},{1,2},{2,3},{3,4},{4,5},{5,6},{6,7},{7,8},{8,9},{9,10},{10,1... | collective-permute-start | bytes 74888 | tf_op jit(solution)/shard_map/ppermute | solution.py:22
  381.8 10.5 %collective-permute-start.37 = (f32[3,8,32,1]{3,2,1,0:T(8,128)S(1)}, f32[3,8,32,1]{3,2,1,0:T(8,128)S(1)}, u32[]{:S(2)}, u32[]{:S(2)}) collective-permute-start(f32[3,8,32,1]{3,2,1,0:T(8,128)S(1)} %get-tuple-element.354), channel_id=1, source_target_pairs={{16,0},{32,16},{48,32},{64,48},{80,64},{96,80},{112,96},{17,1},{33... | collective-permute-start | bytes 9224 | tf_op jit(solution)/shard_map/ppermute | solution.py:24
  383.8 9.8 %collective-permute-start.36 = (f32[3,8,32,1]{3,2,1,0:T(8,128)S(1)}, f32[3,8,32,1]{3,2,1,0:T(8,128)S(1)}, u32[]{:S(2)}, u32[]{:S(2)}) collective-permute-start(f32[3,8,32,1]{3,2,1,0:T(8,128)S(1)} %get-tuple-element.353), channel_id=1, source_target_pairs={{0,16},{16,32},{32,48},{48,64},{64,80},{80,96},{96,112},{1,17},{17... | collective-permute-start | bytes 9224 | tf_op jit(solution)/shard_map/ppermute | solution.py:22
  393.8 8.0 %collective-permute-start.39 = (f32[3,8,1,130]{3,2,1,0:T(1,128)S(1)}, f32[3,8,1,130]{3,2,1,0:T(1,128)S(1)}, u32[]{:S(2)}, u32[]{:S(2)}) collective-permute-start(f32[3,8,1,130]{3,2,1,0:T(1,128)S(1)} %get-tuple-element.298), channel_id=1, source_target_pairs={{1,0},{2,1},{3,2},{4,3},{5,4},{6,5},{7,6},{8,7},{9,8},{10,9},{11,1... | collective-permute-start | bytes 37448 | tf_op jit(solution)/shard_map/ppermute | solution.py:24
  395.1 7.6 %collective-permute-start.38 = (f32[3,8,1,130]{3,2,1,0:T(1,128)S(1)}, f32[3,8,1,130]{3,2,1,0:T(1,128)S(1)}, u32[]{:S(2)}, u32[]{:S(2)}) collective-permute-start(f32[3,8,1,130]{3,2,1,0:T(1,128)S(1)} %get-tuple-element.297), channel_id=1, source_target_pairs={{0,1},{1,2},{2,3},{3,4},{4,5},{5,6},{6,7},{7,8},{8,9},{9,10},{10,1... | collective-permute-start | bytes 37448 | tf_op jit(solution)/shard_map/ppermute | solution.py:22
  409.8 7.5 %collective-permute-start.41 = (f32[6,8,32,1]{2,1,3,0:T(8,128)S(1)}, f32[6,8,32,1]{2,1,3,0:T(8,128)S(1)}, u32[]{:S(2)}, u32[]{:S(2)}) collective-permute-start(f32[6,8,32,1]{2,1,3,0:T(8,128)S(1)} %copy.96), channel_id=1, source_target_pairs={{16,0},{32,16},{48,32},{64,48},{80,64},{96,80},{112,96},{17,1},{33... | collective-permute-start | bytes 18440 | tf_op jit(solution)/shard_map/ppermute | solution.py:24
  412.1 6.2 collective-permute-start.40
  419.0 8.0 %collective-permute-start.43 = (f32[6,8,1,130]{3,2,1,0:T(1,128)S(1)}, f32[6,8,1,130]{3,2,1,0:T(1,128)S(1)}, u32[]{:S(2)}, u32[]{:S(2)}) collective-permute-start(f32[6,8,1,130]{3,2,1,0:T(1,128)S(1)} %get-tuple-element.256), channel_id=1, source_target_pairs={{1,0},{2,1},{3,2},{4,3},{5,4},{6,5},{7,6},{8,7},{9,8},{10,9},{11,1... | collective-permute-start | bytes 74888 | tf_op jit(solution)/shard_map/ppermute | solution.py:24
  420.3 7.9 %collective-permute-start.42 = (f32[6,8,1,130]{3,2,1,0:T(1,128)S(1)}, f32[6,8,1,130]{3,2,1,0:T(1,128)S(1)}, u32[]{:S(2)}, u32[]{:S(2)}) collective-permute-start(f32[6,8,1,130]{3,2,1,0:T(1,128)S(1)} %get-tuple-element.255), channel_id=1, source_target_pairs={{0,1},{1,2},{2,3},{3,4},{4,5},{5,6},{6,7},{7,8},{8,9},{9,10},{10,1... | collective-permute-start | bytes 74888 | tf_op jit(solution)/shard_map/ppermute | solution.py:22
  430.9 10.5 %collective-permute-start.45 = (f32[3,8,32,1]{3,2,1,0:T(8,128)S(1)}, f32[3,8,32,1]{3,2,1,0:T(8,128)S(1)}, u32[]{:S(2)}, u32[]{:S(2)}) collective-permute-start(f32[3,8,32,1]{3,2,1,0:T(8,128)S(1)} %get-tuple-element.352), channel_id=1, source_target_pairs={{16,0},{32,16},{48,32},{64,48},{80,64},{96,80},{112,96},{17,1},{33... | collective-permute-start | bytes 9224 | tf_op jit(solution)/shard_map/ppermute | solution.py:24
  432.9 9.8 %collective-permute-start.44 = (f32[3,8,32,1]{3,2,1,0:T(8,128)S(1)}, f32[3,8,32,1]{3,2,1,0:T(8,128)S(1)}, u32[]{:S(2)}, u32[]{:S(2)}) collective-permute-start(f32[3,8,32,1]{3,2,1,0:T(8,128)S(1)} %get-tuple-element.351), channel_id=1, source_target_pairs={{0,16},{16,32},{32,48},{48,64},{64,80},{80,96},{96,112},{1,17},{17... | collective-permute-start | bytes 9224 | tf_op jit(solution)/shard_map/ppermute | solution.py:22
  442.9 8.2 %collective-permute-start.47 = (f32[3,8,1,130]{3,2,1,0:T(1,128)S(1)}, f32[3,8,1,130]{3,2,1,0:T(1,128)S(1)}, u32[]{:S(2)}, u32[]{:S(2)}) collective-permute-start(f32[3,8,1,130]{3,2,1,0:T(1,128)S(1)} %get-tuple-element.296), channel_id=1, source_target_pairs={{1,0},{2,1},{3,2},{4,3},{5,4},{6,5},{7,6},{8,7},{9,8},{10,9},{11,1... | collective-permute-start | bytes 37448 | tf_op jit(solution)/shard_map/ppermute | solution.py:24
  444.2 7.6 %collective-permute-start.46 = (f32[3,8,1,130]{3,2,1,0:T(1,128)S(1)}, f32[3,8,1,130]{3,2,1,0:T(1,128)S(1)}, u32[]{:S(2)}, u32[]{:S(2)}) collective-permute-start(f32[3,8,1,130]{3,2,1,0:T(1,128)S(1)} %get-tuple-element.295), channel_id=1, source_target_pairs={{0,1},{1,2},{2,3},{3,4},{4,5},{5,6},{6,7},{7,8},{8,9},{9,10},{10,1... | collective-permute-start | bytes 37448 | tf_op jit(solution)/shard_map/ppermute | solution.py:22
  458.2 7.5 %collective-permute-start.49 = (f32[6,8,32,1]{2,1,3,0:T(8,128)S(1)}, f32[6,8,32,1]{2,1,3,0:T(8,128)S(1)}, u32[]{:S(2)}, u32[]{:S(2)}) collective-permute-start(f32[6,8,32,1]{2,1,3,0:T(8,128)S(1)} %copy.100), channel_id=1, source_target_pairs={{16,0},{32,16},{48,32},{64,48},{80,64},{96,80},{112,96},{17,1},{33... | collective-permute-start | bytes 18440 | tf_op jit(solution)/shard_map/ppermute | solution.py:24
  460.5 6.2 collective-permute-start.48
  467.4 8.0 %collective-permute-start.51 = (f32[6,8,1,130]{3,2,1,0:T(1,128)S(1)}, f32[6,8,1,130]{3,2,1,0:T(1,128)S(1)}, u32[]{:S(2)}, u32[]{:S(2)}) collective-permute-start(f32[6,8,1,130]{3,2,1,0:T(1,128)S(1)} %get-tuple-element.254), channel_id=1, source_target_pairs={{1,0},{2,1},{3,2},{4,3},{5,4},{6,5},{7,6},{8,7},{9,8},{10,9},{11,1... | collective-permute-start | bytes 74888 | tf_op jit(solution)/shard_map/ppermute | solution.py:24
  468.7 7.9 %collective-permute-start.50 = (f32[6,8,1,130]{3,2,1,0:T(1,128)S(1)}, f32[6,8,1,130]{3,2,1,0:T(1,128)S(1)}, u32[]{:S(2)}, u32[]{:S(2)}) collective-permute-start(f32[6,8,1,130]{3,2,1,0:T(1,128)S(1)} %get-tuple-element.253), channel_id=1, source_target_pairs={{0,1},{1,2},{2,3},{3,4},{4,5},{5,6},{6,7},{7,8},{8,9},{9,10},{10,1... | collective-permute-start | bytes 74888 | tf_op jit(solution)/shard_map/ppermute | solution.py:22
  479.3 10.5 %collective-permute-start.53 = (f32[3,8,32,1]{3,2,1,0:T(8,128)S(1)}, f32[3,8,32,1]{3,2,1,0:T(8,128)S(1)}, u32[]{:S(2)}, u32[]{:S(2)}) collective-permute-start(f32[3,8,32,1]{3,2,1,0:T(8,128)S(1)} %get-tuple-element.350), channel_id=1, source_target_pairs={{16,0},{32,16},{48,32},{64,48},{80,64},{96,80},{112,96},{17,1},{33... | collective-permute-start | bytes 9224 | tf_op jit(solution)/shard_map/ppermute | solution.py:24
  481.2 9.8 %collective-permute-start.52 = (f32[3,8,32,1]{3,2,1,0:T(8,128)S(1)}, f32[3,8,32,1]{3,2,1,0:T(8,128)S(1)}, u32[]{:S(2)}, u32[]{:S(2)}) collective-permute-start(f32[3,8,32,1]{3,2,1,0:T(8,128)S(1)} %get-tuple-element.349), channel_id=1, source_target_pairs={{0,16},{16,32},{32,48},{48,64},{64,80},{80,96},{96,112},{1,17},{17... | collective-permute-start | bytes 9224 | tf_op jit(solution)/shard_map/ppermute | solution.py:22
  491.2 8.0 %collective-permute-start.55 = (f32[3,8,1,130]{3,2,1,0:T(1,128)S(1)}, f32[3,8,1,130]{3,2,1,0:T(1,128)S(1)}, u32[]{:S(2)}, u32[]{:S(2)}) collective-permute-start(f32[3,8,1,130]{3,2,1,0:T(1,128)S(1)} %get-tuple-element.294), channel_id=1, source_target_pairs={{1,0},{2,1},{3,2},{4,3},{5,4},{6,5},{7,6},{8,7},{9,8},{10,9},{11,1... | collective-permute-start | bytes 37448 | tf_op jit(solution)/shard_map/ppermute | solution.py:24
  492.5 7.6 %collective-permute-start.54 = (f32[3,8,1,130]{3,2,1,0:T(1,128)S(1)}, f32[3,8,1,130]{3,2,1,0:T(1,128)S(1)}, u32[]{:S(2)}, u32[]{:S(2)}) collective-permute-start(f32[3,8,1,130]{3,2,1,0:T(1,128)S(1)} %get-tuple-element.293), channel_id=1, source_target_pairs={{0,1},{1,2},{2,3},{3,4},{4,5},{5,6},{6,7},{7,8},{8,9},{9,10},{10,1... | collective-permute-start | bytes 37448 | tf_op jit(solution)/shard_map/ppermute | solution.py:22
  507.3 7.5 %collective-permute-start.57 = (f32[6,8,32,1]{2,1,3,0:T(8,128)S(1)}, f32[6,8,32,1]{2,1,3,0:T(8,128)S(1)}, u32[]{:S(2)}, u32[]{:S(2)}) collective-permute-start(f32[6,8,32,1]{2,1,3,0:T(8,128)S(1)} %copy.104), channel_id=1, source_target_pairs={{16,0},{32,16},{48,32},{64,48},{80,64},{96,80},{112,96},{17,1},{33... | collective-permute-start | bytes 18440 | tf_op jit(solution)/shard_map/ppermute | solution.py:24
  509.5 6.2 collective-permute-start.56
  516.4 8.0 %collective-permute-start.59 = (f32[6,8,1,130]{3,2,1,0:T(1,128)S(1)}, f32[6,8,1,130]{3,2,1,0:T(1,128)S(1)}, u32[]{:S(2)}, u32[]{:S(2)}) collective-permute-start(f32[6,8,1,130]{3,2,1,0:T(1,128)S(1)} %get-tuple-element.252), channel_id=1, source_target_pairs={{1,0},{2,1},{3,2},{4,3},{5,4},{6,5},{7,6},{8,7},{9,8},{10,9},{11,1... | collective-permute-start | bytes 74888 | tf_op jit(solution)/shard_map/ppermute | solution.py:24
  517.7 7.9 %collective-permute-start.58 = (f32[6,8,1,130]{3,2,1,0:T(1,128)S(1)}, f32[6,8,1,130]{3,2,1,0:T(1,128)S(1)}, u32[]{:S(2)}, u32[]{:S(2)}) collective-permute-start(f32[6,8,1,130]{3,2,1,0:T(1,128)S(1)} %get-tuple-element.251), channel_id=1, source_target_pairs={{0,1},{1,2},{2,3},{3,4},{4,5},{5,6},{6,7},{7,8},{8,9},{9,10},{10,1... | collective-permute-start | bytes 74888 | tf_op jit(solution)/shard_map/ppermute | solution.py:22
  528.3 10.5 %collective-permute-start.61 = (f32[3,8,32,1]{3,2,1,0:T(8,128)S(1)}, f32[3,8,32,1]{3,2,1,0:T(8,128)S(1)}, u32[]{:S(2)}, u32[]{:S(2)}) collective-permute-start(f32[3,8,32,1]{3,2,1,0:T(8,128)S(1)} %get-tuple-element.348), channel_id=1, source_target_pairs={{16,0},{32,16},{48,32},{64,48},{80,64},{96,80},{112,96},{17,1},{33... | collective-permute-start | bytes 9224 | tf_op jit(solution)/shard_map/ppermute | solution.py:24
  530.3 9.8 %collective-permute-start.60 = (f32[3,8,32,1]{3,2,1,0:T(8,128)S(1)}, f32[3,8,32,1]{3,2,1,0:T(8,128)S(1)}, u32[]{:S(2)}, u32[]{:S(2)}) collective-permute-start(f32[3,8,32,1]{3,2,1,0:T(8,128)S(1)} %get-tuple-element.347), channel_id=1, source_target_pairs={{0,16},{16,32},{32,48},{48,64},{64,80},{80,96},{96,112},{1,17},{17... | collective-permute-start | bytes 9224 | tf_op jit(solution)/shard_map/ppermute | solution.py:22
  540.3 8.3 %collective-permute-start.63 = (f32[3,8,1,130]{3,2,1,0:T(1,128)S(1)}, f32[3,8,1,130]{3,2,1,0:T(1,128)S(1)}, u32[]{:S(2)}, u32[]{:S(2)}) collective-permute-start(f32[3,8,1,130]{3,2,1,0:T(1,128)S(1)} %get-tuple-element.292), channel_id=1, source_target_pairs={{1,0},{2,1},{3,2},{4,3},{5,4},{6,5},{7,6},{8,7},{9,8},{10,9},{11,1... | collective-permute-start | bytes 37448 | tf_op jit(solution)/shard_map/ppermute | solution.py:24
  541.6 7.6 %collective-permute-start.62 = (f32[3,8,1,130]{3,2,1,0:T(1,128)S(1)}, f32[3,8,1,130]{3,2,1,0:T(1,128)S(1)}, u32[]{:S(2)}, u32[]{:S(2)}) collective-permute-start(f32[3,8,1,130]{3,2,1,0:T(1,128)S(1)} %get-tuple-element.291), channel_id=1, source_target_pairs={{0,1},{1,2},{2,3},{3,4},{4,5},{5,6},{6,7},{7,8},{8,9},{9,10},{10,1... | collective-permute-start | bytes 37448 | tf_op jit(solution)/shard_map/ppermute | solution.py:22
  589.0 39.6 %all-to-all-start.2 = ((f32[2,8,256]{1,0,2:T(2,128)}), f32[2,8,256]{1,0,2:T(2,128)S(1)}, u32[]{:S(2)}, u32[]{:S(2)}) async-start(f32[2,8,256]{1,0,2:T(2,128)} %scatter_fusion.1), calls=%async_computation.2 | async-start | bytes 524288 | tf_op jit(solution)/shard_map/all_to_all | solution.py:171
  (74 other events, 506.7 us)
where the time goes:
time: 641 us; the launch traced here: 630 us
  starting transfers between devices  282 us (44%)
  waiting for transfers between devices  150 us (23%)
  local copies, waits for them, and re-layouts  107 us (17%)
  other arithmetic  82.8 us (13%)
    ppermute x32, starting transfers between devices, extended(): lax.ppermute(tail, axis, [(i, (i + 1) % count) for i in range(ends)])  180 us
    ppermute x32, waiting for transfers between devices, extended(): lax.ppermute(head, axis, [((i + 1) % count, i) for i in range(ends)])  113 us
    ppermute x32, starting transfers between devices, extended(): lax.ppermute(head, axis, [((i + 1) % count, i) for i in range(ends)])  52.5 us
    all_to_all x1, starting transfers between devices, local(): lax.all_to_all(send_cols, ('gx', 'gy'), split_axis=2, concat_axis=2, tile...  28.2 us
    unnamed x40, other arithmetic  28 us
    ppermute x32, waiting for transfers between devices, extended(): lax.ppermute(tail, axis, [(i, (i + 1) % count) for i in range(ends)])  27.1 us
    scatter x1, local copies, waits for them, and re-layouts, local(): jnp.zeros((2, depth, cols_dev), jnp.float32).at[:, :, send_index]  24.3 us
    reshape x1, local copies, waits for them, and re-layouts, resample_rows(): rows.reshape(rows.shape[0] * 3, samples)  13.7 us
  transfers between devices with their start and end apart: 67, of which 39 were waited for; matrix products, arithmetic and copies ran while one was open for 7% of the time, Pallas kernels for 0%

commit v1 on v0

v1 whole, which is shorter than its diff:
```python
import math

import jax
import jax.numpy as jnp
import numpy as np
from jax import lax
from jax.experimental import pallas as pl
from jax.experimental.pallas import tpu as pltpu
from jax.sharding import PartitionSpec as P

F32 = jnp.float32
BF16 = jnp.bfloat16

NZ, CY, CX = 8, 32, 128
STEPS = 8
SAMPLES = 4096
H = 0.25
N_GX, N_GY = 8, 16
OWNERS = N_GX * N_GY
NX = N_GX * CX
HALO = 8
ROWS = CY + 2 * HALO
PAD = 8
GROUPS = ROWS // 8
FIELDS = 12
WAVES = 9
PLANES = FIELDS * NZ
EDGES = FIELDS // 2 * GROUPS

AROUND = [(dx, dy) for dx in (-1, 0, 1) for dy in (-1, 0, 1) if (dx, dy) != (0, 0)]

VX, VY, VZ, SXX, SYY, SZZ, SXY, SXZ, SYZ = range(WAVES)

VMEM = pl.BlockSpec(memory_space=pltpu.VMEM)
SMEM = pl.BlockSpec(memory_space=pltpu.SMEM)
ANY = pl.BlockSpec(memory_space=pltpu.HBM)


FULL = pltpu.CompilerParams(vmem_limit_bytes=(64 << 20) - (512 << 10))


def lanes_of(shape):
    return lax.broadcasted_iota(jnp.int32, shape, len(shape) - 1)


def rows_of(shape):
    return lax.broadcasted_iota(jnp.int32, shape, len(shape) - 2)


def roll(value, shift):
    return pltpu.roll(value, shift % value.shape[-1], value.ndim - 1)


def three_parts(value):
    high = value.astype(BF16)
    rest = value - high.astype(F32)
    middle = rest.astype(BF16)
    low = (rest - middle.astype(F32)).astype(BF16)
    return high, middle, low


def resample_table():
    per_step = SAMPLES // STEPS
    position = np.arange(SAMPLES, dtype=np.float32) + np.float32(0.5)
    centers = (np.arange(STEPS, dtype=np.float32) + np.float32(0.5)) * np.float32(per_step)
    distance = np.abs(position[:, None] - centers[None, :]) / np.float32(per_step)
    weight = np.maximum(np.float32(0.0), np.float32(1.0) - distance)
    table = (weight / np.float32(math.sqrt(per_step))).astype(BF16)
    wide = np.zeros((SAMPLES, 128), BF16)
    wide[:, :96] = np.tile(table, (1, 12))
    return wide


def rows_kernel(state, lame, shear, buoyancy, cells, up, down, sems):
    copies = []

    def copy(src, dst):
        made = pltpu.make_async_copy(src, dst, sems.at[len(copies)])
        made.start()
        copies.append(made)

    for to, at in ((up, CY - 8), (down, 0)):
        rows = pl.ds(at, 8)
        for f in range(WAVES):
            copy(state.at[f, :, rows, :], to.at[pl.ds(f * NZ, NZ)])
        for m, ref in enumerate((lame, shear, buoyancy)):
            copy(ref.at[:, rows, :], to.at[pl.ds((WAVES + m) * NZ, NZ)])
    lane = lanes_of((8, 128))
    mine = jnp.zeros((8, 128), jnp.int32)
    for k in range(4):
        mine = jnp.where(lane == k, cells[0, k], mine)
    up[PLANES] = mine.astype(F32)
    down[PLANES] = mine.astype(F32)
    for made in copies:
        made.wait()


def edges_kernel(state, lame, shear, buoyancy, below, above, own, right, left):
    lane = lanes_of((8, 128))
    planes = [state.at[f] for f in range(WAVES)] + [lame, shear, buoyancy]
    for group in range(GROUPS):
        tails, heads = [], []
        for f, field in enumerate(planes):
            tail = jnp.zeros((8, 128), F32)
            head = jnp.zeros((8, 128), F32)
            for z in range(NZ):
                if group == 0:
                    plane = below[f * NZ + z]
                elif group == GROUPS - 1:
                    plane = above[f * NZ + z]
                else:
                    plane = field[z, 8 * group - 8 : 8 * group, :]
                tail = jnp.where(lane // 8 == 2 * z, roll(plane, 16 * z - 120), tail)
                head = jnp.where(lane // 8 == 2 * z + 1, roll(plane, 16 * z + 8), head)
            tails.append(tail)
            heads.append(head)
        for pair in range(FIELDS // 2):
            right[pair * GROUPS + group] = tails[2 * pair] + roll(tails[2 * pair + 1], 8)
            left[pair * GROUPS + group] = heads[2 * pair] + roll(heads[2 * pair + 1], -8)
    row = rows_of((8, 128))
    cells = jnp.where(row == 0, below[PLANES], jnp.where(row == 1, own[PLANES], above[PLANES]))
    right[EDGES] = cells
    left[EDGES] = cells


def column_of(row_vector):
    return jnp.transpose(jnp.broadcast_to(row_vector, (128, 128)))


def source_kernel(residual, counts, stations, table, send, held, totals, sems):
    copies = [pltpu.make_async_copy(residual.at[c], held.at[c], sems.at[c]) for c in range(3)]
    for copy in copies:
        copy.start()
    rows = held.shape[1]
    pad = jnp.zeros((1, 128 - rows), F32)
    count = column_of(jnp.concatenate([counts[...].astype(F32), pad], 1))[:rows]
    station_row = jnp.concatenate([stations[...], jnp.full((1, 128 - rows), -1, jnp.int32)], 1)
    station = column_of(station_row.astype(F32))[:rows].astype(jnp.int32)
    lane = lanes_of((rows, 128))
    total = jnp.zeros((rows, 128), F32)
    live = jnp.concatenate(
        [
            jnp.where((lane + 128 * g).astype(F32) < count, 1.0, 0.0).astype(BF16)
            for g in range(SAMPLES // 128)
        ],
        1,
    )
    for c in range(3):
        copies[c].wait()
        masked = held[c] * live
        product = jnp.dot(masked, table[...], preferred_element_type=F32)
        total = jnp.where(lane // 8 % 3 == c, product, total)
    mine = jnp.where(lane // 24 == station % 4, total, 0.0)
    mine = jnp.concatenate([mine, jnp.zeros((128 - rows, 128), F32)], 0)
    owner = rows_of((128, 128))
    names = jnp.where(owner == station_row // 4, 1.0, 0.0)
    by_owner = jnp.dot(
        names, mine, preferred_element_type=F32, precision=lax.Precision.HIGHEST
    )
    totals[0:24, :] = jnp.zeros((24, 128), F32)
    totals[152:176, :] = jnp.zeros((24, 128), F32)
    totals[24:152, :] = by_owner
    lane = lanes_of((128, 128))
    tile_y = owner % N_GY
    for d, (dx, dy) in enumerate(AROUND):
        near = totals[pl.ds(24 + dx * N_GY + dy, 128), :]
        inside = (tile_y + dy >= 0) & (tile_y + dy < N_GY) & (lane < 96)
        near = jnp.where(inside, near, 0.0)
        if d < 3:
            near = jnp.where(lane < 96, near, roll(by_owner, 96 - 32 * d))
        send[pl.ds(d, 128, stride=8), :] = near


def step_kernel(
    where_ref,
    state,
    lame,
    shear,
    buoyancy,
    own_right,
    own_left,
    from_left,
    from_right,
    from_below,
    from_above,
    forward_dilation,
    forward_shear,
    sources,
    tile_map,
    out,
    send,
    main_v,
    main_s,
    strip_v,
    strip_s,
    mats,
    mat_strips,
    fd,
    fs,
    edges,
    plane_src,
    kern,
    sems,
):
    top = PAD + HALO + CY
    wave_planes = WAVES * NZ
    copies = []

    def copy(src, dst):
        made = pltpu.make_async_copy(src, dst, sems.at[len(copies)])
        made.start()
        copies.append(made)

    for i, ref in enumerate((own_right, own_left, from_left, from_right)):
        copy(ref, edges.at[i])
    for f in range(WAVES):
        ref, p = (main_v, f * NZ) if f < 3 else (main_s, (f - 3) * NZ)
        copy(state.at[f], ref.at[pl.ds(p, NZ), pl.ds(PAD + HALO, CY), :])
    for m, ref in enumerate((lame, shear, buoyancy)):
        copy(ref, mats.at[pl.ds(m * NZ, NZ), pl.ds(HALO, CY), :])
    for ref, at in ((from_below, PAD), (from_above, top)):
        copy(ref.at[pl.ds(0, 3 * NZ)], main_v.at[:, pl.ds(at, 8), :])
        copy(ref.at[pl.ds(3 * NZ, 6 * NZ)], main_s.at[:, pl.ds(at, 8), :])
        copy(ref.at[pl.ds(wave_planes, 3 * NZ)], mats.at[:, pl.ds(at - PAD, 8), :])
    copy(forward_dilation, fd)
    copy(forward_shear, fs)

    zero = jnp.zeros((8, 128), F32)
    for ref in (main_v, main_s, strip_v, strip_s):
        for p in range(ref.shape[0]):
            ref[p, 0:8, :] = zero
            ref[p, top + 8 : top + 16, :] = zero
    for p in range(2 * NZ):
        for g in range(CY // 8):
            kern[pl.ds(p * CY + 8 * g, 8), :] = zero

    me, tile_x, tile_y = where_ref[0], where_ref[1], where_ref[2]
    lane = lanes_of((8, 128))
    row = rows_of((8, 128))

    def add_sender(i, carry):
        block = sources[pl.ds(pl.multiple_of(i * 32, 32), 32), :]
        return carry + (block[0:8] + block[8:16]) + (block[16:24] + block[24:32])

    got = lax.fori_loop(0, OWNERS // 4, add_sender, zero)
    own = zero
    for d in range(3):
        own = jnp.where(lane // 32 == d, roll(got, 32 + 32 * d)[d : d + 1], own)
    own = jnp.where((row == 0) & (lane < 96), own, 0.0)
    full = jnp.concatenate([got, own, jnp.zeros((112, 128), F32)], 0)
    turned = jnp.transpose(full)
    values = jnp.zeros((24, 128), F32)
    lane24 = lanes_of((24, 128))
    for k in range(4):
        part = turned[k * 24 : (k + 1) * 24]
        values = jnp.where(lane24 // 16 == k, roll(part, 16 * k), values)
    high, middle, low = three_parts(values)
    high, middle, low = high.astype(F32), middle.astype(F32), low.astype(F32)
    values = jnp.concatenate([jnp.where(lane24 < 64, high, roll(middle, 64)), low], 1)

    for made in copies[:4]:
        made.wait()
    row16 = rows_of((16, 128))
    cells = jnp.zeros((16, 128), F32)
    for d, (dx, dy) in enumerate(AROUND + [(0, 0)]):
        line = edges[(0, 3, 2)[dx], EDGES][dy + 1 : dy + 2]
        cells = jnp.where(row16 == d, line, cells)
    turned = jnp.transpose(jnp.concatenate([cells, jnp.zeros((112, 128), F32)], 0))
    lane1 = lanes_of((1, 128))
    across = jnp.zeros((1, 128), F32)
    for k in range(4):
        across = jnp.where(lane1 // 16 == k, roll(turned[k : k + 1], 16 * k), across)
    across = jnp.where(lane1 < 64, across, roll(across, 64)).astype(jnp.int32)
    across = jnp.concatenate([across, across], 1)
    along = jnp.concatenate([jnp.broadcast_to(cells[:, k : k + 1], (16, 256)) for k in range(4)], 0)
    along = along.astype(jnp.int32)
    at_row = rows_of((ROWS, 256)) == across // NX - tile_y * CY + HALO
    at_x = along % NX - tile_x * CX
    n = lanes_of((64, 256))
    hit = (n == at_x) & (n < 128)
    hit = hit | ((n - 128 == at_x + 8) & (n >= 128) & (n < 144))
    hit = hit | ((n - 192 == at_x - 120) & (n >= 192) & (n < 208))
    hit = jnp.where(hit, 1.0, 0.0).astype(BF16)
    hit = jnp.concatenate([hit, hit, hit, hit], 0)
    spread = jnp.concatenate(
        [jnp.where(at_row, values[i : i + 1], 0.0).astype(BF16) for i in range(24)], 0
    )
    plane_src[...] = jnp.dot(spread, hit, preferred_element_type=F32)

    low = lane // 8 % 2 == 0
    for pair in range(FIELDS // 2):
        for g in range(GROUPS):
            sr, sl, rl, rr = (edges[i, pair * GROUPS + g] for i in range(4))
            made = (
                jnp.where(low, rl, sl),
                jnp.where(low, sr, rr),
                jnp.where(low, roll(rl, -8), roll(sl, 8)),
                jnp.where(low, roll(sr, -8), roll(rr, 8)),
            )
            for i in range(4):
                at = 4 * pair + i
                if at < 6:
                    strip_v[at, PAD + 8 * g : PAD + 8 * g + 8, :] = made[i]
                elif at < 2 * WAVES:
                    strip_s[at - 6, PAD + 8 * g : PAD + 8 * g + 8, :] = made[i]
                else:
                    mat_strips[at - 2 * WAVES, 8 * g : 8 * g + 8, :] = made[i]
    for made in copies[4:]:
        made.wait()

    last = lane == 127
    first = lane == 0

    def mload(f, z, r):
        return main_v[f * NZ + z, pl.ds(r, 8), :] if f < 3 else main_s[(f - 3) * NZ + z, pl.ds(r, 8), :]

    def sload(f, side, r):
        return strip_v[2 * f + side, pl.ds(r, 8), :] if f < 3 else strip_s[2 * f - 6 + side, pl.ds(r, 8), :]

    def next_x(value, edge, z):
        return jnp.where(last, roll(edge, 127 - (16 * z + 8)), roll(value, -1))

    def prev_x(value, edge, z):
        return jnp.where(first, roll(edge, -(16 * z + 7)), roll(value, 1))

    def next_z(value):
        return jnp.where(lane < 112, roll(value, -16), 0.0)

    def prev_z(value):
        return jnp.where(lane >= 16, roll(value, 16), 0.0)

    def velocity_group(step, g):
        r = PAD + 8 * g
        edges = {(f, s): sload(f, s, r) for f in range(SXX, WAVES) for s in range(2)}
        below_xz = below_yz = zero
        zz = mload(SZZ, 0, r)
        for z in range(NZ):
            xx, xy, yy, xz, yz = (mload(f, z, r) for f in (SXX, SXY, SYY, SXZ, SYZ))
            above_zz = mload(SZZ, z + 1, r) if z < NZ - 1 else zero
            ax = (next_x(xx, edges[SXX, 1], z) - xx) + (xy - mload(SXY, z, r - 1)) + (xz - below_xz)
            ay = (xy - prev_x(xy, edges[SXY, 0], z)) + (mload(SYY, z, r + 1) - yy) + (yz - below_yz)
            az = (xz - prev_x(xz, edges[SXZ, 0], z)) + (yz - mload(SYZ, z, r - 1)) + (above_zz - zz)
            below_xz, below_yz, zz = xz, yz, above_zz
            hb = H * mats[2 * NZ + z, pl.ds(r - PAD, 8), :]
            for c, a in enumerate((ax, ay, az)):
                if z == 0:
                    at = pl.multiple_of((c * STEPS + step) * ROWS + 8 * g, 8)
                    a = a + plane_src[pl.ds(at, 8), 0:128]
                main_v[c * NZ + z, pl.ds(r, 8), :] = mload(c, z, r) + hb * a
        for side in range(2):
            xx, yy, zz, xy, xz, yz = (edges[f, side] for f in (SXX, SYY, SZZ, SXY, SXZ, SYZ))
            ax = (roll(xx, -1) - xx) + (xy - sload(SXY, side, r - 1)) + (xz - prev_z(xz))
            ay = (xy - roll(xy, 1)) + (sload(SYY, side, r + 1) - yy) + (yz - prev_z(yz))
            az = (xz - roll(xz, 1)) + (yz - sload(SYZ, side, r - 1)) + (next_z(zz) - zz)
            hb = H * mat_strips[2 * 2 + side, pl.ds(r - PAD, 8), :]
            for c, a in enumerate((ax, ay, az)):
                at = pl.multiple_of((c * STEPS + step) * ROWS + 8 * g, 8)
                src = plane_src[pl.ds(at, 8), 128:256]
                src = jnp.where(lane < 16, roll(src, 64) if side else src, 0.0)
                strip_v[2 * c + side, pl.ds(r, 8), :] = sload(c, side, r) + hb * (a + src)

    def stress_group(g, forward):
        r = PAD + 8 * g
        edges = {(f, s): sload(f, s, r) for f in range(3) for s in range(2)}
        vx, vy = mload(VX, 0, r), mload(VY, 0, r)
        below_vz = zero
        for z in range(NZ):
            vz = mload(VZ, z, r)
            above_vx = mload(VX, z + 1, r) if z < NZ - 1 else zero
            above_vy = mload(VY, z + 1, r) if z < NZ - 1 else zero
            exx = vx - prev_x(vx, edges[VX, 0], z)
            eyy = vy - mload(VY, z, r - 1)
            ezz = vz - below_vz
            dilation = exx + eyy + ezz
            exy = (mload(VX, z, r + 1) - vx) + (next_x(vy, edges[VY, 1], z) - vy)
            exz = (above_vx - vx) + (next_x(vz, edges[VZ, 1], z) - vz)
            eyz = (above_vy - vy) + (mload(VZ, z, r + 1) - vz)
            vx, vy, below_vz = above_vx, above_vy, vz
            pressure = H * mats[z, pl.ds(r - PAD, 8), :] * dilation
            hm = H * mats[NZ + z, pl.ds(r - PAD, 8), :]
            hm2 = hm + hm
            for f, change in (
                (SXX, pressure + hm2 * exx),
                (SYY, pressure + hm2 * eyy),
                (SZZ, pressure + hm2 * ezz),
                (SXY, hm * exy),
                (SXZ, hm * exz),
                (SYZ, hm * eyz),
            ):
                main_s[(f - 3) * NZ + z, pl.ds(r, 8), :] = mload(f, z, r) + change
            if forward is not None:
                for k, strain in ((0, dilation), (1, exy)):
                    at = pl.ds((k * NZ + z) * CY + 8 * (g - 1), 8)
                    kern[at, :] = kern[at, :] + forward[k][z] * (H * strain)
        for side in range(2):
            vx, vy, vz = (edges[f, side] for f in range(3))
            exx = vx - roll(vx, 1)
            eyy = vy - sload(VY, side, r - 1)
            ezz = vz - prev_z(vz)
            exy = (sload(VX, side, r + 1) - vx) + (roll(vy, -1) - vy)
            exz = (next_z(vx) - vx) + (roll(vz, -1) - vz)
            eyz = (next_z(vy) - vy) + (sload(VZ, side, r + 1) - vz)
            pressure = H * mat_strips[side, pl.ds(r - PAD, 8), :] * (exx + eyy + ezz)
            hm = H * mat_strips[2 + side, pl.ds(r - PAD, 8), :]
            hm2 = hm + hm
            for f, change in (
                (SXX, pressure + hm2 * exx),
                (SYY, pressure + hm2 * eyy),
                (SZZ, pressure + hm2 * ezz),
                (SXY, hm * exy),
                (SXZ, hm * exz),
                (SYZ, hm * eyz),
            ):
                strip_s[2 * f - 6 + side, pl.ds(r, 8), :] = sload(f, side, r) + change

    def one_step(step, carry):
        for g in range(GROUPS):
            velocity_group(step, g)
        stress_group(0, None)
        for i in range(CY // 16):
            both = [
                [ref[step, z, 16 * i : 16 * i + 16, :].astype(F32) for z in range(NZ)]
                for ref in (fd, fs)
            ]
            for half in range(2):
                part = [[v[8 * half : 8 * half + 8] for v in vs] for vs in both]
                stress_group(1 + 2 * i + half, part)
        stress_group(GROUPS - 1, None)
        return carry

    lax.fori_loop(0, STEPS, one_step, 0)

    outs = []
    for f in range(WAVES):
        ref, p = (main_v, f * NZ) if f < 3 else (main_s, (f - 3) * NZ)
        made = pltpu.make_async_copy(
            ref.at[pl.ds(p, NZ), pl.ds(PAD + HALO, CY), :], out.at[f], sems.at[f]
        )
        made.start()
        outs.append(made)

    slot = tile_map[...] // 256 * 2 + (tile_map[...] % 256 - 2 * me)
    slot = slot.astype(F32)
    line = jnp.zeros((8, 128), F32)
    for y in range(8):
        half = slot[:, 128 * (y // 4) : 128 * (y // 4) + 128]
        line = jnp.where(row == y, roll(half, -32 * (y % 4)), line)
    widen = jnp.where(lanes_of((128, 128)) // 4 == rows_of((128, 128)), 1.0, 0.0).astype(BF16)
    line = jnp.where(lane < 32, line, 0.0).astype(BF16)
    line = jnp.dot(line, widen, preferred_element_type=F32)
    place = rows_of((256, 128)).astype(F32)
    put = jnp.concatenate(
        [jnp.where(line[y : y + 1] == place, 1.0 / 16, 0.0).astype(BF16) for y in range(8)], 1
    )
    sums = []
    for y in range(8):
        parts = [kern[pl.ds(4 * y + i, 2 * NZ, stride=CY), :] for i in range(4)]
        sums.append((parts[0] + parts[1]) + (parts[2] + parts[3]))
    sums = jnp.concatenate(three_parts(jnp.concatenate(sums, 1)), 0)
    placed = lax.dot_general(put, sums, (((1,), (1,)), ((), ())), preferred_element_type=F32)
    placed = placed[:, 0:16] + placed[:, 16:32] + placed[:, 32:48]
    send[...] = jnp.concatenate([placed, jnp.zeros((256, 112), F32)], 1)
    for made in outs:
        made.wait()


def turn_kernel(got, out):
    out[...] = jnp.transpose(got[...])[0:16]


def shift(value, dx, dy):
    pairs = [
        (x * N_GY + y, (x + dx) * N_GY + y + dy)
        for x in range(N_GX)
        for y in range(N_GY)
        if 0 <= x + dx < N_GX and 0 <= y + dy < N_GY
    ]
    return lax.ppermute(value, ("gx", "gy"), pairs)


def shape(*dims):
    return jax.ShapeDtypeStruct(dims, F32)


def cost(flops, data):
    return pl.CostEstimate(flops=flops, bytes_accessed=data, transcendentals=0)


def local(
    adjoint_state,
    lame_lambda,
    shear_modulus,
    buoyancy,
    forward_dilation,
    forward_shear,
    residual,
    sample_counts,
    station_list,
    receiver_cells,
    tile_map,
):
    tile_x = lax.axis_index("gx")
    tile_y = lax.axis_index("gy")
    here = jnp.stack([tile_x * N_GY + tile_y, tile_x, tile_y]).astype(jnp.int32)
    rows_dev = residual.shape[0]

    up, down = pl.pallas_call(
        rows_kernel,
        out_shape=(shape(PLANES + 1, 8, 128), shape(PLANES + 1, 8, 128)),
        in_specs=[ANY] * 4 + [SMEM],
        out_specs=(VMEM, VMEM),
        scratch_shapes=[pltpu.SemaphoreType.DMA((24,))],
        cost_estimate=cost(0, 1 << 21),
    )(adjoint_state, lame_lambda, shear_modulus, buoyancy, receiver_cells.reshape(1, 4))
    from_below = shift(up, 0, 1)
    from_above = shift(down, 0, -1)

    send = pl.pallas_call(
        source_kernel,
        out_shape=shape(OWNERS * 8, 128),
        in_specs=[ANY, VMEM, VMEM, VMEM],
        out_specs=VMEM,
        scratch_shapes=[
            pltpu.VMEM((3, rows_dev, SAMPLES), BF16),
            pltpu.VMEM((176, 128), F32),
            pltpu.SemaphoreType.DMA((3,)),
        ],
        compiler_params=FULL,
        cost_estimate=cost(1 << 30, 1 << 22),
    )(
        jnp.transpose(residual, (1, 0, 2)),
        sample_counts.reshape(1, rows_dev),
        station_list.reshape(1, rows_dev),
        jnp.asarray(resample_table()),
    )
    sources = lax.all_to_all(send, ("gx", "gy"), 0, 0, tiled=True)

    right, left = pl.pallas_call(
        edges_kernel,
        out_shape=(shape(EDGES + 1, 8, 128), shape(EDGES + 1, 8, 128)),
        in_specs=[VMEM] * 7,
        out_specs=(VMEM, VMEM),
        cost_estimate=cost(1 << 20, 1 << 21),
    )(adjoint_state, lame_lambda, shear_modulus, buoyancy, from_below, from_above, up)
    from_left = shift(right, 1, 0)
    from_right = shift(left, -1, 0)

    wave_planes = WAVES * NZ
    reach = ROWS + 2 * PAD
    adjoint_out, send = pl.pallas_call(
        step_kernel,
        out_shape=(shape(WAVES, NZ, CY, CX), shape(256, 128)),
        in_specs=[SMEM] + [ANY] * 12 + [VMEM, VMEM],
        out_specs=(ANY, VMEM),
        scratch_shapes=[
            pltpu.VMEM((3 * NZ, reach, 128), F32),
            pltpu.VMEM((6 * NZ, reach, 128), F32),
            pltpu.VMEM((6, reach, 128), F32),
            pltpu.VMEM((12, reach, 128), F32),
            pltpu.VMEM((3 * NZ, ROWS, 128), F32),
            pltpu.VMEM((6, ROWS, 128), F32),
            pltpu.VMEM((STEPS, NZ, CY, CX), BF16),
            pltpu.VMEM((STEPS, NZ, CY, CX), BF16),
            pltpu.VMEM((4, EDGES + 1, 8, 128), F32),
            pltpu.VMEM((24 * ROWS, 256), F32),
            pltpu.VMEM((2 * NZ * CY, 128), F32),
            pltpu.SemaphoreType.DMA((32,)),
        ],
        compiler_params=FULL,
        cost_estimate=cost(1 << 27, 1 << 23),
    )(
        here,
        adjoint_state,
        lame_lambda,
        shear_modulus,
        buoyancy,
        right,
        left,
        from_left,
        from_right,
        from_below,
        from_above,
        forward_dilation,
        forward_shear,
        sources,
        tile_map.reshape(1, 256),
    )
    got = lax.all_to_all(send, ("gx", "gy"), 0, 0, tiled=True)
    kernels = pl.pallas_call(
        turn_kernel,
        out_shape=shape(16, 256),
        in_specs=[VMEM],
        out_specs=VMEM,
    )(got)
    return kernels.reshape(2, NZ, 256), adjoint_out


def solution(mesh):
    in_specs = (
        P(None, None, "gy", "gx"),
        P(None, "gy", "gx"),
        P(None, "gy", "gx"),
        P(None, "gy", "gx"),
        P(None, None, "gy", "gx"),
        P(None, None, "gy", "gx"),
        P(("gx", "gy"), None, None),
        P(("gx", "gy")),
        P(("gx", "gy")),
        P(("gx", "gy")),
        P(("gx", "gy")),
    )
    out_specs = (P(None, None, ("gx", "gy")), P(None, None, "gy", "gx"))
    return jax.shard_map(local, mesh=mesh, in_specs=in_specs, out_specs=out_specs, check_vma=False)
```

time: 641 us -> 78.6 us (0.12); the launches traced: 630 us -> 78.1 us
  starting transfers between devices: 282 us -> 25 us
  waiting for transfers between devices: 150 us -> 4.12 us
  local copies, waits for them, and re-layouts: 107 us -> 1.42 us
  other arithmetic: 82.8 us -> 0.67 us
  Pallas kernels: 0 us -> 26.5 us
  blocking collectives: 0 us -> 19.7 us
    ppermute x64 -> x4, starting transfers between devices: 232 us -> 12.1 us  [shift(): return lax.ppermute(value, ('gx', 'gy'), pairs)]
    ppermute x64 -> x4, waiting for transfers between devices: 140 us -> 0.82 us  [shift(): return lax.ppermute(value, ('gx', 'gy'), pairs)]
    scatter x3 -> x0, local copies, waits for them, and re-layouts: 38.3 us -> none  [the longest x1 24.3 us: local(): jnp.zeros((2, depth, cols_dev), jnp.float32).at[:, :, send_index]]
    all_to_all x3 -> x1, starting transfers between devices: 49.9 us -> 12.9 us  [local(): sources = lax.all_to_all(send, ('gx', 'gy'), 0, 0, tiled=True)]
    unnamed x40 -> x0, other arithmetic: 28 us -> none
    pallas_call x0 -> x5, Pallas kernels: none -> 26.5 us  [the longest x1 13.9 us: local(): pl.pallas_call(step_kernel, out_shape=(shape(WAVES, NZ, CY, CX), shape(25...]
    all_to_all x0 -> x1, blocking collectives: none -> 19.7 us  [local(): got = lax.all_to_all(send, ('gx', 'gy'), 0, 0, tiled=True)]
    slice x31 -> x0, local copies, waits for them, and re-layouts: 15.3 us -> none  [the longest x23 9.9 us: extended(): lax.slice_in_dim(cells, cells.shape[dim] - width, cells.shape[dim], axis=...]
  transfers between devices with their start and end apart: 67 -> 5, of which waited for: 39 -> 2; matrix products, arithmetic and copies ran while one was open for 7% -> 1% of each run, Pallas kernels for 0% -> 11%
where the time goes in v1:
time: 78.6 us; the launch traced here: 78.1 us
  Pallas kernels  26.5 us (34%)
  starting transfers between devices  25 us (32%)
  blocking collectives  19.7 us (25%)
  waiting for transfers between devices  4.12 us (5%)
  local copies, waits for them, and re-layouts  1.42 us (2%)
    all_to_all x1, blocking collectives, local(): got = lax.all_to_all(send, ('gx', 'gy'), 0, 0, tiled=True)  19.7 us
    pallas_call x1, Pallas kernels, local(): pl.pallas_call(step_kernel, out_shape=(shape(WAVES, NZ, CY, CX), shape(25...  13.9 us
    all_to_all x1, starting transfers between devices, local(): sources = lax.all_to_all(send, ('gx', 'gy'), 0, 0, tiled=True)  12.9 us
    ppermute x4, starting transfers between devices, shift(): return lax.ppermute(value, ('gx', 'gy'), pairs)  12.1 us
    pallas_call x1, Pallas kernels, local(): pl.pallas_call(source_kernel, out_shape=shape(OWNERS * 8, 128), in_specs=...  4.66 us
    pallas_call x1, Pallas kernels, local(): pl.pallas_call(edges_kernel, out_shape=(shape(EDGES + 1, 8, 128), shape(E...  3.55 us
    all_to_all x1, waiting for transfers between devices, local(): sources = lax.all_to_all(send, ('gx', 'gy'), 0, 0, tiled=True)  3.3 us
    pallas_call x1, Pallas kernels, local(): pl.pallas_call(rows_kernel, out_shape=(shape(PLANES + 1, 8, 128), shape(P...  2.88 us
  transfers between devices with their start and end apart: 5, of which 2 were waited for; matrix products, arithmetic and copies ran while one was open for 1% of the time, Pallas kernels for 11%

profile of v1, /device:TPU:1, one launch (start us, length us, event | category | flops | bytes accessed | tf_op | source)
XLA Modules:
  0.0 78.1 jit_solution(18193989640473292457)
XLA Ops:
  0.6 2.9 %shard_map.131 = (f32[97,8,128]{2,1,0:T(8,128)}, f32[97,8,128]{2,1,0:T(8,128)}) custom-call(f32[9,8,32,128]{3,2,1,0:T(8,128)} %state.5, f32[8,32,128]{2,1,0:T(8,128)} %lame.5, f32[8,32,128]{2,1,0:T(8,128)} %shear.5, f32[8,32,128]{2,1,0:T(8,128)} %buoyancy.5, s32[1,4]{1,0:T(1,128)} %bitcast.18), custom_call_target="tpu_custom_call" | custom-call | bytes 2097152 | tf_op jit(solution)/shard_map/pallas_call | solution.py:507
  3.5 1.3 %collective-permute-start.1 = (f32[97,8,128]{2,1,0:T(8,128)}, f32[97,8,128]{2,1,0:T(8,128)S(1)}, u32[]{:S(2)}, u32[]{:S(2)}) collective-permute-start(f32[97,8,128]{2,1,0:T(8,128)} %get-tuple-element.9), channel_id=1, source_target_pairs={{1,0},{2,1},{3,2},{4,3},{5,4},{6,5},{7,6},{8,7},{9,8},{10,9},{11,1... | collective-permute-start | bytes 1191944 | tf_op jit(solution)/shard_map/ppermute | solution.py:478
  4.8 5.3 %collective-permute-start = (f32[97,8,128]{2,1,0:T(8,128)}, f32[97,8,128]{2,1,0:T(8,128)}, u32[]{:S(2)}, u32[]{:S(2)}) collective-permute-start(f32[97,8,128]{2,1,0:T(8,128)} %get-tuple-element.8.own), channel_id=1, source_target_pairs={{0,1},{1,2},{2,3},{3,4},{4,5},{5,6},{6,7},{7,8},{8,9},{9,10},{10,1... | collective-permute-start | bytes 1191944 | tf_op jit(solution)/shard_map/ppermute | solution.py:478
  10.1 4.7 %shard_map.133 = f32[1024,128]{1,0:T(8,128)} custom-call(bf16[3,96,4096]{2,1,0:T(8,128)(2,1)} %bitcast.19, s32[1,96]{1,0:T(1,128)} %bitcast.20, s32[1,96]{1,0:T(1,128)} %bitcast.21, bf16[4096,128]{1,0:T(8,128)(2,1)} %constant.13.clone.table), custom_call_target="tpu_custom_call" | custom-call | flops 1073741824 | bytes 4194304 | tf_op jit(solution)/shard_map/pallas_call | solution.py:518
  14.8 12.9 %all-to-all-start = ((f32[128,8,128]{2,1,0:T(8,128)}), f32[128,8,128]{2,1,0:T(8,128)}, u32[]{:S(2)}, u32[]{:S(2)}) async-start(f32[128,8,128]{2,1,0:T(8,128)} %bitcast.13), calls=%async_computation | async-start | bytes 1048576 | tf_op jit(solution)/shard_map/all_to_all | solution.py:536
  27.7 0.0 collective-permute-done.1.above.from_above
  27.7 0.0 copy-start
  27.7 0.0 collective-permute-done.below.from_below
  27.7 0.8 copy-done
  28.5 3.5 %shard_map.132 = (f32[37,8,128]{2,1,0:T(8,128)}, f32[37,8,128]{2,1,0:T(8,128)}) custom-call(f32[9,8,32,128]{3,2,1,0:T(8,128)} %state.5, f32[8,32,128]{2,1,0:T(8,128)} %lame.5, f32[8,32,128]{2,1,0:T(8,128)} %shear.5, f32[8,32,128]{2,1,0:T(8,128)} %buoyancy.5, f32[97,8,128]{2,1,0:T(8,128)} %collective-permute-done.below.from_below, f32[97,8,128]{2,1,0:T(8,128)} %copy-done, ...), custom_call_target="tpu_custom_call" | custom-call | flops 1048576 | bytes 2097152 | tf_op jit(solution)/shard_map/pallas_call | solution.py:538
  32.0 3.5 %collective-permute-start.2 = (f32[37,8,128]{2,1,0:T(8,128)}, f32[37,8,128]{2,1,0:T(8,128)S(1)}, u32[]{:S(2)}, u32[]{:S(2)}) collective-permute-start(f32[37,8,128]{2,1,0:T(8,128)} %get-tuple-element.10.own_right), channel_id=1, source_target_pairs={{0,16},{1,17},{2,18},{3,19},{4,20},{5,21},{6,22},{7,23},{8,24},{9,... | collective-permute-start | bytes 454664 | tf_op jit(solution)/shard_map/ppermute | solution.py:478
  35.6 1.9 %collective-permute-start.3 = (f32[37,8,128]{2,1,0:T(8,128)}, f32[37,8,128]{2,1,0:T(8,128)S(1)}, u32[]{:S(2)}, u32[]{:S(2)}) collective-permute-start(f32[37,8,128]{2,1,0:T(8,128)} %get-tuple-element.11.own_left), channel_id=1, source_target_pairs={{16,0},{17,1},{18,2},{19,3},{20,4},{21,5},{22,6},{23,7},{24,8},{25... | collective-permute-start | bytes 454664 | tf_op jit(solution)/shard_map/ppermute | solution.py:478
  37.5 0.7 pad_add_fusion.where_ref
  38.2 3.3 %all-to-all-done = f32[128,8,128]{2,1,0:T(8,128)} async-done(((f32[128,8,128]{2,1,0:T(8,128)}), f32[128,8,128]{2,1,0:T(8,128)}, u32[]{:S(2)}, u32[]{:S(2)}) %all-to-all-start) | async-done | bytes 524320 | tf_op jit(solution)/shard_map/all_to_all | solution.py:536
  41.5 0.0 collective-permute-done.2.from_left
  41.5 0.0 copy-start.1
  41.5 0.8 %collective-permute-done.3.from_right = f32[37,8,128]{2,1,0:T(8,128)S(1)} collective-permute-done((f32[37,8,128]{2,1,0:T(8,128)}, f32[37,8,128]{2,1,0:T(8,128)S(1)}, u32[]{:S(2)}, u32[]{:S(2)}) %collective-permute-start.3) | collective-permute-done | bytes 151584 | tf_op jit(solution)/shard_map/ppermute | solution.py:478
  42.3 0.0 copy-start.2
  42.3 0.0 copy-done.1
  42.3 0.7 copy-done.2
  42.9 13.9 %shard_map.134 = (f32[9,8,32,128]{3,2,1,0:T(8,128)}, f32[256,128]{1,0:T(8,128)}) custom-call(s32[3]{0:T(128)} %pad_add_fusion.where_ref, f32[9,8,32,128]{3,2,1,0:T(8,128)} %state.5, f32[8,32,128]{2,1,0:T(8,128)} %lame.5, f32[8,32,128]{2,1,0:T(8,128)} %shear.5, f32[8,32,128]{2,1,0:T(8,128)} %buoyancy.5, f32[37,8,128]{2,1,0:T(8,128)} %get-tuple-element.10.own_right, ...), custom_call_target="tpu_custom_call" | custom-call | flops 134217728 | bytes 8388608 | tf_op jit(solution)/shard_map/pallas_call | solution.py:550
  56.8 19.7 %all_to_all.22 = f32[128,2,128]{2,1,0:T(2,128)} all-to-all(f32[128,2,128]{2,1,0:T(2,128)} %bitcast.15), channel_id=1, replica_groups=mesh['gx'=8,'gy'=16] {'gx','gy'}, dimensions={0} | all-to-all | bytes 262144 | tf_op jit(solution)/shard_map/all_to_all | solution.py:588
  76.5 1.6 %shard_map.135 = f32[16,256]{1,0:T(8,128)} custom-call(f32[256,128]{1,0:T(8,128)} %bitcast.14), custom_call_target="tpu_custom_call" | custom-call | tf_op jit(solution)/shard_map/pallas_call | solution.py:589
Async XLA Ops:
  3.5 24.2 %collective-permute-start.1 = (f32[97,8,128]{2,1,0:T(8,128)}, f32[97,8,128]{2,1,0:T(8,128)S(1)}, u32[]{:S(2)}, u32[]{:S(2)}) collective-permute-start(f32[97,8,128]{2,1,0:T(8,128)} %get-tuple-element.9), channel_id=1, source_target_pairs={{1,0},{2,1},{3,2},{4,3},{5,4},{6,5},{7,6},{8,7},{9,8},{10,9},{11,1... | collective-permute-start | bytes 1191944 | tf_op jit(solution)/shard_map/ppermute | solution.py:478
  4.8 22.9 %collective-permute-start = (f32[97,8,128]{2,1,0:T(8,128)}, f32[97,8,128]{2,1,0:T(8,128)}, u32[]{:S(2)}, u32[]{:S(2)}) collective-permute-start(f32[97,8,128]{2,1,0:T(8,128)} %get-tuple-element.8.own), channel_id=1, source_target_pairs={{0,1},{1,2},{2,3},{3,4},{4,5},{5,6},{6,7},{7,8},{8,9},{9,10},{10,1... | collective-permute-start | bytes 1191944 | tf_op jit(solution)/shard_map/ppermute | solution.py:478
  14.8 26.7 %all-to-all-start = ((f32[128,8,128]{2,1,0:T(8,128)}), f32[128,8,128]{2,1,0:T(8,128)}, u32[]{:S(2)}, u32[]{:S(2)}) async-start(f32[128,8,128]{2,1,0:T(8,128)} %bitcast.13), calls=%async_computation | async-start | bytes 1048576 | tf_op jit(solution)/shard_map/all_to_all | solution.py:536
  27.7 0.8 copy-start
  32.0 9.4 %collective-permute-start.2 = (f32[37,8,128]{2,1,0:T(8,128)}, f32[37,8,128]{2,1,0:T(8,128)S(1)}, u32[]{:S(2)}, u32[]{:S(2)}) collective-permute-start(f32[37,8,128]{2,1,0:T(8,128)} %get-tuple-element.10.own_right), channel_id=1, source_target_pairs={{0,16},{1,17},{2,18},{3,19},{4,20},{5,21},{6,22},{7,23},{8,24},{9,... | collective-permute-start | bytes 454664 | tf_op jit(solution)/shard_map/ppermute | solution.py:478
  35.6 6.7 %collective-permute-start.3 = (f32[37,8,128]{2,1,0:T(8,128)}, f32[37,8,128]{2,1,0:T(8,128)S(1)}, u32[]{:S(2)}, u32[]{:S(2)}) collective-permute-start(f32[37,8,128]{2,1,0:T(8,128)} %get-tuple-element.11.own_left), channel_id=1, source_target_pairs={{16,0},{17,1},{18,2},{19,3},{20,4},{21,5},{22,6},{23,7},{24,8},{25... | collective-permute-start | bytes 454664 | tf_op jit(solution)/shard_map/ppermute | solution.py:478
  41.5 0.8 %copy-start.1 = (f32[37,8,128]{2,1,0:T(8,128)}, f32[37,8,128]{2,1,0:T(8,128)S(1)}, u32[]{:S(2)}) copy-start(f32[37,8,128]{2,1,0:T(8,128)S(1)} %collective-permute-done.2.from_left) | copy-start | bytes 454660
  42.3 0.7 copy-start.2

commit v2 on v1

--- a/solution.py
+++ b/solution.py
@@ -36,7 +36,7 @@
 ANY = pl.BlockSpec(memory_space=pltpu.HBM)
 
 
-FULL = pltpu.CompilerParams(vmem_limit_bytes=(64 << 20) - (512 << 10))
+PART = pltpu.CompilerParams(vmem_limit_bytes=24 << 20)
 
 
 def lanes_of(shape):
@@ -71,45 +71,60 @@
     return wide
 
 
-def rows_kernel(state, lame, shear, buoyancy, cells, up, down, sems):
+def at_plane(velocity, stress, mats, f):
+    if f < 3:
+        return velocity, f * NZ
+    if f < WAVES:
+        return stress, (f - 3) * NZ
+    return mats, (f - WAVES) * NZ
+
+
+def rows_kernel(state, lame, shear, buoyancy, cells, velocity, stress, mats, up, down, sems):
     copies = []
-
-    def copy(src, dst):
-        made = pltpu.make_async_copy(src, dst, sems.at[len(copies)])
-        made.start()
-        copies.append(made)
-
-    for to, at in ((up, CY - 8), (down, 0)):
-        rows = pl.ds(at, 8)
-        for f in range(WAVES):
-            copy(state.at[f, :, rows, :], to.at[pl.ds(f * NZ, NZ)])
-        for m, ref in enumerate((lame, shear, buoyancy)):
-            copy(ref.at[:, rows, :], to.at[pl.ds((WAVES + m) * NZ, NZ)])
+    for f in range(FIELDS):
+        to, p = at_plane(velocity, stress, mats, f)
+        source = state.at[f] if f < WAVES else (lame, shear, buoyancy)[f - WAVES]
+        to = to.at[pl.ds(p, NZ), pl.ds(PAD + HALO, CY), :]
+        copies.append(pltpu.make_async_copy(source, to, sems.at[f]))
+        copies[f].start()
+    zero = jnp.zeros((8, 128), F32)
+    for ref in (velocity, stress, mats):
+        for p in range(ref.shape[0]):
+            ref[p, 0:8, :] = zero
+            ref[p, 56:64, :] = zero
     lane = lanes_of((8, 128))
     mine = jnp.zeros((8, 128), jnp.int32)
     for k in range(4):
         mine = jnp.where(lane == k, cells[0, k], mine)
     up[PLANES] = mine.astype(F32)
     down[PLANES] = mine.astype(F32)
-    for made in copies:
-        made.wait()
-
-
-def edges_kernel(state, lame, shear, buoyancy, below, above, own, right, left):
+    for f in range(FIELDS):
+        copies[f].wait()
+        ref, p = at_plane(velocity, stress, mats, f)
+        for z in range(NZ):
+            down[f * NZ + z] = ref[p + z, 16:24, :]
+            up[f * NZ + z] = ref[p + z, 40:48, :]
+
+
+def edges_kernel(v_in, s_in, m_in, below, above, own, velocity, stress, mats, right, left):
+    del v_in, s_in, m_in
     lane = lanes_of((8, 128))
-    planes = [state.at[f] for f in range(WAVES)] + [lame, shear, buoyancy]
+    for f in range(FIELDS):
+        ref, p = at_plane(velocity, stress, mats, f)
+        for z in range(NZ):
+            ref[p + z, 8:16, :] = below[f * NZ + z]
+            ref[p + z, 48:56, :] = above[f * NZ + z]
     for group in range(GROUPS):
         tails, heads = [], []
-        for f, field in enumerate(planes):
+        for f in range(FIELDS):
+            ref, p = at_plane(velocity, stress, mats, f)
             tail = jnp.zeros((8, 128), F32)
             head = jnp.zeros((8, 128), F32)
             for z in range(NZ):
-                if group == 0:
-                    plane = below[f * NZ + z]
-                elif group == GROUPS - 1:
-                    plane = above[f * NZ + z]
+                if group in (0, GROUPS - 1):
+                    plane = (above if group else below)[f * NZ + z]
                 else:
-                    plane = field[z, 8 * group - 8 : 8 * group, :]
+                    plane = ref[p + z, PAD + 8 * group : PAD + 8 * group + 8, :]
                 tail = jnp.where(lane // 8 == 2 * z, roll(plane, 16 * z - 120), tail)
                 head = jnp.where(lane // 8 == 2 * z + 1, roll(plane, 16 * z + 8), head)
             tails.append(tail)
@@ -172,69 +187,49 @@
 
 
 def step_kernel(
-    where_ref,
-    state,
-    lame,
-    shear,
-    buoyancy,
+    v_in,
+    s_in,
+    mats,
     own_right,
     own_left,
     from_left,
     from_right,
-    from_below,
-    from_above,
     forward_dilation,
     forward_shear,
     sources,
     tile_map,
+    main_v,
+    main_s,
     out,
     send,
-    main_v,
-    main_s,
     strip_v,
     strip_s,
-    mats,
     mat_strips,
     fd,
     fs,
-    edges,
     plane_src,
     kern,
     sems,
 ):
-    top = PAD + HALO + CY
-    wave_planes = WAVES * NZ
-    copies = []
-
-    def copy(src, dst):
-        made = pltpu.make_async_copy(src, dst, sems.at[len(copies)])
+    del v_in, s_in
+    forward_copies = [
+        pltpu.make_async_copy(forward_dilation, fd, sems.at[0]),
+        pltpu.make_async_copy(forward_shear, fs, sems.at[1]),
+    ]
+    for made in forward_copies:
         made.start()
-        copies.append(made)
-
-    for i, ref in enumerate((own_right, own_left, from_left, from_right)):
-        copy(ref, edges.at[i])
-    for f in range(WAVES):
-        ref, p = (main_v, f * NZ) if f < 3 else (main_s, (f - 3) * NZ)
-        copy(state.at[f], ref.at[pl.ds(p, NZ), pl.ds(PAD + HALO, CY), :])
-    for m, ref in enumerate((lame, shear, buoyancy)):
-        copy(ref, mats.at[pl.ds(m * NZ, NZ), pl.ds(HALO, CY), :])
-    for ref, at in ((from_below, PAD), (from_above, top)):
-        copy(ref.at[pl.ds(0, 3 * NZ)], main_v.at[:, pl.ds(at, 8), :])
-        copy(ref.at[pl.ds(3 * NZ, 6 * NZ)], main_s.at[:, pl.ds(at, 8), :])
-        copy(ref.at[pl.ds(wave_planes, 3 * NZ)], mats.at[:, pl.ds(at - PAD, 8), :])
-    copy(forward_dilation, fd)
-    copy(forward_shear, fs)
-
+    edges = (own_right, own_left, from_left, from_right)
     zero = jnp.zeros((8, 128), F32)
-    for ref in (main_v, main_s, strip_v, strip_s):
+    for ref in (strip_v, strip_s):
         for p in range(ref.shape[0]):
             ref[p, 0:8, :] = zero
-            ref[p, top + 8 : top + 16, :] = zero
+            ref[p, 56:64, :] = zero
     for p in range(2 * NZ):
         for g in range(CY // 8):
             kern[pl.ds(p * CY + 8 * g, 8), :] = zero
 
-    me, tile_x, tile_y = where_ref[0], where_ref[1], where_ref[2]
+    tile_x, tile_y = lax.axis_index("gx"), lax.axis_index("gy")
+    me = tile_x * N_GY + tile_y
     lane = lanes_of((8, 128))
     row = rows_of((8, 128))
 
@@ -258,12 +253,10 @@
     high, middle, low = high.astype(F32), middle.astype(F32), low.astype(F32)
     values = jnp.concatenate([jnp.where(lane24 < 64, high, roll(middle, 64)), low], 1)
 
-    for made in copies[:4]:
-        made.wait()
     row16 = rows_of((16, 128))
     cells = jnp.zeros((16, 128), F32)
     for d, (dx, dy) in enumerate(AROUND + [(0, 0)]):
-        line = edges[(0, 3, 2)[dx], EDGES][dy + 1 : dy + 2]
+        line = edges[(0, 3, 2)[dx]][EDGES][dy + 1 : dy + 2]
         cells = jnp.where(row16 == d, line, cells)
     turned = jnp.transpose(jnp.concatenate([cells, jnp.zeros((112, 128), F32)], 0))
     lane1 = lanes_of((1, 128))
@@ -290,7 +283,7 @@
     low = lane // 8 % 2 == 0
     for pair in range(FIELDS // 2):
         for g in range(GROUPS):
-            sr, sl, rl, rr = (edges[i, pair * GROUPS + g] for i in range(4))
+            sr, sl, rl, rr = (ref[pair * GROUPS + g] for ref in edges)
             made = (
                 jnp.where(low, rl, sl),
                 jnp.where(low, sr, rr),
@@ -305,9 +298,6 @@
                     strip_s[at - 6, PAD + 8 * g : PAD + 8 * g + 8, :] = made[i]
                 else:
                     mat_strips[at - 2 * WAVES, 8 * g : 8 * g + 8, :] = made[i]
-    for made in copies[4:]:
-        made.wait()
-
     last = lane == 127
     first = lane == 0
 
@@ -341,7 +331,7 @@
             ay = (xy - prev_x(xy, edges[SXY, 0], z)) + (mload(SYY, z, r + 1) - yy) + (yz - below_yz)
             az = (xz - prev_x(xz, edges[SXZ, 0], z)) + (yz - mload(SYZ, z, r - 1)) + (above_zz - zz)
             below_xz, below_yz, zz = xz, yz, above_zz
-            hb = H * mats[2 * NZ + z, pl.ds(r - PAD, 8), :]
+            hb = H * mats[2 * NZ + z, pl.ds(r, 8), :]
             for c, a in enumerate((ax, ay, az)):
                 if z == 0:
                     at = pl.multiple_of((c * STEPS + step) * ROWS + 8 * g, 8)
@@ -359,7 +349,7 @@
                 src = jnp.where(lane < 16, roll(src, 64) if side else src, 0.0)
                 strip_v[2 * c + side, pl.ds(r, 8), :] = sload(c, side, r) + hb * (a + src)
 
-    def stress_group(g, forward):
+    def stress_group(g, forward, strips):
         r = PAD + 8 * g
         edges = {(f, s): sload(f, s, r) for f in range(3) for s in range(2)}
         vx, vy = mload(VX, 0, r), mload(VY, 0, r)
@@ -376,8 +366,8 @@
             exz = (above_vx - vx) + (next_x(vz, edges[VZ, 1], z) - vz)
             eyz = (above_vy - vy) + (mload(VZ, z, r + 1) - vz)
             vx, vy, below_vz = above_vx, above_vy, vz
-            pressure = H * mats[z, pl.ds(r - PAD, 8), :] * dilation
-            hm = H * mats[NZ + z, pl.ds(r - PAD, 8), :]
+            pressure = H * mats[z, pl.ds(r, 8), :] * dilation
+            hm = H * mats[NZ + z, pl.ds(r, 8), :]
             hm2 = hm + hm
             for f, change in (
                 (SXX, pressure + hm2 * exx),
@@ -392,7 +382,7 @@
                 for k, strain in ((0, dilation), (1, exy)):
                     at = pl.ds((k * NZ + z) * CY + 8 * (g - 1), 8)
                     kern[at, :] = kern[at, :] + forward[k][z] * (H * strain)
-        for side in range(2):
+        for side in range(2 if strips else 0):
             vx, vy, vz = (edges[f, side] for f in range(3))
             exx = vx - roll(vx, 1)
             eyy = vy - sload(VY, side, r - 1)
@@ -413,10 +403,9 @@
             ):
                 strip_s[2 * f - 6 + side, pl.ds(r, 8), :] = sload(f, side, r) + change
 
-    def one_step(step, carry):
-        for g in range(GROUPS):
-            velocity_group(step, g)
-        stress_group(0, None)
+    def stresses(step, halos):
+        if halos:
+            stress_group(0, None, True)
         for i in range(CY // 16):
             both = [
                 [ref[step, z, 16 * i : 16 * i + 16, :].astype(F32) for z in range(NZ)]
@@ -424,20 +413,36 @@
             ]
             for half in range(2):
                 part = [[v[8 * half : 8 * half + 8] for v in vs] for vs in both]
-                stress_group(1 + 2 * i + half, part)
-        stress_group(GROUPS - 1, None)
+                stress_group(1 + 2 * i + half, part, halos)
+        if halos:
+            stress_group(GROUPS - 1, None, True)
+
+    def one_step(step, carry):
+        for g in range(GROUPS):
+            velocity_group(step, g)
+        stresses(step, True)
         return carry
 
-    lax.fori_loop(0, STEPS, one_step, 0)
-
+    for made in forward_copies:
+        made.wait()
+    lax.fori_loop(0, STEPS - 1, one_step, 0)
+    for g in range(GROUPS):
+        velocity_group(STEPS - 1, g)
     outs = []
-    for f in range(WAVES):
-        ref, p = (main_v, f * NZ) if f < 3 else (main_s, (f - 3) * NZ)
+
+    def deliver(f):
+        ref, p = at_plane(main_v, main_s, None, f)
         made = pltpu.make_async_copy(
-            ref.at[pl.ds(p, NZ), pl.ds(PAD + HALO, CY), :], out.at[f], sems.at[f]
+            ref.at[pl.ds(p, NZ), pl.ds(PAD + HALO, CY), :], out.at[f], sems.at[2 + f]
         )
         made.start()
         outs.append(made)
+
+    for f in range(3):
+        deliver(f)
+    stresses(STEPS - 1, False)
+    for f in range(3, WAVES):
+        deliver(f)
 
     slot = tile_map[...] // 256 * 2 + (tile_map[...] % 256 - 2 * me)
     slot = slot.astype(F32)
@@ -499,19 +504,31 @@
     receiver_cells,
     tile_map,
 ):
-    tile_x = lax.axis_index("gx")
-    tile_y = lax.axis_index("gy")
-    here = jnp.stack([tile_x * N_GY + tile_y, tile_x, tile_y]).astype(jnp.int32)
     rows_dev = residual.shape[0]
-
-    up, down = pl.pallas_call(
+    in_hbm = lambda value: pltpu.with_memory_space_constraint(value, pltpu.HBM)
+    adjoint_state, lame_lambda, shear_modulus, buoyancy, forward_dilation, forward_shear = (
+        in_hbm(value)
+        for value in (
+            adjoint_state,
+            lame_lambda,
+            shear_modulus,
+            buoyancy,
+            forward_dilation,
+            forward_shear,
+        )
+    )
+
+    reach = ROWS + 2 * PAD
+    held = (shape(3 * NZ, reach, 128), shape(6 * NZ, reach, 128), shape(3 * NZ, reach, 128))
+    velocity, stress, mats, up, down = pl.pallas_call(
         rows_kernel,
-        out_shape=(shape(PLANES + 1, 8, 128), shape(PLANES + 1, 8, 128)),
+        out_shape=held + (shape(PLANES + 1, 8, 128), shape(PLANES + 1, 8, 128)),
         in_specs=[ANY] * 4 + [SMEM],
-        out_specs=(VMEM, VMEM),
-        scratch_shapes=[pltpu.SemaphoreType.DMA((24,))],
+        out_specs=(VMEM,) * 5,
+        scratch_shapes=[pltpu.SemaphoreType.DMA((FIELDS,))],
+        compiler_params=PART,
         cost_estimate=cost(0, 1 << 21),
-    )(adjoint_state, lame_lambda, shear_modulus, buoyancy, receiver_cells.reshape(1, 4))
+    )(adjoint_state, lame_lambda, shear_modulus, buoyancy, in_hbm(receiver_cells.reshape(1, 4)))
     from_below = shift(up, 0, 1)
     from_above = shift(down, 0, -1)
 
@@ -525,61 +542,55 @@
             pltpu.VMEM((176, 128), F32),
             pltpu.SemaphoreType.DMA((3,)),
         ],
-        compiler_params=FULL,
+        compiler_params=PART,
         cost_estimate=cost(1 << 30, 1 << 22),
     )(
-        jnp.transpose(residual, (1, 0, 2)),
-        sample_counts.reshape(1, rows_dev),
-        station_list.reshape(1, rows_dev),
+        in_hbm(jnp.transpose(residual, (1, 0, 2))),
+        in_hbm(sample_counts.reshape(1, rows_dev)),
+        in_hbm(station_list.reshape(1, rows_dev)),
         jnp.asarray(resample_table()),
     )
+    send = in_hbm(send)
     sources = lax.all_to_all(send, ("gx", "gy"), 0, 0, tiled=True)
 
-    right, left = pl.pallas_call(
+    velocity, stress, mats, right, left = pl.pallas_call(
         edges_kernel,
-        out_shape=(shape(EDGES + 1, 8, 128), shape(EDGES + 1, 8, 128)),
-        in_specs=[VMEM] * 7,
-        out_specs=(VMEM, VMEM),
+        out_shape=held + (shape(EDGES + 1, 8, 128), shape(EDGES + 1, 8, 128)),
+        in_specs=[VMEM] * 6,
+        out_specs=(VMEM,) * 5,
+        input_output_aliases={0: 0, 1: 1, 2: 2},
+        compiler_params=PART,
         cost_estimate=cost(1 << 20, 1 << 21),
-    )(adjoint_state, lame_lambda, shear_modulus, buoyancy, from_below, from_above, up)
+    )(velocity, stress, mats, from_below, from_above, up)
     from_left = shift(right, 1, 0)
     from_right = shift(left, -1, 0)
 
-    wave_planes = WAVES * NZ
-    reach = ROWS + 2 * PAD
-    adjoint_out, send = pl.pallas_call(
+    _, _, adjoint_out, send = pl.pallas_call(
         step_kernel,
-        out_shape=(shape(WAVES, NZ, CY, CX), shape(256, 128)),
-        in_specs=[SMEM] + [ANY] * 12 + [VMEM, VMEM],
-        out_specs=(ANY, VMEM),
+        out_shape=held[:2] + (shape(WAVES, NZ, CY, CX), shape(256, 128)),
+        in_specs=[VMEM] * 7 + [ANY] * 2 + [VMEM, VMEM],
+        out_specs=(VMEM, VMEM, ANY, VMEM),
+        input_output_aliases={0: 0, 1: 1},
         scratch_shapes=[
-            pltpu.VMEM((3 * NZ, reach, 128), F32),
-            pltpu.VMEM((6 * NZ, reach, 128), F32),
             pltpu.VMEM((6, reach, 128), F32),
             pltpu.VMEM((12, reach, 128), F32),
-            pltpu.VMEM((3 * NZ, ROWS, 128), F32),
             pltpu.VMEM((6, ROWS, 128), F32),
             pltpu.VMEM((STEPS, NZ, CY, CX), BF16),
             pltpu.VMEM((STEPS, NZ, CY, CX), BF16),
-            pltpu.VMEM((4, EDGES + 1, 8, 128), F32),
             pltpu.VMEM((24 * ROWS, 256), F32),
             pltpu.VMEM((2 * NZ * CY, 128), F32),
-            pltpu.SemaphoreType.DMA((32,)),
+            pltpu.SemaphoreType.DMA((2 + WAVES,)),
         ],
-        compiler_params=FULL,
+        compiler_params=PART,
         cost_estimate=cost(1 << 27, 1 << 23),
     )(
-        here,
-        adjoint_state,
-        lame_lambda,
-        shear_modulus,
-        buoyancy,
+        velocity,
+        stress,
+        mats,
         right,
         left,
         from_left,
         from_right,
-        from_below,
-        from_above,
         forward_dilation,
         forward_shear,
         sources,

time: 78.6 us -> 72.8 us (0.926)
  Pallas kernels: 26.5 us -> 22.9 us
  waiting for transfers between devices: 4.12 us -> 5.37 us
  starting transfers between devices: 25 us -> 23.8 us
  blocking collectives: 19.7 us -> 18.9 us
    pallas_call x3, Pallas kernels: 20.3 us -> 18 us  [the longest x1 12 us: local(): pl.pallas_call(step_kernel, out_shape=held[:2] + (shape(WAVES, NZ, CY, CX...]
    all_to_all x1, waiting for transfers between devices: 3.3 us -> 5.36 us  [local(): sources = lax.all_to_all(send, ('gx', 'gy'), 0, 0, tiled=True)]
    pallas_call x1, Pallas kernels: 4.66 us -> 3.29 us  [local(): pl.pallas_call(source_kernel, out_shape=shape(OWNERS * 8, 128), in_specs=...]
    ppermute x4, waiting for transfers between devices: 0.82 us -> 0.01 us  [shift(): return lax.ppermute(value, ('gx', 'gy'), pairs)]
    all_to_all x1, blocking collectives: 19.7 us -> 18.9 us  [local(): got = lax.all_to_all(send, ('gx', 'gy'), 0, 0, tiled=True)]
  transfers between devices with their start and end apart: 5 -> 5, of which waited for: 2 -> 1; matrix products, arithmetic and copies ran while one was open for 1% -> 0% of each run, Pallas kernels for 11% -> 9%
where the time goes in v2:
time: 72.8 us; the launch traced here: 72.4 us
  starting transfers between devices  23.8 us (33%)
  Pallas kernels  22.9 us (31%)
  blocking collectives  18.9 us (26%)
  waiting for transfers between devices  5.37 us (7%)
  local copies, waits for them, and re-layouts  0.8 us (1%)
  between operations  0.74 us (1%)
    all_to_all x1, blocking collectives, local(): got = lax.all_to_all(send, ('gx', 'gy'), 0, 0, tiled=True)  18.9 us
    all_to_all x1, starting transfers between devices, local(): sources = lax.all_to_all(send, ('gx', 'gy'), 0, 0, tiled=True)  12.3 us
    pallas_call x1, Pallas kernels, local(): pl.pallas_call(step_kernel, out_shape=held[:2] + (shape(WAVES, NZ, CY, CX...  12 us
    ppermute x4, starting transfers between devices, shift(): return lax.ppermute(value, ('gx', 'gy'), pairs)  11.4 us
    all_to_all x1, waiting for transfers between devices, local(): sources = lax.all_to_all(send, ('gx', 'gy'), 0, 0, tiled=True)  5.36 us
    pallas_call x1, Pallas kernels, local(): pl.pallas_call(source_kernel, out_shape=shape(OWNERS * 8, 128), in_specs=...  3.29 us
    pallas_call x1, Pallas kernels, local(): pl.pallas_call(rows_kernel, out_shape=held + (shape(PLANES + 1, 8, 128),...  3.09 us
    pallas_call x1, Pallas kernels, local(): pl.pallas_call(edges_kernel, out_shape=held + (shape(EDGES + 1, 8, 128),...  2.91 us
  transfers between devices with their start and end apart: 5, of which 1 were waited for; matrix products, arithmetic and copies ran while one was open for 0% of the time, Pallas kernels for 9%

profile of v2, /device:TPU:1, one launch (start us, length us, event | category | flops | bytes accessed | tf_op | source)
XLA Modules:
  0.0 72.4 jit_solution(5111917186987047458)
XLA Ops:
  0.6 0.0 copy-start.2
  0.6 3.1 %shard_map.131 = (f32[24,64,128]{2,1,0:T(8,128)S(1)}, f32[48,64,128]{2,1,0:T(8,128)S(1)}, f32[24,64,128]{2,1,0:T(8,128)S(1)}, f32[97,8,128]{2,1,0:T(8,128)S(1)}, f32[97,8,128]{2,1,0:T(8,128)}) custom-call(f32[9,8,32,128]{3,2,1,0:T(8,128)} %state.1, f32[8,32,128]{2,1,0:T(8,128)} %lame.1, f32[8,32,128]{2,1,0:T(8,128)} %shear.1, f32[8,32,128]{2,1,0:T(8,128)} %buoyancy.1, ...), custom_call_target="tpu_custom_call" | custom-call | bytes 2097152 | tf_op jit(solution)/shard_map/pallas_call | solution.py:523
  3.7 4.7 %collective-permute-start = (f32[97,8,128]{2,1,0:T(8,128)S(1)}, f32[97,8,128]{2,1,0:T(8,128)}, u32[]{:S(2)}, u32[]{:S(2)}) collective-permute-start(f32[97,8,128]{2,1,0:T(8,128)S(1)} %get-tuple-element.17.own), channel_id=1, source_target_pairs={{0,1},{1,2},{2,3},{3,4},{4,5},{5,6},{6,7},{7,8},{8,9},{9,10},{10,1... | collective-permute-start | bytes 1191944 | tf_op jit(solution)/shard_map/ppermute | solution.py:483
  8.4 1.3 %collective-permute-start.1 = (f32[97,8,128]{2,1,0:T(8,128)}, f32[97,8,128]{2,1,0:T(8,128)}, u32[]{:S(2)}, u32[]{:S(2)}) collective-permute-start(f32[97,8,128]{2,1,0:T(8,128)} %get-tuple-element.18), channel_id=1, source_target_pairs={{1,0},{2,1},{3,2},{4,3},{5,4},{6,5},{7,6},{8,7},{9,8},{10,9},{11,1... | collective-permute-start | bytes 1191944 | tf_op jit(solution)/shard_map/ppermute | solution.py:483
  9.7 0.0 copy-done.2
  9.7 3.3 %shard_map.133 = f32[1024,128]{1,0:T(8,128)S(1)} custom-call(bf16[3,96,4096]{2,1,0:T(8,128)(2,1)} %bitcast.16, s32[1,96]{1,0:T(1,128)} %bitcast.17, s32[1,96]{1,0:T(1,128)} %bitcast.18, bf16[4096,128]{1,0:T(8,128)(2,1)S(1)} %copy-done.2), custom_call_target="tpu_custom_call" | custom-call | flops 1073741824 | bytes 4194304 | tf_op jit(solution)/shard_map/pallas_call | solution.py:535
  13.0 0.0 copy-start
  13.0 0.8 %copy-done = f32[1024,128]{1,0:T(8,128)} copy-done((f32[1024,128]{1,0:T(8,128)}, f32[1024,128]{1,0:T(8,128)S(1)}, u32[]{:S(2)}) %copy-start) | copy-done | bytes 524312
  13.8 12.3 %all-to-all-start = ((f32[128,8,128]{2,1,0:T(8,128)}), f32[128,8,128]{2,1,0:T(8,128)}, u32[]{:S(2)}, u32[]{:S(2)}) async-start(f32[128,8,128]{2,1,0:T(8,128)} %bitcast.10), calls=%async_computation | async-start | bytes 1048576 | tf_op jit(solution)/shard_map/all_to_all | solution.py:554
  26.2 0.0 collective-permute-done.below
  26.2 0.0 collective-permute-done.1.above
  26.2 0.0 copy-start.1
  26.2 2.9 %shard_map.132 = (f32[24,64,128]{2,1,0:T(8,128)S(1)}, f32[48,64,128]{2,1,0:T(8,128)S(1)}, f32[24,64,128]{2,1,0:T(8,128)S(1)}, f32[37,8,128]{2,1,0:T(8,128)}, f32[37,8,128]{2,1,0:T(8,128)}) custom-call(f32[24,64,128]{2,1,0:T(8,128)S(1)} %get-tuple-element.14.v_in, ...), custom_call_target="tpu_custom_call", output_to_operand_aliasing={{0}: (0, {}), {1}: (1, {}), {2}: (2, {})} | custom-call | flops 1048576 | bytes 2097152 | tf_op jit(solution)/shard_map/pallas_call | solution.py:556
  29.1 3.5 %collective-permute-start.2 = (f32[37,8,128]{2,1,0:T(8,128)}, f32[37,8,128]{2,1,0:T(8,128)S(1)}, u32[]{:S(2)}, u32[]{:S(2)}) collective-permute-start(f32[37,8,128]{2,1,0:T(8,128)} %get-tuple-element.22.own_right), channel_id=1, source_target_pairs={{0,16},{1,17},{2,18},{3,19},{4,20},{5,21},{6,22},{7,23},{8,24},{9,... | collective-permute-start | bytes 454664 | tf_op jit(solution)/shard_map/ppermute | solution.py:483
  32.6 1.9 %collective-permute-start.3 = (f32[37,8,128]{2,1,0:T(8,128)}, f32[37,8,128]{2,1,0:T(8,128)S(1)}, u32[]{:S(2)}, u32[]{:S(2)}) collective-permute-start(f32[37,8,128]{2,1,0:T(8,128)} %get-tuple-element.23.own_left), channel_id=1, source_target_pairs={{16,0},{17,1},{18,2},{19,3},{20,4},{21,5},{22,6},{23,7},{24,8},{25... | collective-permute-start | bytes 454664 | tf_op jit(solution)/shard_map/ppermute | solution.py:483
  34.6 5.4 %all-to-all-done = f32[128,8,128]{2,1,0:T(8,128)} async-done(((f32[128,8,128]{2,1,0:T(8,128)}), f32[128,8,128]{2,1,0:T(8,128)}, u32[]{:S(2)}, u32[]{:S(2)}) %all-to-all-start) | async-done | bytes 524320 | tf_op jit(solution)/shard_map/all_to_all | solution.py:554
  39.9 0.0 collective-permute-done.2.from_left
  39.9 0.0 collective-permute-done.3.from_right
  39.9 0.0 copy-done.1
  39.9 12.0 %shard_map.134 = (f32[24,64,128]{2,1,0:T(8,128)S(1)}, f32[48,64,128]{2,1,0:T(8,128)S(1)}, f32[9,8,32,128]{3,2,1,0:T(8,128)}, f32[256,128]{1,0:T(8,128)S(1)}) custom-call(f32[24,64,128]{2,1,0:T(8,128)S(1)} %get-tuple-element.19.v_in, f32[48,64,128]{2,1,0:T(8,128)S(1)} %get-tuple-element.20.s_in, ...), custom_call_target="tpu_custom_call", output_to_operand_aliasing={{0}: (0, {}), {1}: (1, {})} | custom-call | flops 134217728 | bytes 8388608 | tf_op jit(solution)/shard_map/pallas_call | solution.py:568
  51.9 18.9 %all_to_all.22 = f32[128,2,128]{2,1,0:T(2,128)} all-to-all(f32[128,2,128]{2,1,0:T(2,128)S(1)} %bitcast.11), channel_id=1, replica_groups=mesh['gx'=8,'gy'=16] {'gx','gy'}, dimensions={0} | all-to-all | bytes 262144 | tf_op jit(solution)/shard_map/all_to_all | solution.py:599
  70.8 1.6 %shard_map.135 = f32[16,256]{1,0:T(8,128)} custom-call(f32[256,128]{1,0:T(8,128)} %bitcast.13), custom_call_target="tpu_custom_call" | custom-call | tf_op jit(solution)/shard_map/pallas_call | solution.py:600
Async XLA Ops:
  0.6 9.1 %copy-start.2 = (bf16[4096,128]{1,0:T(8,128)(2,1)S(1)}, bf16[4096,128]{1,0:T(8,128)(2,1)}, u32[]{:S(2)}) copy-start(bf16[4096,128]{1,0:T(8,128)(2,1)} %constant.2.clone.table) | copy-start | bytes 3145732
  3.7 22.4 %collective-permute-start = (f32[97,8,128]{2,1,0:T(8,128)S(1)}, f32[97,8,128]{2,1,0:T(8,128)}, u32[]{:S(2)}, u32[]{:S(2)}) collective-permute-start(f32[97,8,128]{2,1,0:T(8,128)S(1)} %get-tuple-element.17.own), channel_id=1, source_target_pairs={{0,1},{1,2},{2,3},{3,4},{4,5},{5,6},{6,7},{7,8},{8,9},{9,10},{10,1... | collective-permute-start | bytes 1191944 | tf_op jit(solution)/shard_map/ppermute | solution.py:483
  8.4 17.7 %collective-permute-start.1 = (f32[97,8,128]{2,1,0:T(8,128)}, f32[97,8,128]{2,1,0:T(8,128)}, u32[]{:S(2)}, u32[]{:S(2)}) collective-permute-start(f32[97,8,128]{2,1,0:T(8,128)} %get-tuple-element.18), channel_id=1, source_target_pairs={{1,0},{2,1},{3,2},{4,3},{5,4},{6,5},{7,6},{8,7},{9,8},{10,9},{11,1... | collective-permute-start | bytes 1191944 | tf_op jit(solution)/shard_map/ppermute | solution.py:483
  13.0 0.8 %copy-start = (f32[1024,128]{1,0:T(8,128)}, f32[1024,128]{1,0:T(8,128)S(1)}, u32[]{:S(2)}) copy-start(f32[1024,128]{1,0:T(8,128)S(1)} %shard_map.133) | copy-start | bytes 1572868
  13.8 26.1 %all-to-all-start = ((f32[128,8,128]{2,1,0:T(8,128)}), f32[128,8,128]{2,1,0:T(8,128)}, u32[]{:S(2)}, u32[]{:S(2)}) async-start(f32[128,8,128]{2,1,0:T(8,128)} %bitcast.10), calls=%async_computation | async-start | bytes 1048576 | tf_op jit(solution)/shard_map/all_to_all | solution.py:554
  26.2 13.8 %copy-start.1 = (s32[256]{0:T(256)S(1)}, s32[256]{0:T(256)}, u32[]{:S(2)}) copy-start(s32[256]{0:T(256)} %param.22) | copy-start | bytes 3076
  29.1 10.8 %collective-permute-start.2 = (f32[37,8,128]{2,1,0:T(8,128)}, f32[37,8,128]{2,1,0:T(8,128)S(1)}, u32[]{:S(2)}, u32[]{:S(2)}) collective-permute-start(f32[37,8,128]{2,1,0:T(8,128)} %get-tuple-element.22.own_right), channel_id=1, source_target_pairs={{0,16},{1,17},{2,18},{3,19},{4,20},{5,21},{6,22},{7,23},{8,24},{9,... | collective-permute-start | bytes 454664 | tf_op jit(solution)/shard_map/ppermute | solution.py:483
  32.6 7.3 %collective-permute-start.3 = (f32[37,8,128]{2,1,0:T(8,128)}, f32[37,8,128]{2,1,0:T(8,128)S(1)}, u32[]{:S(2)}, u32[]{:S(2)}) collective-permute-start(f32[37,8,128]{2,1,0:T(8,128)} %get-tuple-element.23.own_left), channel_id=1, source_target_pairs={{16,0},{17,1},{18,2},{19,3},{20,4},{21,5},{22,6},{23,7},{24,8},{25... | collective-permute-start | bytes 454664 | tf_op jit(solution)/shard_map/ppermute | solution.py:483

commit v3 on v2

v3 whole, which is shorter than its diff:
```python
import math

import jax
import jax.numpy as jnp
import numpy as np
from jax import lax
from jax.experimental import pallas as pl
from jax.experimental.pallas import tpu as pltpu
from jax.sharding import PartitionSpec as P

F32 = jnp.float32
BF16 = jnp.bfloat16

NZ, CY, CX = 8, 32, 128
STEPS = 8
SAMPLES = 4096
H = 0.25
N_GX, N_GY = 8, 16
OWNERS = N_GX * N_GY
NX = N_GX * CX
HALO = 8
ROWS = CY + 2 * HALO
GROUPS = ROWS // 8
FIELDS = 12
WAVES = 9
PLANES = FIELDS * NZ
EDGES = FIELDS // 2 * GROUPS

AROUND = [(dx, dy) for dx in (-1, 0, 1) for dy in (-1, 0, 1) if (dx, dy) != (0, 0)]

VX, VY, VZ, SXX, SYY, SZZ, SXY, SXZ, SYZ = range(WAVES)

VMEM = pl.BlockSpec(memory_space=pltpu.VMEM)
SMEM = pl.BlockSpec(memory_space=pltpu.SMEM)
ANY = pl.BlockSpec(memory_space=pltpu.HBM)


PART = pltpu.CompilerParams(vmem_limit_bytes=24 << 20)


def lanes_of(shape):
    return lax.broadcasted_iota(jnp.int32, shape, len(shape) - 1)


def rows_of(shape):
    return lax.broadcasted_iota(jnp.int32, shape, len(shape) - 2)


def roll(value, shift):
    return pltpu.roll(value, shift % value.shape[-1], value.ndim - 1)


def three_parts(value):
    high = value.astype(BF16)
    rest = value - high.astype(F32)
    middle = rest.astype(BF16)
    low = (rest - middle.astype(F32)).astype(BF16)
    return high, middle, low


def resample_table():
    per_step = SAMPLES // STEPS
    position = np.arange(SAMPLES, dtype=np.float32) + np.float32(0.5)
    centers = (np.arange(STEPS, dtype=np.float32) + np.float32(0.5)) * np.float32(per_step)
    distance = np.abs(position[:, None] - centers[None, :]) / np.float32(per_step)
    weight = np.maximum(np.float32(0.0), np.float32(1.0) - distance)
    table = (weight / np.float32(math.sqrt(per_step))).astype(BF16)
    wide = np.zeros((SAMPLES, 128), BF16)
    wide[:, :96] = np.tile(table, (1, 12))
    return wide


def at_plane(velocity, stress, mats, f):
    if f < 3:
        return velocity, f * NZ
    if f < WAVES:
        return stress, (f - 3) * NZ
    return mats, (f - WAVES) * NZ


def first_kernel(
    state,
    lame,
    shear,
    buoyancy,
    cells,
    residual,
    counts,
    stations,
    weights,
    velocity,
    stress,
    mats,
    up,
    down,
    by_owner,
    table,
    held,
    sems,
):
    copies = []
    for f in range(FIELDS):
        to, p = at_plane(velocity, stress, mats, f)
        source = state.at[f] if f < WAVES else (lame, shear, buoyancy)[f - WAVES]
        to = to.at[pl.ds(p, NZ), pl.ds(HALO, CY), :]
        copies.append(pltpu.make_async_copy(source, to, sems.at[f]))
        copies[f].start()
    table_copy = pltpu.make_async_copy(weights, table, sems.at[FIELDS])
    table_copy.start()
    rows_in = [
        pltpu.make_async_copy(residual.at[c], held.at[c], sems.at[FIELDS + 1 + c]) for c in range(3)
    ]
    for copy in rows_in:
        copy.start()
    lane = lanes_of((8, 128))
    mine = jnp.zeros((8, 128), jnp.int32)
    for k in range(4):
        mine = jnp.where(lane == k, cells[0, k], mine)
    up[PLANES] = mine.astype(F32)
    down[PLANES] = mine.astype(F32)
    rows = held.shape[1]
    pad = jnp.zeros((1, 128 - rows), F32)
    count = column_of(jnp.concatenate([counts[...].astype(F32), pad], 1))[:rows]
    station_row = jnp.concatenate([stations[...], jnp.full((1, 128 - rows), -1, jnp.int32)], 1)
    station = column_of(station_row.astype(F32))[:rows].astype(jnp.int32)
    for f in range(FIELDS):
        copies[f].wait()
        ref, p = at_plane(velocity, stress, mats, f)
        for z in range(NZ):
            down[f * NZ + z] = ref[p + z, 8:16, :]
            up[f * NZ + z] = ref[p + z, 32:40, :]
    table_copy.wait()
    by_owner[...] = sums_by_owner(rows_in, held, table, count, station, station_row)


def edges_kernel(v_in, s_in, m_in, below, above, own, velocity, stress, mats, right, left):
    del v_in, s_in, m_in
    lane = lanes_of((8, 128))
    for f in range(FIELDS):
        ref, p = at_plane(velocity, stress, mats, f)
        for z in range(NZ):
            if f < WAVES:
                ref[p + z, 0:8, :] = below[f * NZ + z]
                ref[p + z, 40:48, :] = above[f * NZ + z]
            else:
                ref[p + z, 0:8, :] = H * below[f * NZ + z]
                ref[p + z, 8:40, :] = H * ref[p + z, 8:40, :]
                ref[p + z, 40:48, :] = H * above[f * NZ + z]
    for group in range(GROUPS):
        tails, heads = [], []
        for f in range(FIELDS):
            ref, p = at_plane(velocity, stress, mats, f)
            tail = jnp.zeros((8, 128), F32)
            head = jnp.zeros((8, 128), F32)
            for z in range(NZ):
                plane = ref[p + z, 8 * group : 8 * group + 8, :]
                tail = jnp.where(lane // 8 == 2 * z, roll(plane, 16 * z - 120), tail)
                head = jnp.where(lane // 8 == 2 * z + 1, roll(plane, 16 * z + 8), head)
            tails.append(tail)
            heads.append(head)
        for pair in range(FIELDS // 2):
            right[pair * GROUPS + group] = tails[2 * pair] + roll(tails[2 * pair + 1], 8)
            left[pair * GROUPS + group] = heads[2 * pair] + roll(heads[2 * pair + 1], -8)
    row = rows_of((8, 128))
    cells = jnp.where(row == 0, below[PLANES], jnp.where(row == 1, own[PLANES], above[PLANES]))
    right[EDGES] = cells
    left[EDGES] = cells


def column_of(row_vector):
    return jnp.transpose(jnp.broadcast_to(row_vector, (128, 128)))


def sums_by_owner(rows_in, held, table, count, station, station_row):
    rows = held.shape[1]
    lane = lanes_of((rows, 128))
    total = jnp.zeros((rows, 128), F32)
    live = jnp.concatenate(
        [
            jnp.where((lane + 128 * g).astype(F32) < count, 1.0, 0.0).astype(BF16)
            for g in range(SAMPLES // 128)
        ],
        1,
    )
    for c in range(3):
        rows_in[c].wait()
        product = jnp.dot(held[c] * live, table[...], preferred_element_type=F32)
        total = jnp.where(lane // 8 % 3 == c, product, total)
    mine = jnp.where(lane // 24 == station % 4, total, 0.0)
    mine = jnp.concatenate([mine, jnp.zeros((128 - rows, 128), F32)], 0)
    names = jnp.where(rows_of((128, 128)) == station_row // 4, 1.0, 0.0)
    return jnp.dot(names, mine, preferred_element_type=F32, precision=lax.Precision.HIGHEST)


def send_kernel(by_owner, send, made_send, totals, sems):
    totals[0:24, :] = jnp.zeros((24, 128), F32)
    totals[152:176, :] = jnp.zeros((24, 128), F32)
    totals[24:152, :] = by_owner[...]
    lane = lanes_of((32, 128))
    tile_y = rows_of((32, 128)) % N_GY
    copies = []
    for i in range(OWNERS // 32):
        for d, (dx, dy) in enumerate(AROUND):
            near = totals[pl.ds(24 + 32 * i + dx * N_GY + dy, 32), :]
            inside = (tile_y + dy >= 0) & (tile_y + dy < N_GY) & (lane < 96)
            near = jnp.where(inside, near, 0.0)
            if d < 3:
                near = jnp.where(lane < 96, near, roll(by_owner[32 * i : 32 * i + 32], 96 - 32 * d))
            made_send[pl.ds(256 * i + d, 32, stride=8), :] = near
        part = pl.ds(256 * i, 256)
        copies.append(pltpu.make_async_copy(made_send.at[part], send.at[part], sems.at[i]))
        copies[i].start()
    for copy in copies:
        copy.wait()


def stencil_tools(main_v, main_s, strip_v, strip_s):
    lane = lanes_of((8, 128))
    last = lane == 127
    first = lane == 0

    def load(ref, p, r):
        if r < 0:
            return pltpu.roll(ref[p, 0:8, :], 1, 0)
        if r > ROWS - 8:
            return pltpu.roll(ref[p, ROWS - 8 : ROWS, :], 7, 0)
        return ref[p, r : r + 8, :]

    def mload(f, z, r):
        return load(main_v, f * NZ + z, r) if f < 3 else load(main_s, (f - 3) * NZ + z, r)

    def sload(f, side, r):
        return load(strip_v, 2 * f + side, r) if f < 3 else load(strip_s, 2 * f - 6 + side, r)

    def next_x(value, edge, z):
        return jnp.where(last, roll(edge, 127 - (16 * z + 8)), roll(value, -1))

    def prev_x(value, edge, z):
        return jnp.where(first, roll(edge, -(16 * z + 7)), roll(value, 1))

    def next_z(value):
        return jnp.where(lane < 112, roll(value, -16), 0.0)

    def prev_z(value):
        return jnp.where(lane >= 16, roll(value, 16), 0.0)

    return mload, sload, next_x, prev_x, next_z, prev_z


def stress_planes(tools, mats, main_s, kern, g, forward, update):
    mload, sload, next_x, prev_x = tools[:4]
    zero = jnp.zeros((8, 128), F32)
    r = 8 * g
    left_vx = sload(VX, 0, r)
    right_vy, right_vz = sload(VY, 1, r), sload(VZ, 1, r)
    vx, vy = mload(VX, 0, r), mload(VY, 0, r)
    below_vz = zero
    for z in range(NZ):
        vz = mload(VZ, z, r)
        above_vx = mload(VX, z + 1, r) if z < NZ - 1 else zero
        above_vy = mload(VY, z + 1, r) if z < NZ - 1 else zero
        exx = vx - prev_x(vx, left_vx, z)
        eyy = vy - mload(VY, z, r - 1)
        ezz = vz - below_vz
        dilation = exx + eyy + ezz
        exy = (mload(VX, z, r + 1) - vx) + (next_x(vy, right_vy, z) - vy)
        if forward is not None:
            for k, strain in ((0, dilation), (1, exy)):
                at = pl.ds((k * NZ + z) * CY + 8 * (g - 1), 8)
                kern[at, :] = kern[at, :] + forward[k][z] * (H * strain)
        if update:
            exz = (above_vx - vx) + (next_x(vz, right_vz, z) - vz)
            eyz = (above_vy - vy) + (mload(VZ, z, r + 1) - vz)
            pressure = mats[z, pl.ds(r, 8), :] * dilation
            hm = mats[NZ + z, pl.ds(r, 8), :]
            hm2 = hm + hm
            for f, change in (
                (SXX, pressure + hm2 * exx),
                (SYY, pressure + hm2 * eyy),
                (SZZ, pressure + hm2 * ezz),
                (SXY, hm * exy),
                (SXZ, hm * exz),
                (SYZ, hm * eyz),
            ):
                main_s[(f - 3) * NZ + z, pl.ds(r, 8), :] = mload(f, z, r) + change
        vx, vy, below_vz = above_vx, above_vy, vz


def step_kernel(
    v_in,
    s_in,
    mats,
    own_right,
    own_left,
    from_left,
    from_right,
    forward_dilation,
    forward_shear,
    sources,
    tile_map,
    main_v,
    main_s,
    send,
    strip_out,
    strip_v,
    strip_s,
    mat_strips,
    fd,
    fs,
    plane_src,
    kern,
    got_sources,
    made_send,
    sems,
):
    del v_in, s_in
    source_copy = pltpu.make_async_copy(sources, got_sources, sems.at[2 * STEPS])
    source_copy.start()

    def forward_copies(t):
        return (
            pltpu.make_async_copy(forward_dilation.at[t], fd.at[t], sems.at[t]),
            pltpu.make_async_copy(forward_shear.at[t], fs.at[t], sems.at[STEPS + t]),
        )

    for t in range(STEPS):
        for made in forward_copies(t):
            made.start()
    edges = (own_right, own_left, from_left, from_right)
    zero = jnp.zeros((8, 128), F32)
    for p in range(2 * NZ):
        for g in range(CY // 8):
            kern[pl.ds(p * CY + 8 * g, 8), :] = zero

    tile_x, tile_y = lax.axis_index("gx"), lax.axis_index("gy")
    me = tile_x * N_GY + tile_y
    lane = lanes_of((8, 128))
    row = rows_of((8, 128))

    low = lane // 8 % 2 == 0
    for pair in range(FIELDS // 2):
        for g in range(GROUPS):
            sr, sl, rl, rr = (ref[pair * GROUPS + g] for ref in edges)
            made = (
                jnp.where(low, rl, sl),
                jnp.where(low, sr, rr),
                jnp.where(low, roll(rl, -8), roll(sl, 8)),
                jnp.where(low, roll(sr, -8), roll(rr, 8)),
            )
            for i in range(4):
                at = 4 * pair + i
                if at < 6:
                    strip_v[at, 8 * g : 8 * g + 8, :] = made[i]
                elif at < 2 * WAVES:
                    strip_s[at - 6, 8 * g : 8 * g + 8, :] = made[i]
                else:
                    mat_strips[at - 2 * WAVES, 8 * g : 8 * g + 8, :] = made[i]
    def add_sender(i, carry):
        block = got_sources[pl.ds(pl.multiple_of(i * 32, 32), 32), :]
        return carry + (block[0:8] + block[8:16]) + (block[16:24] + block[24:32])

    source_copy.wait()
    got = lax.fori_loop(0, OWNERS // 4, add_sender, zero)
    own = zero
    for d in range(3):
        own = jnp.where(lane // 32 == d, roll(got, 32 + 32 * d)[d : d + 1], own)
    own = jnp.where((row == 0) & (lane < 96), own, 0.0)
    full = jnp.concatenate([got, own, jnp.zeros((112, 128), F32)], 0)
    turned = jnp.transpose(full)
    values = jnp.zeros((24, 128), F32)
    lane24 = lanes_of((24, 128))
    for k in range(4):
        part = turned[k * 24 : (k + 1) * 24]
        values = jnp.where(lane24 // 16 == k, roll(part, 16 * k), values)
    high, middle, low = three_parts(values)
    high, middle, low = high.astype(F32), middle.astype(F32), low.astype(F32)
    values = jnp.concatenate([jnp.where(lane24 < 64, high, roll(middle, 64)), low], 1)

    row16 = rows_of((16, 128))
    cells = jnp.zeros((16, 128), F32)
    for d, (dx, dy) in enumerate(AROUND + [(0, 0)]):
        line = edges[(0, 3, 2)[dx]][EDGES][dy + 1 : dy + 2]
        cells = jnp.where(row16 == d, line, cells)
    turned = jnp.transpose(jnp.concatenate([cells, jnp.zeros((112, 128), F32)], 0))
    lane1 = lanes_of((1, 128))
    across = jnp.zeros((1, 128), F32)
    for k in range(4):
        across = jnp.where(lane1 // 16 == k, roll(turned[k : k + 1], 16 * k), across)
    across = jnp.where(lane1 < 64, across, roll(across, 64)).astype(jnp.int32)
    across = jnp.concatenate([across, across], 1)
    along = jnp.concatenate([jnp.broadcast_to(cells[:, k : k + 1], (16, 256)) for k in range(4)], 0)
    along = along.astype(jnp.int32)
    at_row = rows_of((ROWS, 256)) == across // NX - tile_y * CY + HALO
    at_x = along % NX - tile_x * CX
    n = lanes_of((64, 256))
    hit = (n == at_x) & (n < 128)
    hit = hit | ((n - 128 == at_x + 8) & (n >= 128) & (n < 144))
    hit = hit | ((n - 192 == at_x - 120) & (n >= 192) & (n < 208))
    hit = jnp.where(hit, 1.0, 0.0).astype(BF16)
    hit = jnp.concatenate([hit, hit, hit, hit], 0)
    spread = jnp.concatenate(
        [jnp.where(at_row, values[i : i + 1], 0.0).astype(BF16) for i in range(24)], 0
    )
    plane_src[...] = jnp.dot(spread, hit, preferred_element_type=F32)

    tools = stencil_tools(main_v, main_s, strip_v, strip_s)
    mload, sload, next_x, prev_x, next_z, prev_z = tools

    def velocity_group(step, g):
        r = 8 * g
        edges = {(f, s): sload(f, s, r) for f in range(SXX, WAVES) for s in range(2)}
        below_xz = below_yz = zero
        zz = mload(SZZ, 0, r)
        for z in range(NZ):
            xx, xy, yy, xz, yz = (mload(f, z, r) for f in (SXX, SXY, SYY, SXZ, SYZ))
            above_zz = mload(SZZ, z + 1, r) if z < NZ - 1 else zero
            ax = (next_x(xx, edges[SXX, 1], z) - xx) + (xy - mload(SXY, z, r - 1)) + (xz - below_xz)
            ay = (xy - prev_x(xy, edges[SXY, 0], z)) + (mload(SYY, z, r + 1) - yy) + (yz - below_yz)
            az = (xz - prev_x(xz, edges[SXZ, 0], z)) + (yz - mload(SYZ, z, r - 1)) + (above_zz - zz)
            below_xz, below_yz, zz = xz, yz, above_zz
            hb = mats[2 * NZ + z, pl.ds(r, 8), :]
            for c, a in enumerate((ax, ay, az)):
                if z == 0:
                    at = pl.multiple_of((c * STEPS + step) * ROWS + 8 * g, 8)
                    a = a + plane_src[pl.ds(at, 8), 0:128]
                main_v[c * NZ + z, pl.ds(r, 8), :] = mload(c, z, r) + hb * a
        for side in range(2):
            xx, yy, zz, xy, xz, yz = (edges[f, side] for f in (SXX, SYY, SZZ, SXY, SXZ, SYZ))
            ax = (roll(xx, -1) - xx) + (xy - sload(SXY, side, r - 1)) + (xz - prev_z(xz))
            ay = (xy - roll(xy, 1)) + (sload(SYY, side, r + 1) - yy) + (yz - prev_z(yz))
            az = (xz - roll(xz, 1)) + (yz - sload(SYZ, side, r - 1)) + (next_z(zz) - zz)
            hb = mat_strips[2 * 2 + side, pl.ds(r, 8), :]
            for c, a in enumerate((ax, ay, az)):
                at = pl.multiple_of((c * STEPS + step) * ROWS + 8 * g, 8)
                src = plane_src[pl.ds(at, 8), 128:256]
                src = jnp.where(lane < 16, roll(src, 64) if side else src, 0.0)
                strip_v[2 * c + side, pl.ds(r, 8), :] = sload(c, side, r) + hb * (a + src)

    def stress_strips(g):
        r = 8 * g
        for side in range(2):
            vx, vy, vz = (sload(f, side, r) for f in range(3))
            exx = vx - roll(vx, 1)
            eyy = vy - sload(VY, side, r - 1)
            ezz = vz - prev_z(vz)
            exy = (sload(VX, side, r + 1) - vx) + (roll(vy, -1) - vy)
            exz = (next_z(vx) - vx) + (roll(vz, -1) - vz)
            eyz = (next_z(vy) - vy) + (sload(VZ, side, r + 1) - vz)
            pressure = mat_strips[side, pl.ds(r, 8), :] * (exx + eyy + ezz)
            hm = mat_strips[2 + side, pl.ds(r, 8), :]
            hm2 = hm + hm
            for f, change in (
                (SXX, pressure + hm2 * exx),
                (SYY, pressure + hm2 * eyy),
                (SZZ, pressure + hm2 * ezz),
                (SXY, hm * exy),
                (SXZ, hm * exz),
                (SYZ, hm * eyz),
            ):
                strip_s[2 * f - 6 + side, pl.ds(r, 8), :] = sload(f, side, r) + change

    def stresses(step, update):
        for made in forward_copies(step):
            made.wait()
        if update:
            stress_planes(tools, mats, main_s, kern, 0, None, True)
        for i in range(CY // 16):
            both = [
                [ref[step, z, 16 * i : 16 * i + 16, :].astype(F32) for z in range(NZ)]
                for ref in (fd, fs)
            ]
            for half in range(2):
                part = [[v[8 * half : 8 * half + 8] for v in vs] for vs in both]
                stress_planes(tools, mats, main_s, kern, 1 + 2 * i + half, part, update)
        if update:
            stress_planes(tools, mats, main_s, kern, GROUPS - 1, None, True)
            for g in range(GROUPS):
                stress_strips(g)

    def one_step(step, carry):
        for g in range(GROUPS):
            velocity_group(step, g)
        stresses(step, True)
        return carry

    lax.fori_loop(0, STEPS - 1, one_step, 0)
    for g in range(GROUPS):
        velocity_group(STEPS - 1, g)
    strip_copy = pltpu.make_async_copy(strip_v, strip_out, sems.at[2 * STEPS])
    strip_copy.start()
    stresses(STEPS - 1, False)

    slot = tile_map[...] // 256 * 2 + (tile_map[...] % 256 - 2 * me)
    slot = slot.astype(F32)
    line = jnp.zeros((8, 128), F32)
    for y in range(8):
        half = slot[:, 128 * (y // 4) : 128 * (y // 4) + 128]
        line = jnp.where(row == y, roll(half, -32 * (y % 4)), line)
    widen = jnp.where(lanes_of((128, 128)) // 4 == rows_of((128, 128)), 1.0, 0.0).astype(BF16)
    line = jnp.where(lane < 32, line, 0.0).astype(BF16)
    line = jnp.dot(line, widen, preferred_element_type=F32)
    place = rows_of((256, 128)).astype(F32)
    put = jnp.concatenate(
        [jnp.where(line[y : y + 1] == place, 1.0 / 16, 0.0).astype(BF16) for y in range(8)], 1
    )
    sums = []
    for y in range(8):
        parts = [kern[pl.ds(4 * y + i, 2 * NZ, stride=CY), :] for i in range(4)]
        sums.append((parts[0] + parts[1]) + (parts[2] + parts[3]))
    sums = jnp.concatenate(three_parts(jnp.concatenate(sums, 1)), 0)
    placed = lax.dot_general(put, sums, (((1,), (1,)), ((), ())), preferred_element_type=F32)
    placed = placed[:, 0:16] + placed[:, 16:32] + placed[:, 32:48]
    made_send[...] = jnp.concatenate([placed, jnp.zeros((256, 112), F32)], 1)
    send_copy = pltpu.make_async_copy(made_send, send, sems.at[0])
    send_copy.start()
    send_copy.wait()
    strip_copy.wait()


def finish_kernel(velocity, s_in, mats, strip_in, stress, out, strip_v, sems):
    del s_in
    pltpu.sync_copy(strip_in, strip_v)
    tools = stencil_tools(velocity, stress, strip_v, None)
    copies = []

    def deliver(f, rows, start):
        ref, p = at_plane(velocity, stress, None, f)
        made = pltpu.make_async_copy(
            ref.at[pl.ds(p, NZ), pl.ds(HALO + start, rows), :],
            out.at[f, :, pl.ds(start, rows), :],
            sems.at[len(copies)],
        )
        made.start()
        copies.append(made)

    for f in range(3):
        deliver(f, CY, 0)
    for g in range(CY // 8):
        stress_planes(tools, mats, stress, None, g + 1, None, True)
        for f in range(3, WAVES):
            deliver(f, 8, 8 * g)
    for made in copies:
        made.wait()


def turn_kernel(got, out):
    out[...] = jnp.transpose(got[...])[0:16]


def shift(value, dx, dy):
    pairs = [
        (x * N_GY + y, (x + dx) * N_GY + y + dy)
        for x in range(N_GX)
        for y in range(N_GY)
        if 0 <= x + dx < N_GX and 0 <= y + dy < N_GY
    ]
    return lax.ppermute(value, ("gx", "gy"), pairs)


def shape(*dims):
    return jax.ShapeDtypeStruct(dims, F32)


def cost(flops, data):
    return pl.CostEstimate(flops=flops, bytes_accessed=data, transcendentals=0)


def local(
    adjoint_state,
    lame_lambda,
    shear_modulus,
    buoyancy,
    forward_dilation,
    forward_shear,
    residual,
    sample_counts,
    station_list,
    receiver_cells,
    tile_map,
):
    rows_dev = residual.shape[0]
    in_hbm = lambda value: pltpu.with_memory_space_constraint(value, pltpu.HBM)
    adjoint_state, lame_lambda, shear_modulus, buoyancy, forward_dilation, forward_shear = (
        in_hbm(value)
        for value in (
            adjoint_state,
            lame_lambda,
            shear_modulus,
            buoyancy,
            forward_dilation,
            forward_shear,
        )
    )

    held = (shape(3 * NZ, ROWS, 128), shape(6 * NZ, ROWS, 128), shape(3 * NZ, ROWS, 128))
    velocity, stress, mats, up, down, by_owner = pl.pallas_call(
        first_kernel,
        out_shape=held + (shape(PLANES + 1, 8, 128), shape(PLANES + 1, 8, 128), shape(128, 128)),
        in_specs=[ANY] * 4 + [SMEM, ANY, VMEM, VMEM, ANY],
        out_specs=(VMEM,) * 6,
        scratch_shapes=[
            pltpu.VMEM((SAMPLES, 128), BF16),
            pltpu.VMEM((3, rows_dev, SAMPLES), BF16),
            pltpu.SemaphoreType.DMA((FIELDS + 4,)),
        ],
        compiler_params=PART,
        cost_estimate=cost(1 << 30, 1 << 22),
    )(
        adjoint_state,
        lame_lambda,
        shear_modulus,
        buoyancy,
        in_hbm(receiver_cells.reshape(1, 4)),
        in_hbm(jnp.transpose(residual, (1, 0, 2))),
        in_hbm(sample_counts.reshape(1, rows_dev)),
        in_hbm(station_list.reshape(1, rows_dev)),
        in_hbm(jnp.asarray(resample_table())),
    )
    from_below = shift(up, 0, 1)
    from_above = shift(down, 0, -1)

    send = pl.pallas_call(
        send_kernel,
        out_shape=pltpu.HBM((OWNERS * 8, 128), F32),
        in_specs=[VMEM],
        out_specs=ANY,
        scratch_shapes=[
            pltpu.VMEM((OWNERS * 8, 128), F32),
            pltpu.VMEM((176, 128), F32),
            pltpu.SemaphoreType.DMA((4,)),
        ],
        compiler_params=PART,
        cost_estimate=cost(1 << 20, 1 << 20),
    )(by_owner)
    sources = lax.all_to_all(send, ("gx", "gy"), 0, 0, tiled=True)

    velocity, stress, mats, right, left = pl.pallas_call(
        edges_kernel,
        out_shape=held + (shape(EDGES + 1, 8, 128), shape(EDGES + 1, 8, 128)),
        in_specs=[VMEM] * 6,
        out_specs=(VMEM,) * 5,
        input_output_aliases={0: 0, 1: 1, 2: 2},
        compiler_params=PART,
        cost_estimate=cost(1 << 20, 1 << 21),
    )(velocity, stress, mats, from_below, from_above, up)
    from_left = shift(right, 1, 0)
    from_right = shift(left, -1, 0)

    velocity, stress, send, strip_v = pl.pallas_call(
        step_kernel,
        out_shape=held[:2] + (pltpu.HBM((256, 128), F32), pltpu.HBM((6, ROWS, 128), F32)),
        in_specs=[VMEM] * 7 + [ANY] * 3 + [VMEM],
        out_specs=(VMEM, VMEM, ANY, ANY),
        input_output_aliases={0: 0, 1: 1},
        scratch_shapes=[
            pltpu.VMEM((6, ROWS, 128), F32),
            pltpu.VMEM((12, ROWS, 128), F32),
            pltpu.VMEM((6, ROWS, 128), F32),
            pltpu.VMEM((STEPS, NZ, CY, CX), BF16),
            pltpu.VMEM((STEPS, NZ, CY, CX), BF16),
            pltpu.VMEM((24 * ROWS, 256), F32),
            pltpu.VMEM((2 * NZ * CY, 128), F32),
            pltpu.VMEM((OWNERS * 8, 128), F32),
            pltpu.VMEM((256, 128), F32),
            pltpu.SemaphoreType.DMA((2 * STEPS + 1,)),
        ],
        compiler_params=PART,
        cost_estimate=cost(1 << 27, 1 << 23),
    )(
        velocity,
        stress,
        mats,
        right,
        left,
        from_left,
        from_right,
        forward_dilation,
        forward_shear,
        sources,
        in_hbm(tile_map.reshape(1, 256)),
    )
    got = lax.all_to_all(send, ("gx", "gy"), 0, 0, tiled=True)
    _, adjoint_out = pl.pallas_call(
        finish_kernel,
        out_shape=(held[1], shape(WAVES, NZ, CY, CX)),
        in_specs=[VMEM] * 3 + [ANY],
        out_specs=(VMEM, ANY),
        input_output_aliases={1: 0},
        scratch_shapes=[pltpu.VMEM((6, ROWS, 128), F32), pltpu.SemaphoreType.DMA((27,))],
        compiler_params=PART,
        cost_estimate=cost(1 << 24, 1 << 22),
    )(velocity, stress, mats, strip_v)
    kernels = pl.pallas_call(
        turn_kernel,
        out_shape=shape(16, 256),
        in_specs=[VMEM],
        out_specs=VMEM,
        compiler_params=PART,
    )(got)
    return kernels.reshape(2, NZ, 256), adjoint_out


def solution(mesh):
    in_specs = (
        P(None, None, "gy", "gx"),
        P(None, "gy", "gx"),
        P(None, "gy", "gx"),
        P(None, "gy", "gx"),
        P(None, None, "gy", "gx"),
        P(None, None, "gy", "gx"),
        P(("gx", "gy"), None, None),
        P(("gx", "gy")),
        P(("gx", "gy")),
        P(("gx", "gy")),
        P(("gx", "gy")),
    )
    out_specs = (P(None, None, ("gx", "gy")), P(None, None, "gy", "gx"))
    return jax.shard_map(local, mesh=mesh, in_specs=in_specs, out_specs=out_specs, check_vma=False)
```

time: 72.8 us -> 69 us (0.948)
  blocking collectives: 18.9 us -> 0 us
  starting transfers between devices: 23.8 us -> 32.6 us
  waiting for transfers between devices: 5.37 us -> 13.7 us
  Pallas kernels: 22.9 us -> 20.8 us
    all_to_all x1 -> x0, blocking collectives: 18.9 us -> none  [local(): got = lax.all_to_all(send, ('gx', 'gy'), 0, 0, tiled=True)]
    all_to_all x0 -> x1, starting transfers between devices: none -> 8.08 us  [local(): got = lax.all_to_all(send, ('gx', 'gy'), 0, 0, tiled=True)]
    all_to_all x0 -> x1, waiting for transfers between devices: none -> 7.86 us  [local(): got = lax.all_to_all(send, ('gx', 'gy'), 0, 0, tiled=True)]
    pallas_call x3 -> x4, Pallas kernels: 18.4 us -> 17.3 us  [the longest x1 10.6 us: local(): pl.pallas_call(step_kernel, out_shape=held[:2] + (pltpu.HBM((256, 128), F...]
    pallas_call x1, Pallas kernels: 1.58 us -> 0.68 us  [local(): pl.pallas_call(turn_kernel, out_shape=shape(16, 256), in_specs=[VMEM], ou...]
  transfers between devices with their start and end apart: 5 -> 6, of which waited for: 1 -> 2; matrix products, arithmetic and copies ran while one was open for 0% -> 0% of each run, Pallas kernels for 9% -> 8%
where the time goes in v3:
time: 69 us; the launch traced here: 68.7 us
  starting transfers between devices  32.6 us (47%)
  Pallas kernels  20.8 us (30%)
  waiting for transfers between devices  13.7 us (20%)
  local copies, waits for them, and re-layouts  0.91 us (1%)
  between operations  0.73 us (1%)
    all_to_all x1, starting transfers between devices, local(): sources = lax.all_to_all(send, ('gx', 'gy'), 0, 0, tiled=True)  12.4 us
    ppermute x4, starting transfers between devices, shift(): return lax.ppermute(value, ('gx', 'gy'), pairs)  12.1 us
    pallas_call x1, Pallas kernels, local(): pl.pallas_call(step_kernel, out_shape=held[:2] + (pltpu.HBM((256, 128), F...  10.6 us
    all_to_all x1, starting transfers between devices, local(): got = lax.all_to_all(send, ('gx', 'gy'), 0, 0, tiled=True)  8.08 us
    all_to_all x1, waiting for transfers between devices, local(): got = lax.all_to_all(send, ('gx', 'gy'), 0, 0, tiled=True)  7.86 us
    all_to_all x1, waiting for transfers between devices, local(): sources = lax.all_to_all(send, ('gx', 'gy'), 0, 0, tiled=True)  5.79 us
    pallas_call x1, Pallas kernels, local(): pl.pallas_call(first_kernel, out_shape=held + (shape(PLANES + 1, 8, 128),...  4.38 us
    pallas_call x1, Pallas kernels, local(): pl.pallas_call(edges_kernel, out_shape=held + (shape(EDGES + 1, 8, 128),...  2.85 us
  transfers between devices with their start and end apart: 6, of which 2 were waited for; matrix products, arithmetic and copies ran while one was open for 0% of the time, Pallas kernels for 8%

profile of v3, /device:TPU:1, one launch (start us, length us, event | category | flops | bytes accessed | tf_op | source)
XLA Modules:
  0.0 68.7 jit_solution(18144508306886340246)
XLA Ops:
  0.6 4.4 %shard_map.131 = (f32[24,48,128]{2,1,0:T(8,128)S(1)}, f32[48,48,128]{2,1,0:T(8,128)S(1)}, f32[24,48,128]{2,1,0:T(8,128)S(1)}, f32[97,8,128]{2,1,0:T(8,128)S(1)},...) custom-call(f32[9,8,32,128]{3,2,1,0:T(8,128)} %state.1, f32[8,32,128]{2,1,0:T(8,128)} %lame.1, f32[8,32,128]{2,1,0:T(8,128)} %shear.1, ...), custom_call_target="tpu_custom_call" | custom-call | flops 1073741824 | bytes 4194304 | tf_op jit(solution)/shard_map/pallas_call | solution.py:596
  5.0 1.3 %collective-permute-start.1 = (f32[97,8,128]{2,1,0:T(8,128)}, f32[97,8,128]{2,1,0:T(8,128)}, u32[]{:S(2)}, u32[]{:S(2)}) collective-permute-start(f32[97,8,128]{2,1,0:T(8,128)} %get-tuple-element.22), channel_id=1, source_target_pairs={{1,0},{2,1},{3,2},{4,3},{5,4},{6,5},{7,6},{8,7},{9,8},{10,9},{11,1... | collective-permute-start | bytes 1191944 | tf_op jit(solution)/shard_map/ppermute | solution.py:557
  6.3 5.3 %collective-permute-start = (f32[97,8,128]{2,1,0:T(8,128)S(1)}, f32[97,8,128]{2,1,0:T(8,128)}, u32[]{:S(2)}, u32[]{:S(2)}) collective-permute-start(f32[97,8,128]{2,1,0:T(8,128)S(1)} %get-tuple-element.21.own), channel_id=1, source_target_pairs={{0,1},{1,2},{2,3},{3,4},{4,5},{5,6},{6,7},{7,8},{8,9},{9,10},{10,1... | collective-permute-start | bytes 1191944 | tf_op jit(solution)/shard_map/ppermute | solution.py:557
  11.6 0.9 %shard_map.133 = f32[1024,128]{1,0:T(8,128)} custom-call(f32[128,128]{1,0:T(8,128)S(1)} %get-tuple-element.28.by_owner), custom_call_target="tpu_custom_call" | custom-call | flops 1048576 | bytes 1048576 | tf_op jit(solution)/shard_map/pallas_call | solution.py:622
  12.5 12.4 %all-to-all-start = ((f32[128,8,128]{2,1,0:T(8,128)}), f32[128,8,128]{2,1,0:T(8,128)S(1)}, u32[]{:S(2)}, u32[]{:S(2)}) async-start(f32[128,8,128]{2,1,0:T(8,128)} %bitcast.13), calls=%async_computation | async-start | bytes 1048576 | tf_op jit(solution)/shard_map/all_to_all | solution.py:635
  25.0 0.0 collective-permute-done.1.above
  25.0 0.0 collective-permute-done.below
  25.0 2.8 %shard_map.132 = (f32[24,48,128]{2,1,0:T(8,128)S(1)}, f32[48,48,128]{2,1,0:T(8,128)S(1)}, f32[24,48,128]{2,1,0:T(8,128)S(1)}, f32[37,8,128]{2,1,0:T(8,128)S(1)}, f32[37,8,128]{2,1,0:T(8,128)}) custom-call(f32[24,48,128]{2,1,0:T(8,128)S(1)} %get-tuple-element.18.v_in, ...), custom_call_target="tpu_custom_call", output_to_operand_aliasing={{0}: (0, {}), {1}: (1, {}), {2}: (2, {})} | custom-call | flops 1048576 | bytes 2097152 | tf_op jit(solution)/shard_map/pallas_call | solution.py:637
  27.9 3.5 %collective-permute-start.2 = (f32[37,8,128]{2,1,0:T(8,128)S(1)}, f32[37,8,128]{2,1,0:T(8,128)S(1)}, u32[]{:S(2)}, u32[]{:S(2)}) collective-permute-start(f32[37,8,128]{2,1,0:T(8,128)S(1)} %get-tuple-element.26.own_right), channel_id=1, source_target_pairs={{0,16},{1,17},{2,18},{3,19},{4,20},{5,21},{6,22},{7,23},{8,24},{9,... | collective-permute-start | bytes 454664 | tf_op jit(solution)/shard_map/ppermute | solution.py:557
  31.4 1.9 %collective-permute-start.3 = (f32[37,8,128]{2,1,0:T(8,128)}, f32[37,8,128]{2,1,0:T(8,128)S(1)}, u32[]{:S(2)}, u32[]{:S(2)}) collective-permute-start(f32[37,8,128]{2,1,0:T(8,128)} %get-tuple-element.27.own_left), channel_id=1, source_target_pairs={{16,0},{17,1},{18,2},{19,3},{20,4},{21,5},{22,6},{23,7},{24,8},{25... | collective-permute-start | bytes 454664 | tf_op jit(solution)/shard_map/ppermute | solution.py:557
  33.3 5.8 %all-to-all-done = f32[128,8,128]{2,1,0:T(8,128)S(1)} async-done(((f32[128,8,128]{2,1,0:T(8,128)}), f32[128,8,128]{2,1,0:T(8,128)S(1)}, u32[]{:S(2)}, u32[]{:S(2)}) %all-to-all-start) | async-done | bytes 524320 | tf_op jit(solution)/shard_map/all_to_all | solution.py:635
  39.1 0.0 collective-permute-done.2.from_left
  39.1 0.0 collective-permute-done.3.from_right
  39.1 10.6 %shard_map.134 = (f32[24,48,128]{2,1,0:T(8,128)S(1)}, f32[48,48,128]{2,1,0:T(8,128)S(1)}, f32[256,128]{1,0:T(8,128)}, f32[6,48,128]{2,1,0:T(8,128)}) custom-call(f32[24,48,128]{2,1,0:T(8,128)S(1)} %get-tuple-element.23.v_in, f32[48,48,128]{2,1,0:T(8,128)S(1)} %get-tuple-element.24.s_in, ...), custom_call_target="tpu_custom_call", output_to_operand_aliasing={{0}: (0, {}), {1}: (1, {})} | custom-call | flops 134217728 | bytes 8388608 | tf_op jit(solution)/shard_map/pallas_call | solution.py:649
  49.7 8.1 %all-to-all-start.1 = ((f32[128,2,128]{2,1,0:T(2,128)}), f32[128,2,128]{2,1,0:T(2,128)S(1)}, u32[]{:S(2)}, u32[]{:S(2)}) async-start(f32[128,2,128]{2,1,0:T(2,128)} %bitcast.14), calls=%async_computation.1 | async-start | bytes 262144 | tf_op jit(solution)/shard_map/all_to_all | solution.py:682
  57.8 0.0 copy-start
  57.8 0.9 %copy-done = f32[6,48,128]{2,1,0:T(8,128)S(1)} copy-done((f32[6,48,128]{2,1,0:T(8,128)S(1)}, f32[6,48,128]{2,1,0:T(8,128)}, u32[]{:S(2)}) %copy-start) | copy-done | bytes 147480
  58.7 1.4 %shard_map.136 = (f32[48,48,128]{2,1,0:T(8,128)S(1)}, f32[9,8,32,128]{3,2,1,0:T(8,128)}) custom-call(f32[24,48,128]{2,1,0:T(8,128)S(1)} %get-tuple-element.30.velocity, f32[48,48,128]{2,1,0:T(8,128)S(1)} %get-tuple-element.31.s_in, f32[24,48,128]{2,1,0:T(8,128)S(1)} %get-tuple-element.25.mats, f32[6,48,128]{2,1,0:T(8,128)S(1)} %copy-done), custom_call_target="tpu_custom_call", output_to_operand_aliasing={{0}: (1, {})} | custom-call | flops 16777216 | bytes 4194304 | tf_op jit(solution)/shard_map/pallas_call | solution.py:683
  60.1 7.9 %all-to-all-done.1 = f32[128,2,128]{2,1,0:T(2,128)S(1)} async-done(((f32[128,2,128]{2,1,0:T(2,128)}), f32[128,2,128]{2,1,0:T(2,128)S(1)}, u32[]{:S(2)}, u32[]{:S(2)}) %all-to-all-start.1) | async-done | bytes 131104 | tf_op jit(solution)/shard_map/all_to_all | solution.py:682
  68.0 0.7 shard_map.135
Async XLA Ops:
  5.0 20.0 %collective-permute-start.1 = (f32[97,8,128]{2,1,0:T(8,128)}, f32[97,8,128]{2,1,0:T(8,128)}, u32[]{:S(2)}, u32[]{:S(2)}) collective-permute-start(f32[97,8,128]{2,1,0:T(8,128)} %get-tuple-element.22), channel_id=1, source_target_pairs={{1,0},{2,1},{3,2},{4,3},{5,4},{6,5},{7,6},{8,7},{9,8},{10,9},{11,1... | collective-permute-start | bytes 1191944 | tf_op jit(solution)/shard_map/ppermute | solution.py:557
  6.3 18.7 %collective-permute-start = (f32[97,8,128]{2,1,0:T(8,128)S(1)}, f32[97,8,128]{2,1,0:T(8,128)}, u32[]{:S(2)}, u32[]{:S(2)}) collective-permute-start(f32[97,8,128]{2,1,0:T(8,128)S(1)} %get-tuple-element.21.own), channel_id=1, source_target_pairs={{0,1},{1,2},{2,3},{3,4},{4,5},{5,6},{6,7},{7,8},{8,9},{9,10},{10,1... | collective-permute-start | bytes 1191944 | tf_op jit(solution)/shard_map/ppermute | solution.py:557
  12.5 26.6 %all-to-all-start = ((f32[128,8,128]{2,1,0:T(8,128)}), f32[128,8,128]{2,1,0:T(8,128)S(1)}, u32[]{:S(2)}, u32[]{:S(2)}) async-start(f32[128,8,128]{2,1,0:T(8,128)} %bitcast.13), calls=%async_computation | async-start | bytes 1048576 | tf_op jit(solution)/shard_map/all_to_all | solution.py:635
  27.9 11.3 %collective-permute-start.2 = (f32[37,8,128]{2,1,0:T(8,128)S(1)}, f32[37,8,128]{2,1,0:T(8,128)S(1)}, u32[]{:S(2)}, u32[]{:S(2)}) collective-permute-start(f32[37,8,128]{2,1,0:T(8,128)S(1)} %get-tuple-element.26.own_right), channel_id=1, source_target_pairs={{0,16},{1,17},{2,18},{3,19},{4,20},{5,21},{6,22},{7,23},{8,24},{9,... | collective-permute-start | bytes 454664 | tf_op jit(solution)/shard_map/ppermute | solution.py:557
  31.4 7.7 %collective-permute-start.3 = (f32[37,8,128]{2,1,0:T(8,128)}, f32[37,8,128]{2,1,0:T(8,128)S(1)}, u32[]{:S(2)}, u32[]{:S(2)}) collective-permute-start(f32[37,8,128]{2,1,0:T(8,128)} %get-tuple-element.27.own_left), channel_id=1, source_target_pairs={{16,0},{17,1},{18,2},{19,3},{20,4},{21,5},{22,6},{23,7},{24,8},{25... | collective-permute-start | bytes 454664 | tf_op jit(solution)/shard_map/ppermute | solution.py:557
  49.7 18.3 %all-to-all-start.1 = ((f32[128,2,128]{2,1,0:T(2,128)}), f32[128,2,128]{2,1,0:T(2,128)S(1)}, u32[]{:S(2)}, u32[]{:S(2)}) async-start(f32[128,2,128]{2,1,0:T(2,128)} %bitcast.14), calls=%async_computation.1 | async-start | bytes 262144 | tf_op jit(solution)/shard_map/all_to_all | solution.py:682
  57.8 0.9 %copy-start = (f32[6,48,128]{2,1,0:T(8,128)S(1)}, f32[6,48,128]{2,1,0:T(8,128)}, u32[]{:S(2)}) copy-start(f32[6,48,128]{2,1,0:T(8,128)} %get-tuple-element.32.strip_in) | copy-start | bytes 442372

commit v4 on v3

--- a/solution.py
+++ b/solution.py
@@ -65,8 +65,8 @@
     distance = np.abs(position[:, None] - centers[None, :]) / np.float32(per_step)
     weight = np.maximum(np.float32(0.0), np.float32(1.0) - distance)
     table = (weight / np.float32(math.sqrt(per_step))).astype(BF16)
-    wide = np.zeros((SAMPLES, 128), BF16)
-    wide[:, :96] = np.tile(table, (1, 12))
+    wide = np.zeros((per_step, 128), BF16)
+    wide[:, :96] = np.tile(table[per_step : 2 * per_step], (1, 12))
     return wide
 
 
@@ -94,10 +94,13 @@
     up,
     down,
     by_owner,
+    base,
     table,
     held,
     sems,
 ):
+    weights_in = pltpu.make_async_copy(weights, base, sems.at[FIELDS])
+    weights_in.start()
     copies = []
     for f in range(FIELDS):
         to, p = at_plane(velocity, stress, mats, f)
@@ -105,8 +108,6 @@
         to = to.at[pl.ds(p, NZ), pl.ds(HALO, CY), :]
         copies.append(pltpu.make_async_copy(source, to, sems.at[f]))
         copies[f].start()
-    table_copy = pltpu.make_async_copy(weights, table, sems.at[FIELDS])
-    table_copy.start()
     rows_in = [
         pltpu.make_async_copy(residual.at[c], held.at[c], sems.at[FIELDS + 1 + c]) for c in range(3)
     ]
@@ -123,13 +124,21 @@
     count = column_of(jnp.concatenate([counts[...].astype(F32), pad], 1))[:rows]
     station_row = jnp.concatenate([stations[...], jnp.full((1, 128 - rows), -1, jnp.int32)], 1)
     station = column_of(station_row.astype(F32))[:rows].astype(jnp.int32)
+    weights_in.wait()
+    per_step = SAMPLES // STEPS
+    middle = base[...].astype(F32)
+    slot = lanes_of((per_step, 128)) % STEPS
+    for j in range(STEPS):
+        moved = roll(middle, j - 1)
+        if j in (0, STEPS - 1):
+            moved = jnp.where(slot == STEPS - 1 - j, 0.0, moved)
+        table[per_step * j : per_step * (j + 1), :] = moved.astype(BF16)
     for f in range(FIELDS):
         copies[f].wait()
         ref, p = at_plane(velocity, stress, mats, f)
         for z in range(NZ):
             down[f * NZ + z] = ref[p + z, 8:16, :]
             up[f * NZ + z] = ref[p + z, 32:40, :]
-    table_copy.wait()
     by_owner[...] = sums_by_owner(rows_in, held, table, count, station, station_row)
 
 
@@ -267,7 +276,7 @@
         if forward is not None:
             for k, strain in ((0, dilation), (1, exy)):
                 at = pl.ds((k * NZ + z) * CY + 8 * (g - 1), 8)
-                kern[at, :] = kern[at, :] + forward[k][z] * (H * strain)
+                kern[at, :] = kern[at, :] + forward(k, z) * strain
         if update:
             exz = (above_vx - vx) + (next_x(vz, right_vz, z) - vz)
             eyz = (above_vy - vy) + (mload(VZ, z, r + 1) - vz)
@@ -309,14 +318,10 @@
     fs,
     plane_src,
     kern,
-    got_sources,
     made_send,
     sems,
 ):
     del v_in, s_in
-    source_copy = pltpu.make_async_copy(sources, got_sources, sems.at[2 * STEPS])
-    source_copy.start()
-
     def forward_copies(t):
         return (
             pltpu.make_async_copy(forward_dilation.at[t], fd.at[t], sems.at[t]),
@@ -356,11 +361,12 @@
                 else:
                     mat_strips[at - 2 * WAVES, 8 * g : 8 * g + 8, :] = made[i]
     def add_sender(i, carry):
-        block = got_sources[pl.ds(pl.multiple_of(i * 32, 32), 32), :]
-        return carry + (block[0:8] + block[8:16]) + (block[16:24] + block[24:32])
-
-    source_copy.wait()
-    got = lax.fori_loop(0, OWNERS // 4, add_sender, zero)
+        parts = [sources[pl.ds(pl.multiple_of(i * 128 + 8 * j, 8), 8), :] for j in range(16)]
+        while len(parts) > 1:
+            parts = [a + b for a, b in zip(parts[::2], parts[1::2])]
+        return carry + parts[0]
+
+    got = lax.fori_loop(0, OWNERS // 16, add_sender, zero)
     own = zero
     for d in range(3):
         own = jnp.where(lane // 32 == d, roll(got, 32 + 32 * d)[d : d + 1], own)
@@ -459,36 +465,37 @@
             ):
                 strip_s[2 * f - 6 + side, pl.ds(r, 8), :] = sload(f, side, r) + change
 
-    def stresses(step, update):
+    def stress_rows(step, g, update):
+        forward = None
+        if 0 < g < GROUPS - 1:
+            at = (g - 1) // 2 * 16
+
+            def forward(k, z):
+                both = (fd, fs)[k][step, z, at : at + 16, :].astype(F32)
+                return both[(g - 1) % 2 * 8 : (g - 1) % 2 * 8 + 8]
+
+        if update or forward is not None:
+            stress_planes(tools, mats, main_s, kern, g, forward, update)
+        if update:
+            stress_strips(g)
+
+    def step_rows(step, update):
         for made in forward_copies(step):
             made.wait()
-        if update:
-            stress_planes(tools, mats, main_s, kern, 0, None, True)
-        for i in range(CY // 16):
-            both = [
-                [ref[step, z, 16 * i : 16 * i + 16, :].astype(F32) for z in range(NZ)]
-                for ref in (fd, fs)
-            ]
-            for half in range(2):
-                part = [[v[8 * half : 8 * half + 8] for v in vs] for vs in both]
-                stress_planes(tools, mats, main_s, kern, 1 + 2 * i + half, part, update)
-        if update:
-            stress_planes(tools, mats, main_s, kern, GROUPS - 1, None, True)
-            for g in range(GROUPS):
-                stress_strips(g)
-
-    def one_step(step, carry):
         for g in range(GROUPS):
             velocity_group(step, g)
-        stresses(step, True)
+            if g > 0:
+                stress_rows(step, g - 1, update)
+        stress_rows(step, GROUPS - 1, update)
+
+    def one_step(step, carry):
+        step_rows(step, True)
         return carry
 
     lax.fori_loop(0, STEPS - 1, one_step, 0)
-    for g in range(GROUPS):
-        velocity_group(STEPS - 1, g)
+    step_rows(STEPS - 1, False)
     strip_copy = pltpu.make_async_copy(strip_v, strip_out, sems.at[2 * STEPS])
     strip_copy.start()
-    stresses(STEPS - 1, False)
 
     slot = tile_map[...] // 256 * 2 + (tile_map[...] % 256 - 2 * me)
     slot = slot.astype(F32)
@@ -501,7 +508,7 @@
     line = jnp.dot(line, widen, preferred_element_type=F32)
     place = rows_of((256, 128)).astype(F32)
     put = jnp.concatenate(
-        [jnp.where(line[y : y + 1] == place, 1.0 / 16, 0.0).astype(BF16) for y in range(8)], 1
+        [jnp.where(line[y : y + 1] == place, H / 16, 0.0).astype(BF16) for y in range(8)], 1
     )
     sums = []
     for y in range(8):
@@ -599,6 +606,7 @@
         in_specs=[ANY] * 4 + [SMEM, ANY, VMEM, VMEM, ANY],
         out_specs=(VMEM,) * 6,
         scratch_shapes=[
+            pltpu.VMEM((SAMPLES // STEPS, 128), BF16),
             pltpu.VMEM((SAMPLES, 128), BF16),
             pltpu.VMEM((3, rows_dev, SAMPLES), BF16),
             pltpu.SemaphoreType.DMA((FIELDS + 4,)),
@@ -649,7 +657,7 @@
     velocity, stress, send, strip_v = pl.pallas_call(
         step_kernel,
         out_shape=held[:2] + (pltpu.HBM((256, 128), F32), pltpu.HBM((6, ROWS, 128), F32)),
-        in_specs=[VMEM] * 7 + [ANY] * 3 + [VMEM],
+        in_specs=[VMEM] * 7 + [ANY] * 2 + [VMEM] * 2,
         out_specs=(VMEM, VMEM, ANY, ANY),
         input_output_aliases={0: 0, 1: 1},
         scratch_shapes=[
@@ -660,7 +668,6 @@
             pltpu.VMEM((STEPS, NZ, CY, CX), BF16),
             pltpu.VMEM((24 * ROWS, 256), F32),
             pltpu.VMEM((2 * NZ * CY, 128), F32),
-            pltpu.VMEM((OWNERS * 8, 128), F32),
             pltpu.VMEM((256, 128), F32),
             pltpu.SemaphoreType.DMA((2 * STEPS + 1,)),
         ],

time: 69 us -> 68.4 us (level)
  no operation moved by 1% of the time
where the time goes in v4:
time: 68.4 us; the launch traced here: 68.1 us
  starting transfers between devices  32.6 us (48%)
  Pallas kernels  20.2 us (30%)
  waiting for transfers between devices  13.7 us (20%)
  local copies, waits for them, and re-layouts  0.91 us (1%)
  between operations  0.73 us (1%)
    all_to_all x1, starting transfers between devices, local(): sources = lax.all_to_all(send, ('gx', 'gy'), 0, 0, tiled=True)  12.4 us
    ppermute x4, starting transfers between devices, shift(): return lax.ppermute(value, ('gx', 'gy'), pairs)  12.1 us
    pallas_call x1, Pallas kernels, local(): pl.pallas_call(step_kernel, out_shape=held[:2] + (pltpu.HBM((256, 128), F...  10.3 us
    all_to_all x1, starting transfers between devices, local(): got = lax.all_to_all(send, ('gx', 'gy'), 0, 0, tiled=True)  8.08 us
    all_to_all x1, waiting for transfers between devices, local(): got = lax.all_to_all(send, ('gx', 'gy'), 0, 0, tiled=True)  7.86 us
    all_to_all x1, waiting for transfers between devices, local(): sources = lax.all_to_all(send, ('gx', 'gy'), 0, 0, tiled=True)  5.79 us
    pallas_call x1, Pallas kernels, local(): pl.pallas_call(first_kernel, out_shape=held + (shape(PLANES + 1, 8, 128),...  4.1 us
    pallas_call x1, Pallas kernels, local(): pl.pallas_call(edges_kernel, out_shape=held + (shape(EDGES + 1, 8, 128),...  2.85 us
  transfers between devices with their start and end apart: 6, of which 2 were waited for; matrix products, arithmetic and copies ran while one was open for 0% of the time, Pallas kernels for 8%

profile of v4, /device:TPU:1, one launch (start us, length us, event | category | flops | bytes accessed | tf_op | source)
XLA Modules:
  0.0 68.1 jit_solution(8558660691629299409)
XLA Ops:
  0.6 4.1 %shard_map.131 = (f32[24,48,128]{2,1,0:T(8,128)S(1)}, f32[48,48,128]{2,1,0:T(8,128)S(1)}, f32[24,48,128]{2,1,0:T(8,128)S(1)}, f32[97,8,128]{2,1,0:T(8,128)S(1)},...) custom-call(f32[9,8,32,128]{3,2,1,0:T(8,128)} %state.1, f32[8,32,128]{2,1,0:T(8,128)} %lame.1, f32[8,32,128]{2,1,0:T(8,128)} %shear.1, ...), custom_call_target="tpu_custom_call" | custom-call | flops 1073741824 | bytes 4194304 | tf_op jit(solution)/shard_map/pallas_call | solution.py:603
  4.7 1.3 %collective-permute-start.1 = (f32[97,8,128]{2,1,0:T(8,128)}, f32[97,8,128]{2,1,0:T(8,128)}, u32[]{:S(2)}, u32[]{:S(2)}) collective-permute-start(f32[97,8,128]{2,1,0:T(8,128)} %get-tuple-element.22), channel_id=1, source_target_pairs={{1,0},{2,1},{3,2},{4,3},{5,4},{6,5},{7,6},{8,7},{9,8},{10,9},{11,1... | collective-permute-start | bytes 1191944 | tf_op jit(solution)/shard_map/ppermute | solution.py:564
  6.0 5.3 %collective-permute-start = (f32[97,8,128]{2,1,0:T(8,128)S(1)}, f32[97,8,128]{2,1,0:T(8,128)}, u32[]{:S(2)}, u32[]{:S(2)}) collective-permute-start(f32[97,8,128]{2,1,0:T(8,128)S(1)} %get-tuple-element.21.own), channel_id=1, source_target_pairs={{0,1},{1,2},{2,3},{3,4},{4,5},{5,6},{6,7},{7,8},{8,9},{9,10},{10,1... | collective-permute-start | bytes 1191944 | tf_op jit(solution)/shard_map/ppermute | solution.py:564
  11.4 0.9 %shard_map.133 = f32[1024,128]{1,0:T(8,128)} custom-call(f32[128,128]{1,0:T(8,128)S(1)} %get-tuple-element.28.by_owner), custom_call_target="tpu_custom_call" | custom-call | flops 1048576 | bytes 1048576 | tf_op jit(solution)/shard_map/pallas_call | solution.py:630
  12.3 12.4 %all-to-all-start = ((f32[128,8,128]{2,1,0:T(8,128)}), f32[128,8,128]{2,1,0:T(8,128)S(1)}, u32[]{:S(2)}, u32[]{:S(2)}) async-start(f32[128,8,128]{2,1,0:T(8,128)} %bitcast.13), calls=%async_computation | async-start | bytes 1048576 | tf_op jit(solution)/shard_map/all_to_all | solution.py:643
  24.7 0.0 collective-permute-done.1.above
  24.7 0.0 collective-permute-done.below
  24.7 2.8 %shard_map.132 = (f32[24,48,128]{2,1,0:T(8,128)S(1)}, f32[48,48,128]{2,1,0:T(8,128)S(1)}, f32[24,48,128]{2,1,0:T(8,128)S(1)}, f32[37,8,128]{2,1,0:T(8,128)S(1)}, f32[37,8,128]{2,1,0:T(8,128)}) custom-call(f32[24,48,128]{2,1,0:T(8,128)S(1)} %get-tuple-element.18.v_in, ...), custom_call_target="tpu_custom_call", output_to_operand_aliasing={{0}: (0, {}), {1}: (1, {}), {2}: (2, {})} | custom-call | flops 1048576 | bytes 2097152 | tf_op jit(solution)/shard_map/pallas_call | solution.py:645
  27.6 3.5 %collective-permute-start.2 = (f32[37,8,128]{2,1,0:T(8,128)S(1)}, f32[37,8,128]{2,1,0:T(8,128)S(1)}, u32[]{:S(2)}, u32[]{:S(2)}) collective-permute-start(f32[37,8,128]{2,1,0:T(8,128)S(1)} %get-tuple-element.26.own_right), channel_id=1, source_target_pairs={{0,16},{1,17},{2,18},{3,19},{4,20},{5,21},{6,22},{7,23},{8,24},{9,... | collective-permute-start | bytes 454664 | tf_op jit(solution)/shard_map/ppermute | solution.py:564
  31.1 1.9 %collective-permute-start.3 = (f32[37,8,128]{2,1,0:T(8,128)}, f32[37,8,128]{2,1,0:T(8,128)S(1)}, u32[]{:S(2)}, u32[]{:S(2)}) collective-permute-start(f32[37,8,128]{2,1,0:T(8,128)} %get-tuple-element.27.own_left), channel_id=1, source_target_pairs={{16,0},{17,1},{18,2},{19,3},{20,4},{21,5},{22,6},{23,7},{24,8},{25... | collective-permute-start | bytes 454664 | tf_op jit(solution)/shard_map/ppermute | solution.py:564
  33.0 5.8 %all-to-all-done = f32[128,8,128]{2,1,0:T(8,128)S(1)} async-done(((f32[128,8,128]{2,1,0:T(8,128)}), f32[128,8,128]{2,1,0:T(8,128)S(1)}, u32[]{:S(2)}, u32[]{:S(2)}) %all-to-all-start) | async-done | bytes 524320 | tf_op jit(solution)/shard_map/all_to_all | solution.py:643
  38.8 0.0 collective-permute-done.2.from_left
  38.8 0.0 collective-permute-done.3.from_right
  38.8 10.3 %shard_map.134 = (f32[24,48,128]{2,1,0:T(8,128)S(1)}, f32[48,48,128]{2,1,0:T(8,128)S(1)}, f32[256,128]{1,0:T(8,128)}, f32[6,48,128]{2,1,0:T(8,128)}) custom-call(f32[24,48,128]{2,1,0:T(8,128)S(1)} %get-tuple-element.23.v_in, f32[48,48,128]{2,1,0:T(8,128)S(1)} %get-tuple-element.24.s_in, ...), custom_call_target="tpu_custom_call", output_to_operand_aliasing={{0}: (0, {}), {1}: (1, {})} | custom-call | flops 134217728 | bytes 8388608 | tf_op jit(solution)/shard_map/pallas_call | solution.py:657
  49.1 8.1 %all-to-all-start.1 = ((f32[128,2,128]{2,1,0:T(2,128)}), f32[128,2,128]{2,1,0:T(2,128)S(1)}, u32[]{:S(2)}, u32[]{:S(2)}) async-start(f32[128,2,128]{2,1,0:T(2,128)} %bitcast.14), calls=%async_computation.1 | async-start | bytes 262144 | tf_op jit(solution)/shard_map/all_to_all | solution.py:689
  57.2 0.0 copy-start
  57.2 0.9 %copy-done = f32[6,48,128]{2,1,0:T(8,128)S(1)} copy-done((f32[6,48,128]{2,1,0:T(8,128)S(1)}, f32[6,48,128]{2,1,0:T(8,128)}, u32[]{:S(2)}) %copy-start) | copy-done | bytes 147480
  58.1 1.4 %shard_map.136 = (f32[48,48,128]{2,1,0:T(8,128)S(1)}, f32[9,8,32,128]{3,2,1,0:T(8,128)}) custom-call(f32[24,48,128]{2,1,0:T(8,128)S(1)} %get-tuple-element.30.velocity, f32[48,48,128]{2,1,0:T(8,128)S(1)} %get-tuple-element.31.s_in, f32[24,48,128]{2,1,0:T(8,128)S(1)} %get-tuple-element.25.mats, f32[6,48,128]{2,1,0:T(8,128)S(1)} %copy-done), custom_call_target="tpu_custom_call", output_to_operand_aliasing={{0}: (1, {})} | custom-call | flops 16777216 | bytes 4194304 | tf_op jit(solution)/shard_map/pallas_call | solution.py:690
  59.6 7.9 %all-to-all-done.1 = f32[128,2,128]{2,1,0:T(2,128)S(1)} async-done(((f32[128,2,128]{2,1,0:T(2,128)}), f32[128,2,128]{2,1,0:T(2,128)S(1)}, u32[]{:S(2)}, u32[]{:S(2)}) %all-to-all-start.1) | async-done | bytes 131104 | tf_op jit(solution)/shard_map/all_to_all | solution.py:689
  67.4 0.7 shard_map.135
Async XLA Ops:
  4.7 20.0 %collective-permute-start.1 = (f32[97,8,128]{2,1,0:T(8,128)}, f32[97,8,128]{2,1,0:T(8,128)}, u32[]{:S(2)}, u32[]{:S(2)}) collective-permute-start(f32[97,8,128]{2,1,0:T(8,128)} %get-tuple-element.22), channel_id=1, source_target_pairs={{1,0},{2,1},{3,2},{4,3},{5,4},{6,5},{7,6},{8,7},{9,8},{10,9},{11,1... | collective-permute-start | bytes 1191944 | tf_op jit(solution)/shard_map/ppermute | solution.py:564
  6.0 18.7 %collective-permute-start = (f32[97,8,128]{2,1,0:T(8,128)S(1)}, f32[97,8,128]{2,1,0:T(8,128)}, u32[]{:S(2)}, u32[]{:S(2)}) collective-permute-start(f32[97,8,128]{2,1,0:T(8,128)S(1)} %get-tuple-element.21.own), channel_id=1, source_target_pairs={{0,1},{1,2},{2,3},{3,4},{4,5},{5,6},{6,7},{7,8},{8,9},{9,10},{10,1... | collective-permute-start | bytes 1191944 | tf_op jit(solution)/shard_map/ppermute | solution.py:564
  12.3 26.6 %all-to-all-start = ((f32[128,8,128]{2,1,0:T(8,128)}), f32[128,8,128]{2,1,0:T(8,128)S(1)}, u32[]{:S(2)}, u32[]{:S(2)}) async-start(f32[128,8,128]{2,1,0:T(8,128)} %bitcast.13), calls=%async_computation | async-start | bytes 1048576 | tf_op jit(solution)/shard_map/all_to_all | solution.py:643
  27.6 11.3 %collective-permute-start.2 = (f32[37,8,128]{2,1,0:T(8,128)S(1)}, f32[37,8,128]{2,1,0:T(8,128)S(1)}, u32[]{:S(2)}, u32[]{:S(2)}) collective-permute-start(f32[37,8,128]{2,1,0:T(8,128)S(1)} %get-tuple-element.26.own_right), channel_id=1, source_target_pairs={{0,16},{1,17},{2,18},{3,19},{4,20},{5,21},{6,22},{7,23},{8,24},{9,... | collective-permute-start | bytes 454664 | tf_op jit(solution)/shard_map/ppermute | solution.py:564
  31.1 7.7 %collective-permute-start.3 = (f32[37,8,128]{2,1,0:T(8,128)}, f32[37,8,128]{2,1,0:T(8,128)S(1)}, u32[]{:S(2)}, u32[]{:S(2)}) collective-permute-start(f32[37,8,128]{2,1,0:T(8,128)} %get-tuple-element.27.own_left), channel_id=1, source_target_pairs={{16,0},{17,1},{18,2},{19,3},{20,4},{21,5},{22,6},{23,7},{24,8},{25... | collective-permute-start | bytes 454664 | tf_op jit(solution)/shard_map/ppermute | solution.py:564
  49.1 18.3 %all-to-all-start.1 = ((f32[128,2,128]{2,1,0:T(2,128)}), f32[128,2,128]{2,1,0:T(2,128)S(1)}, u32[]{:S(2)}, u32[]{:S(2)}) async-start(f32[128,2,128]{2,1,0:T(2,128)} %bitcast.14), calls=%async_computation.1 | async-start | bytes 262144 | tf_op jit(solution)/shard_map/all_to_all | solution.py:689
  57.2 0.9 %copy-start = (f32[6,48,128]{2,1,0:T(8,128)S(1)}, f32[6,48,128]{2,1,0:T(8,128)}, u32[]{:S(2)}) copy-start(f32[6,48,128]{2,1,0:T(8,128)} %get-tuple-element.32.strip_in) | copy-start | bytes 442372

commit v5 on v4

--- a/solution.py
+++ b/solution.py
@@ -93,7 +93,11 @@
     mats,
     up,
     down,
+    send,
     by_owner,
+    made_send,
+    totals,
+    send_sems,
     base,
     table,
     held,
@@ -140,6 +144,7 @@
             down[f * NZ + z] = ref[p + z, 8:16, :]
             up[f * NZ + z] = ref[p + z, 32:40, :]
     by_owner[...] = sums_by_owner(rows_in, held, table, count, station, station_row)
+    send_kernel(by_owner, send, made_send, totals, send_sems)
 
 
 def edges_kernel(v_in, s_in, m_in, below, above, own, velocity, stress, mats, right, left):
@@ -600,12 +605,16 @@
     )
 
     held = (shape(3 * NZ, ROWS, 128), shape(6 * NZ, ROWS, 128), shape(3 * NZ, ROWS, 128))
-    velocity, stress, mats, up, down, by_owner = pl.pallas_call(
+    velocity, stress, mats, up, down, send = pl.pallas_call(
         first_kernel,
-        out_shape=held + (shape(PLANES + 1, 8, 128), shape(PLANES + 1, 8, 128), shape(128, 128)),
+        out_shape=held + (shape(PLANES + 1, 8, 128), shape(PLANES + 1, 8, 128), pltpu.HBM((OWNERS * 8, 128), F32)),
         in_specs=[ANY] * 4 + [SMEM, ANY, VMEM, VMEM, ANY],
-        out_specs=(VMEM,) * 6,
+        out_specs=(VMEM,) * 5 + (ANY,),
         scratch_shapes=[
+            pltpu.VMEM((128, 128), F32),
+            pltpu.VMEM((OWNERS * 8, 128), F32),
+            pltpu.VMEM((176, 128), F32),
+            pltpu.SemaphoreType.DMA((4,)),
             pltpu.VMEM((SAMPLES // STEPS, 128), BF16),
             pltpu.VMEM((SAMPLES, 128), BF16),
             pltpu.VMEM((3, rows_dev, SAMPLES), BF16),
@@ -627,19 +636,6 @@
     from_below = shift(up, 0, 1)
     from_above = shift(down, 0, -1)
 
-    send = pl.pallas_call(
-        send_kernel,
-        out_shape=pltpu.HBM((OWNERS * 8, 128), F32),
-        in_specs=[VMEM],
-        out_specs=ANY,
-        scratch_shapes=[
-            pltpu.VMEM((OWNERS * 8, 128), F32),
-            pltpu.VMEM((176, 128), F32),
-            pltpu.SemaphoreType.DMA((4,)),
-        ],
-        compiler_params=PART,
-        cost_estimate=cost(1 << 20, 1 << 20),
-    )(by_owner)
     sources = lax.all_to_all(send, ("gx", "gy"), 0, 0, tiled=True)
 
     velocity, stress, mats, right, left = pl.pallas_call(

time: 68.4 us -> 69.2 us (1.012)
    pallas_call x1, Pallas kernels: 4.1 us -> 5.57 us  [local(): pl.pallas_call(first_kernel, out_shape=held + (shape(PLANES + 1, 8, 128),...]
    pallas_call x1 -> x0, Pallas kernels: 0.9 us -> none  [local(): pl.pallas_call(send_kernel, out_shape=pltpu.HBM((OWNERS * 8, 128), F32),...]
  transfers between devices with their start and end apart: 6 -> 6, of which waited for: 2 -> 2; matrix products, arithmetic and copies ran while one was open for 0% -> 0% of each run, Pallas kernels for 8% -> 6%
where the time goes in v5:
time: 69.2 us; the launch traced here: 68.8 us
  starting transfers between devices  32.7 us (47%)
  Pallas kernels  20.8 us (30%)
  waiting for transfers between devices  13.7 us (20%)
  local copies, waits for them, and re-layouts  0.91 us (1%)
  between operations  0.72 us (1%)
    all_to_all x1, starting transfers between devices, local(): sources = lax.all_to_all(send, ('gx', 'gy'), 0, 0, tiled=True)  12.4 us
    ppermute x4, starting transfers between devices, shift(): return lax.ppermute(value, ('gx', 'gy'), pairs)  12.1 us
    pallas_call x1, Pallas kernels, local(): pl.pallas_call(step_kernel, out_shape=held[:2] + (pltpu.HBM((256, 128), F...  10.3 us
    all_to_all x1, starting transfers between devices, local(): got = lax.all_to_all(send, ('gx', 'gy'), 0, 0, tiled=True)  8.24 us
    all_to_all x1, waiting for transfers between devices, local(): got = lax.all_to_all(send, ('gx', 'gy'), 0, 0, tiled=True)  7.86 us
    all_to_all x1, waiting for transfers between devices, local(): sources = lax.all_to_all(send, ('gx', 'gy'), 0, 0, tiled=True)  5.79 us
    pallas_call x1, Pallas kernels, local(): pl.pallas_call(first_kernel, out_shape=held + (shape(PLANES + 1, 8, 128),...  5.57 us
    pallas_call x1, Pallas kernels, local(): pl.pallas_call(edges_kernel, out_shape=held + (shape(EDGES + 1, 8, 128),...  2.85 us
  transfers between devices with their start and end apart: 6, of which 2 were waited for; matrix products, arithmetic and copies ran while one was open for 0% of the time, Pallas kernels for 6%

profile of v5, /device:TPU:1, one launch (start us, length us, event | category | flops | bytes accessed | tf_op | source)
XLA Modules:
  0.0 68.8 jit_solution(17187688746264276657)
XLA Ops:
  0.6 5.6 %shard_map.131 = (f32[24,48,128]{2,1,0:T(8,128)S(1)}, f32[48,48,128]{2,1,0:T(8,128)S(1)}, f32[24,48,128]{2,1,0:T(8,128)S(1)}, f32[97,8,128]{2,1,0:T(8,128)S(1)},...) custom-call(f32[9,8,32,128]{3,2,1,0:T(8,128)} %state.1, f32[8,32,128]{2,1,0:T(8,128)} %lame.1, f32[8,32,128]{2,1,0:T(8,128)} %shear.1, ...), custom_call_target="tpu_custom_call" | custom-call | flops 1073741824 | bytes 4194304 | tf_op jit(solution)/shard_map/pallas_call | solution.py:608
  6.2 1.3 %collective-permute-start.1 = (f32[97,8,128]{2,1,0:T(8,128)}, f32[97,8,128]{2,1,0:T(8,128)}, u32[]{:S(2)}, u32[]{:S(2)}) collective-permute-start(f32[97,8,128]{2,1,0:T(8,128)} %get-tuple-element.22), channel_id=1, source_target_pairs={{1,0},{2,1},{3,2},{4,3},{5,4},{6,5},{7,6},{8,7},{9,8},{10,9},{11,1... | collective-permute-start | bytes 1191944 | tf_op jit(solution)/shard_map/ppermute | solution.py:569
  7.5 5.3 %collective-permute-start = (f32[97,8,128]{2,1,0:T(8,128)S(1)}, f32[97,8,128]{2,1,0:T(8,128)}, u32[]{:S(2)}, u32[]{:S(2)}) collective-permute-start(f32[97,8,128]{2,1,0:T(8,128)S(1)} %get-tuple-element.21.own), channel_id=1, source_target_pairs={{0,1},{1,2},{2,3},{3,4},{4,5},{5,6},{6,7},{7,8},{8,9},{9,10},{10,1... | collective-permute-start | bytes 1191944 | tf_op jit(solution)/shard_map/ppermute | solution.py:569
  12.8 12.4 %all-to-all-start = ((f32[128,8,128]{2,1,0:T(8,128)}), f32[128,8,128]{2,1,0:T(8,128)S(1)}, u32[]{:S(2)}, u32[]{:S(2)}) async-start(f32[128,8,128]{2,1,0:T(8,128)} %bitcast.13), calls=%async_computation | async-start | bytes 1048576 | tf_op jit(solution)/shard_map/all_to_all | solution.py:639
  25.3 0.0 collective-permute-done.1.above
  25.3 0.0 collective-permute-done.below
  25.3 2.8 %shard_map.132 = (f32[24,48,128]{2,1,0:T(8,128)S(1)}, f32[48,48,128]{2,1,0:T(8,128)S(1)}, f32[24,48,128]{2,1,0:T(8,128)S(1)}, f32[37,8,128]{2,1,0:T(8,128)S(1)}, f32[37,8,128]{2,1,0:T(8,128)}) custom-call(f32[24,48,128]{2,1,0:T(8,128)S(1)} %get-tuple-element.18.v_in, ...), custom_call_target="tpu_custom_call", output_to_operand_aliasing={{0}: (0, {}), {1}: (1, {}), {2}: (2, {})} | custom-call | flops 1048576 | bytes 2097152 | tf_op jit(solution)/shard_map/pallas_call | solution.py:641
  28.1 3.5 %collective-permute-start.2 = (f32[37,8,128]{2,1,0:T(8,128)S(1)}, f32[37,8,128]{2,1,0:T(8,128)S(1)}, u32[]{:S(2)}, u32[]{:S(2)}) collective-permute-start(f32[37,8,128]{2,1,0:T(8,128)S(1)} %get-tuple-element.26.own_right), channel_id=1, source_target_pairs={{0,16},{1,17},{2,18},{3,19},{4,20},{5,21},{6,22},{7,23},{8,24},{9,... | collective-permute-start | bytes 454664 | tf_op jit(solution)/shard_map/ppermute | solution.py:569
  31.7 1.9 %collective-permute-start.3 = (f32[37,8,128]{2,1,0:T(8,128)}, f32[37,8,128]{2,1,0:T(8,128)S(1)}, u32[]{:S(2)}, u32[]{:S(2)}) collective-permute-start(f32[37,8,128]{2,1,0:T(8,128)} %get-tuple-element.27.own_left), channel_id=1, source_target_pairs={{16,0},{17,1},{18,2},{19,3},{20,4},{21,5},{22,6},{23,7},{24,8},{25... | collective-permute-start | bytes 454664 | tf_op jit(solution)/shard_map/ppermute | solution.py:569
  33.6 5.8 %all-to-all-done = f32[128,8,128]{2,1,0:T(8,128)S(1)} async-done(((f32[128,8,128]{2,1,0:T(8,128)}), f32[128,8,128]{2,1,0:T(8,128)S(1)}, u32[]{:S(2)}, u32[]{:S(2)}) %all-to-all-start) | async-done | bytes 524320 | tf_op jit(solution)/shard_map/all_to_all | solution.py:639
  39.4 0.0 collective-permute-done.2.from_left
  39.4 0.0 collective-permute-done.3.from_right
  39.4 10.3 %shard_map.133 = (f32[24,48,128]{2,1,0:T(8,128)S(1)}, f32[48,48,128]{2,1,0:T(8,128)S(1)}, f32[256,128]{1,0:T(8,128)}, f32[6,48,128]{2,1,0:T(8,128)}) custom-call(f32[24,48,128]{2,1,0:T(8,128)S(1)} %get-tuple-element.23.v_in, f32[48,48,128]{2,1,0:T(8,128)S(1)} %get-tuple-element.24.s_in, ...), custom_call_target="tpu_custom_call", output_to_operand_aliasing={{0}: (0, {}), {1}: (1, {})} | custom-call | flops 134217728 | bytes 8388608 | tf_op jit(solution)/shard_map/pallas_call | solution.py:653
  49.7 8.2 %all-to-all-start.1 = ((f32[128,2,128]{2,1,0:T(2,128)}), f32[128,2,128]{2,1,0:T(2,128)S(1)}, u32[]{:S(2)}, u32[]{:S(2)}) async-start(f32[128,2,128]{2,1,0:T(2,128)} %bitcast.14), calls=%async_computation.1 | async-start | bytes 262144 | tf_op jit(solution)/shard_map/all_to_all | solution.py:685
  57.9 0.0 copy-start
  57.9 0.9 %copy-done = f32[6,48,128]{2,1,0:T(8,128)S(1)} copy-done((f32[6,48,128]{2,1,0:T(8,128)S(1)}, f32[6,48,128]{2,1,0:T(8,128)}, u32[]{:S(2)}) %copy-start) | copy-done | bytes 147480
  58.8 1.4 %shard_map.135 = (f32[48,48,128]{2,1,0:T(8,128)S(1)}, f32[9,8,32,128]{3,2,1,0:T(8,128)}) custom-call(f32[24,48,128]{2,1,0:T(8,128)S(1)} %get-tuple-element.30.velocity, f32[48,48,128]{2,1,0:T(8,128)S(1)} %get-tuple-element.31.s_in, f32[24,48,128]{2,1,0:T(8,128)S(1)} %get-tuple-element.25.mats, f32[6,48,128]{2,1,0:T(8,128)S(1)} %copy-done), custom_call_target="tpu_custom_call", output_to_operand_aliasing={{0}: (1, {})} | custom-call | flops 16777216 | bytes 4194304 | tf_op jit(solution)/shard_map/pallas_call | solution.py:686
  60.3 7.9 %all-to-all-done.1 = f32[128,2,128]{2,1,0:T(2,128)S(1)} async-done(((f32[128,2,128]{2,1,0:T(2,128)}), f32[128,2,128]{2,1,0:T(2,128)S(1)}, u32[]{:S(2)}, u32[]{:S(2)}) %all-to-all-start.1) | async-done | bytes 131104 | tf_op jit(solution)/shard_map/all_to_all | solution.py:685
  68.1 0.7 shard_map.134
Async XLA Ops:
  6.2 19.1 %collective-permute-start.1 = (f32[97,8,128]{2,1,0:T(8,128)}, f32[97,8,128]{2,1,0:T(8,128)}, u32[]{:S(2)}, u32[]{:S(2)}) collective-permute-start(f32[97,8,128]{2,1,0:T(8,128)} %get-tuple-element.22), channel_id=1, source_target_pairs={{1,0},{2,1},{3,2},{4,3},{5,4},{6,5},{7,6},{8,7},{9,8},{10,9},{11,1... | collective-permute-start | bytes 1191944 | tf_op jit(solution)/shard_map/ppermute | solution.py:569
  7.5 17.8 %collective-permute-start = (f32[97,8,128]{2,1,0:T(8,128)S(1)}, f32[97,8,128]{2,1,0:T(8,128)}, u32[]{:S(2)}, u32[]{:S(2)}) collective-permute-start(f32[97,8,128]{2,1,0:T(8,128)S(1)} %get-tuple-element.21.own), channel_id=1, source_target_pairs={{0,1},{1,2},{2,3},{3,4},{4,5},{5,6},{6,7},{7,8},{8,9},{9,10},{10,1... | collective-permute-start | bytes 1191944 | tf_op jit(solution)/shard_map/ppermute | solution.py:569
  12.8 26.6 %all-to-all-start = ((f32[128,8,128]{2,1,0:T(8,128)}), f32[128,8,128]{2,1,0:T(8,128)S(1)}, u32[]{:S(2)}, u32[]{:S(2)}) async-start(f32[128,8,128]{2,1,0:T(8,128)} %bitcast.13), calls=%async_computation | async-start | bytes 1048576 | tf_op jit(solution)/shard_map/all_to_all | solution.py:639
  28.1 11.3 %collective-permute-start.2 = (f32[37,8,128]{2,1,0:T(8,128)S(1)}, f32[37,8,128]{2,1,0:T(8,128)S(1)}, u32[]{:S(2)}, u32[]{:S(2)}) collective-permute-start(f32[37,8,128]{2,1,0:T(8,128)S(1)} %get-tuple-element.26.own_right), channel_id=1, source_target_pairs={{0,16},{1,17},{2,18},{3,19},{4,20},{5,21},{6,22},{7,23},{8,24},{9,... | collective-permute-start | bytes 454664 | tf_op jit(solution)/shard_map/ppermute | solution.py:569
  31.7 7.7 %collective-permute-start.3 = (f32[37,8,128]{2,1,0:T(8,128)}, f32[37,8,128]{2,1,0:T(8,128)S(1)}, u32[]{:S(2)}, u32[]{:S(2)}) collective-permute-start(f32[37,8,128]{2,1,0:T(8,128)} %get-tuple-element.27.own_left), channel_id=1, source_target_pairs={{16,0},{17,1},{18,2},{19,3},{20,4},{21,5},{22,6},{23,7},{24,8},{25... | collective-permute-start | bytes 454664 | tf_op jit(solution)/shard_map/ppermute | solution.py:569
  49.7 18.4 %all-to-all-start.1 = ((f32[128,2,128]{2,1,0:T(2,128)}), f32[128,2,128]{2,1,0:T(2,128)S(1)}, u32[]{:S(2)}, u32[]{:S(2)}) async-start(f32[128,2,128]{2,1,0:T(2,128)} %bitcast.14), calls=%async_computation.1 | async-start | bytes 262144 | tf_op jit(solution)/shard_map/all_to_all | solution.py:685
  57.9 0.9 %copy-start = (f32[6,48,128]{2,1,0:T(8,128)S(1)}, f32[6,48,128]{2,1,0:T(8,128)}, u32[]{:S(2)}) copy-start(f32[6,48,128]{2,1,0:T(8,128)} %get-tuple-element.32.strip_in) | copy-start | bytes 442372
